TPU v7x, 256 devices: a whole 4x4x8 slice. The times are simulated.
256 devices in a mesh: row: 32 (over z, y), col: 8 (over x, core).
Axes of the slice: x: 4, y: 4, z: 8, core: 2. Of those that a mesh axis runs over, the one named last changes fastest.
Arguments:
- coupling: float32 [1, 8, 4, 32, 512, 512], P(None, 'col', None, 'row'), may hold values from -0.046875 to 0.046875
- earlier: float32 [4, 32, 512, 1536], P(None, 'row'), may hold values from -6 to 6
- right_sides: float32 [1, 8, 512, 1536], P(None, 'col', 'row'), may hold values from -6 to 6
- panel_blocks: float32 [1, 8, 2, 512, 512], P(None, 'col', None, 'row'), may hold values from -4 to 4, as said below
- block_inverses: float32 [2, 512, 512], replicated, may hold values from -4 to 4, as said below
Outputs:
- solved: float32 [2, 512, 1536], replicated
- pending: float32 [1, 8, 512, 1536], P(None, 'col', 'row')
Inputs may be any that keep to these rules, and one draw needn't show every extreme that they name: `panel_blocks`: block row a * 8 + c of column index k is zero where a * 8 + c >= 7 - k. `block_inverses`: each block is upper triangular with a positive diagonal.
All inputs are finite; a program needn't handle non-finite values.
Results may differ from a plain program's by a relative error of at most 0.000088.
Values sent between devices are 32-bit elements; how exact they have to be, the bound alone decides.
No kernel may reach another device: no remote copies, remote signals or barrier semaphores. Data moves between devices by JAX's collectives and lax.ppermute only.
A program may use at most 128 MiB of HBM per device.

v0:
```python
import functools

import jax
import jax.numpy as jnp
from jax import lax
from jax.experimental import pallas as pl
from jax.experimental.pallas import tpu as pltpu
from jax.sharding import Mesh
from jax.sharding import PartitionSpec as P

NZ, NY, NX, NCORE = 8, 4, 4, 2
SLAB = 16
HALF = 768
PART = 384
BITREV = (0, 4, 2, 6, 1, 5, 3, 7)
HALVES = (((0, 3, 1, 2), (1, 3)), ((0, 1, 3, 2), (3, 1)))


def split(x):
    high = x.astype(jnp.bfloat16)
    return high, (x - high.astype(jnp.float32)).astype(jnp.bfloat16)


def dot3(a, b):
    ah, al = split(a)
    bh, bl = split(b)
    mul = functools.partial(jnp.dot, preferred_element_type=jnp.float32)
    return mul(ah, bh) + (mul(ah, bl) + mul(al, bh))


def term_kernel(index_ref, c_ref, ea_ref, eb_ref, oa_ref, ob_ref, acc):
    k = pl.program_id(0)
    product = dot3(c_ref[0], jnp.concatenate([ea_ref[0], eb_ref[0]], axis=1))

    @pl.when(k == 0)
    def _():
        acc[...] = product

    @pl.when(k > 0)
    def _():
        acc[...] += product

    @pl.when(k == pl.num_programs(0) - 1)
    def _():
        for half, o_ref in enumerate((oa_ref, ob_ref)):
            for i in range(NZ * NY):
                row = pl.multiple_of(index_ref[half * NZ * NY + i] * SLAB, SLAB)
                o_ref[i] = acc[pl.ds(row, SLAB), half * PART : (half + 1) * PART]


def term(index, coupling, earlier, chunk):
    out = pl.BlockSpec((NZ * NY, SLAB, PART), lambda k, i: (0, 0, 0))
    return pl.pallas_call(
        term_kernel,
        grid_spec=pltpu.PrefetchScalarGridSpec(
            num_scalar_prefetch=1,
            grid=(4,),
            in_specs=[
                pl.BlockSpec((1, 512, 512), lambda k, i: (k, 0, 0)),
                pl.BlockSpec((1, 512, PART), lambda k, i: (k, 0, chunk)),
                pl.BlockSpec((1, 512, PART), lambda k, i: (k, 0, 2 + chunk)),
            ],
            out_specs=(out, out),
            scratch_shapes=[pltpu.VMEM((512, HALF), jnp.float32)],
        ),
        out_shape=(jax.ShapeDtypeStruct((NZ * NY, SLAB, PART), jnp.float32),) * 2,
        compiler_params=pltpu.CompilerParams(vmem_limit_bytes=56 * 2**20),
        cost_estimate=pl.CostEstimate(
            flops=6 * 512 * 2048 * HALF, bytes_accessed=12 * 2**20, transcendentals=0
        ),
        name="term",
    )(index, coupling, earlier, earlier)


def solve_kernel(counts, with_link, index_ref, core_ref, inv_ref, *refs):
    pieces, refs = refs[: len(counts)], refs[len(counts) :]
    if with_link:
        link_own, link_other, o_ref, link_ref, b = refs
    else:
        link_ref, o_ref, b = refs
    rows, at = [], 0
    for piece, count in zip(pieces, counts):
        for i in range(count):
            rows.append(pl.ds(pl.multiple_of(index_ref[at] * SLAB, SLAB), SLAB))
            for block in (0, 1):
                b[block, rows[at], :] = piece[i, :, block * PART : (block + 1) * PART]
            at += 1
    if with_link:
        here = pl.ds(pl.multiple_of(core_ref[0] * 256, 128), 256)
        there = pl.ds(pl.multiple_of((1 - core_ref[0]) * 256, 128), 256)
        for i, row in enumerate(rows):
            link_ref[row, here] = link_own[i]
            link_ref[row, there] = link_other[i]
    first = dot3(inv_ref[0], b[0])
    o_ref[0] = first
    middle = b[1] - dot3(link_ref[...], first)
    o_ref[1] = dot3(inv_ref[1], middle)


def solve(index, core, inverses, pieces, links):
    counts = tuple(p.shape[0] for p in pieces)
    with_link = len(links) == 2
    whole = pl.BlockSpec(memory_space=pltpu.VMEM)
    scalar = pl.BlockSpec(memory_space=pltpu.SMEM)
    out = jax.ShapeDtypeStruct((2, 512, PART), jnp.float32)
    link = jax.ShapeDtypeStruct((512, 512), jnp.float32)
    return pl.pallas_call(
        functools.partial(solve_kernel, counts, with_link),
        in_specs=[scalar] * 2 + [whole] * (1 + len(pieces) + len(links)),
        out_specs=(whole, whole) if with_link else whole,
        scratch_shapes=[pltpu.VMEM((2, 512, PART), jnp.float32)],
        out_shape=(out, link) if with_link else out,
        compiler_params=pltpu.CompilerParams(vmem_limit_bytes=24 * 2**20),
        cost_estimate=pl.CostEstimate(
            flops=18 * 512 * 512 * PART, bytes_accessed=6 * 2**20, transcendentals=0
        ),
        name="solve",
    )(index, core, inverses, *pieces, *links)


def finish_kernel(core_ref, own1, own2, other1, other2, a1, b1, a2, b2, panel, solved, pending, sems):
    core = core_ref[0]
    mine, theirs = core * HALF, (1 - core) * HALF
    places = ((own1, mine), (own2, mine + PART), (other1, theirs), (other2, theirs + PART))
    copies = []
    for i, (ref, at) in enumerate(places):
        columns = pl.ds(pl.multiple_of(at, 128), PART)
        copies.append(pltpu.make_async_copy(ref, solved.at[:, :, columns], sems.at[i]))
        copies[-1].start()
    for i, base in enumerate((a1, a2, b1, b2)):
        pending[:, i * PART : (i + 1) * PART] = base[...]
    for ref, at in places:
        columns = pl.ds(pl.multiple_of(at, 128), PART)
        update = dot3(panel[0], ref[0]) + dot3(panel[1], ref[1])
        pending[:, columns] = pending[:, columns] - update
    for copy in copies:
        copy.wait()


def finish(core, *operands):
    whole = pl.BlockSpec(memory_space=pltpu.VMEM)
    return pl.pallas_call(
        finish_kernel,
        in_specs=[pl.BlockSpec(memory_space=pltpu.SMEM)] + [whole] * len(operands),
        out_specs=(pl.BlockSpec(memory_space=pl.ANY), whole),
        scratch_shapes=[pltpu.SemaphoreType.DMA((4,))],
        out_shape=(
            jax.ShapeDtypeStruct((2, 512, 2 * HALF), jnp.float32),
            jax.ShapeDtypeStruct((SLAB, 2 * HALF), jnp.float32),
        ),
        compiler_params=pltpu.CompilerParams(vmem_limit_bytes=24 * 2**20),
        name="finish",
    )(core, *operands)


def swap(x, axis, bit):
    return lax.ppermute(x, axis, [(i, i ^ bit) for i in range(lax.axis_size(axis))])


def step(x, axis, by):
    n = lax.axis_size(axis)
    return lax.ppermute(x, axis, [(i, (i + by) % n) for i in range(n)])


def reduce_rows(slabs):
    near = []
    for half in (0, 1):
        first, second = HALVES[half][1]
        s = slabs[half]
        s = s[:16] + swap(s[16:], "y", first)
        near.append(s[:8] + swap(s[8:], "y", second))
    s = jnp.stack(near, axis=1)
    s = s[:4] + swap(s[4:], "z", 1)
    s = s[:2] + swap(s[2:], "z", 2)
    s = s[:1] + swap(s[1:], "z", 4)
    return s[0, 0], s[0, 1]


def spread_x(v):
    others = [lax.ppermute(v, "x", [(NX - 1, i)]) for i in range(NX - 1)]
    return jnp.where(lax.axis_index("x") == NX - 1, v, others[0] + others[1] + others[2])


def gather_rows(v):
    v = v[None]
    for bit in (4, 2, 1):
        v = jnp.concatenate([v, swap(v, "z", bit)])
    up, down = step(v, "y", 1), step(v, "y", -1)
    return [v, up, down, step(up[:4], "y", 1), step(down[4:], "y", -1)]


def local(coupling, earlier, right_sides, panel_blocks, block_inverses):
    z, y, core = (lax.axis_index(a) for a in ("z", "y", "core"))
    coupling, earlier = coupling[0, 0, :, 0], earlier[:, 0]
    right, panel = right_sides[0, 0], panel_blocks[0, 0]
    is_first = core == 0
    core_id = core.astype(jnp.int32).reshape(1)

    slab_order = [(z ^ kz) * NY + (y ^ ky) for order, _ in HALVES for ky in order for kz in BITREV]
    slab_order = jnp.stack(slab_order).astype(jnp.int32)
    offsets = ((0, BITREV), (-1, BITREV), (1, BITREV), (2, BITREV[:4]), (2, BITREV[4:]))
    row_order = [(z ^ kz) * NY + (y + oy) % NY for oy, along in offsets for kz in along]
    row_order = jnp.stack(row_order).astype(jnp.int32)

    bases, solutions = [], []
    link = None
    for chunk in (0, 1):
        slabs = term(slab_order, coupling, earlier, chunk)
        if chunk == 0:
            slabs, coupling = lax.optimization_barrier((slabs, coupling))
        total = reduce_rows(slabs)
        at = chunk * PART
        base = right[:, at : at + PART] - total[0], right[:, HALF + at : HALF + at + PART] - total[1]
        bases += base
        kept = jnp.where(is_first, base[0], base[1])
        given = jnp.where(is_first, base[1], base[0])
        if chunk == 0:
            given = jnp.concatenate([given, panel[0, :, 256:]], axis=1)
        came = swap(given, "core", 1)
        last = jnp.where(is_first, came[:, :PART], kept)
        other = jnp.where(is_first, kept, came[:, :PART])
        v = [last, other]
        if chunk == 0:
            v.append(jnp.where(is_first, panel[0, :, :256], came[:, PART:]))
        pieces = gather_rows(spread_x(jnp.concatenate(v, axis=1)))
        if chunk == 0:
            part = jnp.concatenate([p[:, :, HALF:] for p in pieces])
            own, link = solve(row_order, core_id, block_inverses, pieces, (part, swap(part, "core", 1)))
        else:
            own = solve(row_order, core_id, block_inverses, pieces, (link,))
        solutions.append((own, swap(own, "core", 1)))
    (own1, other1), (own2, other2) = solutions
    solved, pending = finish(core_id, own1, own2, other1, other2, *bases, panel)
    return solved, pending[None, None]


def solution(mesh):
    inner = Mesh(mesh.devices.reshape(NZ, NY, NX, NCORE), ("z", "y", "x", "core"))
    row, col = ("z", "y"), ("x", "core")
    in_specs = (
        P(None, col, None, row, None, None),
        P(None, row, None, None),
        P(None, col, row, None),
        P(None, col, None, row, None),
        P(),
    )
    out_specs = (P(), P(None, col, row, None))
    return jax.shard_map(local, mesh=inner, in_specs=in_specs, out_specs=out_specs, check_vma=False)
```

profile of v0, /device:TPU:1, one launch (start us, length us, event | category | flops | bytes accessed | tf_op | source)
XLA Modules:
  0.0 177.7 jit_solution(13590571493975762373)
XLA Ops:
  1.4 10.0 %term.2 = (f32[32,16,384]{2,1,0:T(8,128)}, f32[32,16,384]{2,1,0:T(8,128)}) custom-call(s32[64]{0:T(128)} %stack.313.index_ref, f32[4,512,512]{2,1,0:T(8,128)} %bitcast.115, f32[4,512,1536]{2,1,0:T(8,128)} %bitcast.111, f32[4,512,1536]{2,1,0:T(8,128)} %bitcast.112), custom_call_target="tpu_custom_call" | custom-call | flops 4831838208 | bytes 12582912 | tf_op jit(solution)/shard_map/term/pallas_call | solution.py:53
  11.4 1.8 %slice.154 = f32[16,16,384]{2,1,0:T(8,128)} slice(f32[32,16,384]{2,1,0:T(8,128)} %get-tuple-element.16), slice={[16:32], [0:16], [0:384]} | slice | bytes 786432 | tf_op jit(solution)/shard_map/slice | solution.py:170
  13.2 3.6 %collective-permute-start.2 = (f32[16,16,384]{2,1,0:T(8,128)}, f32[16,16,384]{2,1,0:T(8,128)}, u32[]{:S(2)}, u32[]{:S(2)}) collective-permute-start(f32[16,16,384]{2,1,0:T(8,128)} %slice.154), channel_id=1, source_target_pairs={{0,24},{8,16},{16,8},{24,0},{1,25},{9,17},{17,9},{25,1},{2,26},{10... | collective-permute-start | bytes 1179656 | tf_op jit(solution)/shard_map/ppermute | solution.py:157
  16.8 1.8 %slice.150 = f32[16,16,384]{2,1,0:T(8,128)} slice(f32[32,16,384]{2,1,0:T(8,128)} %get-tuple-element.15), slice={[16:32], [0:16], [0:384]} | slice | bytes 786432 | tf_op jit(solution)/shard_map/slice | solution.py:170
  18.6 10.1 %term.3 = (f32[32,16,384]{2,1,0:T(8,128)}, f32[32,16,384]{2,1,0:T(8,128)}) custom-call(s32[64]{0:T(128)} %stack.313.index_ref, f32[4,512,512]{2,1,0:T(8,128)} %bitcast.116, f32[4,512,1536]{2,1,0:T(8,128)} %bitcast.113, f32[4,512,1536]{2,1,0:T(8,128)} %bitcast.114), custom_call_target="tpu_custom_call" | custom-call | flops 4831838208 | bytes 12582912 | tf_op jit(solution)/shard_map/term/pallas_call | solution.py:53
  28.7 1.1 slice.183
  32.4 1.1 slice_add_fusion.2
  34.2 1.0 slice_add_fusion.3
  35.3 2.3 %collective-permute-start.1 = (f32[8,16,384]{2,1,0:T(8,128)S(1)}, f32[8,16,384]{2,1,0:T(8,128)S(1)}, u32[]{:S(2)}, u32[]{:S(2)}) collective-permute-start(f32[8,16,384]{2,1,0:T(8,128)S(1)} %slice.199), channel_id=1, source_target_pairs={{0,24},{8,16},{16,8},{24,0},{1,25},{9,17},{17,9},{25,1},{2,26},{10... | collective-permute-start | bytes 589832 | tf_op jit(solution)/shard_map/ppermute | solution.py:157
  37.6 3.2 %collective-permute-done.21 = f32[16,16,384]{2,1,0:T(8,128)} collective-permute-done((f32[16,16,384]{2,1,0:T(8,128)S(1)}, f32[16,16,384]{2,1,0:T(8,128)}, u32[]{:S(2)}, u32[]{:S(2)}) %collective-permute-start.21) | collective-permute-done | bytes 393248 | tf_op jit(solution)/shard_map/ppermute | solution.py:157
  41.9 1.1 slice_add_fusion.1
  43.0 1.2 collective-permute-start.20
  44.9 1.7 collective-permute-start.4
  46.6 2.2 %collective-permute-done.22 = f32[8,16,384]{2,1,0:T(8,128)S(1)} collective-permute-done((f32[8,16,384]{2,1,0:T(8,128)S(1)}, f32[8,16,384]{2,1,0:T(8,128)S(1)}, u32[]{:S(2)}, u32[]{:S(2)}) %collective-permute-start.22) | collective-permute-done | bytes 196640 | tf_op jit(solution)/shard_map/ppermute | solution.py:157
  49.0 1.9 %collective-permute-start.23 = (f32[4,2,16,384]{3,2,1,0:T(8,128)S(1)}, f32[4,2,16,384]{3,2,1,0:T(8,128)S(1)}, u32[]{:S(2)}, u32[]{:S(2)}) collective-permute-start(f32[4,2,16,384]{3,2,1,0:T(8,128)S(1)} %pad_maximum_fusion.3), channel_id=1, source_target_pairs={{0,32},{32,0},{64,96},{96,64},{128,160},{160,128},{192,224},{224,1... | collective-permute-start | bytes 589832 | tf_op jit(solution)/shard_map/ppermute | solution.py:157
  50.9 3.1 %collective-permute-start.5 = (f32[2,2,16,384]{3,2,1,0:T(8,128)S(1)}, f32[2,2,16,384]{3,2,1,0:T(8,128)S(1)}, u32[]{:S(2)}, u32[]{:S(2)}) collective-permute-start(f32[2,2,16,384]{3,2,1,0:T(8,128)S(1)} %slice.205), channel_id=1, source_target_pairs={{0,64},{32,96},{64,0},{96,32},{128,192},{160,224},{192,128},{224,1... | collective-permute-start | bytes 294920 | tf_op jit(solution)/shard_map/ppermute | solution.py:157
  54.0 2.8 %collective-permute-done.23 = f32[4,2,16,384]{3,2,1,0:T(8,128)S(1)} collective-permute-done((f32[4,2,16,384]{3,2,1,0:T(8,128)S(1)}, f32[4,2,16,384]{3,2,1,0:T(8,128)S(1)}, u32[]{:S(2)}, u32[]{:S(2)}) %collective-permute-start.23) | collective-permute-done | bytes 196640 | tf_op jit(solution)/shard_map/ppermute | solution.py:157
  56.9 2.2 %collective-permute-start.24 = (f32[2,2,16,384]{3,2,1,0:T(8,128)S(1)}, f32[2,2,16,384]{3,2,1,0:T(8,128)S(1)}, u32[]{:S(2)}, u32[]{:S(2)}) collective-permute-start(f32[2,2,16,384]{3,2,1,0:T(8,128)S(1)} %slice.230), channel_id=1, source_target_pairs={{0,64},{32,96},{64,0},{96,32},{128,192},{160,224},{192,128},{224,1... | collective-permute-start | bytes 294920 | tf_op jit(solution)/shard_map/ppermute | solution.py:157
  59.1 4.7 %collective-permute-start.6 = (f32[1,2,16,384]{3,2,1,0:T(8,128)S(1)}, f32[1,2,16,384]{3,2,1,0:T(8,128)S(1)}, u32[]{:S(2)}, u32[]{:S(2)}) collective-permute-start(f32[1,2,16,384]{3,2,1,0:T(8,128)S(1)} %slice.207), channel_id=1, source_target_pairs={{0,128},{32,160},{64,192},{96,224},{128,0},{160,32},{192,64},{224,... | collective-permute-start | bytes 147464 | tf_op jit(solution)/shard_map/ppermute | solution.py:157
  63.8 7.2 %collective-permute-start.25 = (f32[1,2,16,384]{3,2,1,0:T(8,128)S(1)}, f32[1,2,16,384]{3,2,1,0:T(8,128)S(1)}, u32[]{:S(2)}, u32[]{:S(2)}) collective-permute-start(f32[1,2,16,384]{3,2,1,0:T(8,128)S(1)} %slice.232), channel_id=1, source_target_pairs={{0,128},{32,160},{64,192},{96,224},{128,0},{160,32},{192,64},{224,... | collective-permute-start | bytes 147464 | tf_op jit(solution)/shard_map/ppermute | solution.py:157
  71.1 1.5 collective-permute-done.25
  72.6 8.7 %collective-permute-start.7 = (f32[16,640]{1,0:T(8,128)S(1)}, f32[16,640]{1,0:T(8,128)S(1)}, u32[]{:S(2)}, u32[]{:S(2)}) collective-permute-start(f32[16,640]{1,0:T(8,128)S(1)} %pad_maximum_fusion.10), channel_id=1, source_target_pairs={{0,1},{1,0},{2,3},{3,2},{4,5},{5,4},{6,7},{7,6},{8,9},{9,8},{10,11... | collective-permute-start | bytes 122888 | tf_op jit(solution)/shard_map/ppermute | solution.py:157
  83.6 1.3 collective-permute-start.8
  84.9 6.5 %collective-permute-done.8 = f32[16,1024]{1,0:T(8,128)S(1)} collective-permute-done((f32[16,1024]{1,0:T(8,128)S(1)}, f32[16,1024]{1,0:T(8,128)S(1)}, u32[]{:S(2)}, u32[]{:S(2)}) %collective-permute-start.8) | collective-permute-done | bytes 65568 | tf_op jit(solution)/shard_map/ppermute | solution.py:180
  91.4 2.4 %collective-permute-start.11 = (f32[1,16,1024]{2,1,0:T(8,128)S(1)}, f32[1,16,1024]{2,1,0:T(8,128)S(1)}, u32[]{:S(2)}, u32[]{:S(2)}) collective-permute-start(f32[1,16,1024]{2,1,0:T(8,128)S(1)} %select_bitcast_fusion), channel_id=1, source_target_pairs={{0,128},{32,160},{64,192},{96,224},{128,0},{160,32},{192,64},{224,... | collective-permute-start | bytes 196616 | tf_op jit(solution)/shard_map/ppermute | solution.py:157
  93.8 1.8 %collective-permute-start.26 = (f32[16,384]{1,0:T(8,128)S(1)}, f32[16,384]{1,0:T(8,128)S(1)}, u32[]{:S(2)}, u32[]{:S(2)}) collective-permute-start(f32[16,384]{1,0:T(8,128)S(1)} %get-tuple-element.24), channel_id=1, source_target_pairs={{0,1},{1,0},{2,3},{3,2},{4,5},{5,4},{6,7},{7,6},{8,9},{9,8},{10,11... | collective-permute-start | bytes 73736 | tf_op jit(solution)/shard_map/ppermute | solution.py:157
  95.6 3.1 %collective-permute-done.11 = f32[1,16,1024]{2,1,0:T(8,128)S(1)} collective-permute-done((f32[1,16,1024]{2,1,0:T(8,128)S(1)}, f32[1,16,1024]{2,1,0:T(8,128)S(1)}, u32[]{:S(2)}, u32[]{:S(2)}) %collective-permute-start.11) | collective-permute-done | bytes 65568 | tf_op jit(solution)/shard_map/ppermute | solution.py:157
  100.2 1.3 collective-permute-start.27
  101.5 2.9 %collective-permute-done.12 = f32[2,16,1024]{2,1,0:T(8,128)S(1)} collective-permute-done((f32[2,16,1024]{2,1,0:T(8,128)S(1)}, f32[2,16,1024]{2,1,0:T(8,128)S(1)}, u32[]{:S(2)}, u32[]{:S(2)}) %collective-permute-start.12) | collective-permute-done | bytes 131104 | tf_op jit(solution)/shard_map/ppermute | solution.py:157
  104.6 2.0 %collective-permute-done.27 = f32[16,768]{1,0:T(8,128)S(1)} collective-permute-done((f32[16,768]{1,0:T(8,128)S(1)}, f32[16,768]{1,0:T(8,128)S(1)}, u32[]{:S(2)}, u32[]{:S(2)}) %collective-permute-start.27) | collective-permute-done | bytes 49184 | tf_op jit(solution)/shard_map/ppermute | solution.py:180
  106.7 2.4 %collective-permute-start.30 = (f32[1,16,768]{2,1,0:T(8,128)S(1)}, f32[1,16,768]{2,1,0:T(8,128)S(1)}, u32[]{:S(2)}, u32[]{:S(2)}) collective-permute-start(f32[1,16,768]{2,1,0:T(8,128)S(1)} %select_bitcast_fusion.1), channel_id=1, source_target_pairs={{0,128},{32,160},{64,192},{96,224},{128,0},{160,32},{192,64},{224,... | collective-permute-start | bytes 147464 | tf_op jit(solution)/shard_map/ppermute | solution.py:157
  110.1 4.3 %collective-permute-start.15 = (f32[8,16,1024]{2,1,0:T(8,128)S(1)}, f32[8,16,1024]{2,1,0:T(8,128)S(1)}, u32[]{:S(2)}, u32[]{:S(2)}) collective-permute-start(f32[8,16,1024]{2,1,0:T(8,128)S(1)} %pad_maximum_fusion.refs_0_), channel_id=1, source_target_pairs={{0,24},{8,0},{16,8},{24,16},{1,25},{9,1},{17,9},{25,17},{2,26},{10... | collective-permute-start | bytes 1572872 | tf_op jit(solution)/shard_map/ppermute | solution.py:162
  114.4 2.6 %collective-permute-start.31 = (f32[2,16,768]{2,1,0:T(8,128)S(1)}, f32[2,16,768]{2,1,0:T(8,128)S(1)}, u32[]{:S(2)}, u32[]{:S(2)}) collective-permute-start(f32[2,16,768]{2,1,0:T(8,128)S(1)} %pad_maximum_fusion.7), channel_id=1, source_target_pairs={{0,64},{32,96},{64,0},{96,32},{128,192},{160,224},{192,128},{224,1... | collective-permute-start | bytes 294920 | tf_op jit(solution)/shard_map/ppermute | solution.py:157
  117.0 2.0 %collective-permute-done.31 = f32[2,16,768]{2,1,0:T(8,128)S(1)} collective-permute-done((f32[2,16,768]{2,1,0:T(8,128)S(1)}, f32[2,16,768]{2,1,0:T(8,128)S(1)}, u32[]{:S(2)}, u32[]{:S(2)}) %collective-permute-start.31) | collective-permute-done | bytes 98336 | tf_op jit(solution)/shard_map/ppermute | solution.py:157
  119.0 2.2 %collective-permute-start.32 = (f32[4,16,768]{2,1,0:T(8,128)S(1)}, f32[4,16,768]{2,1,0:T(8,128)S(1)}, u32[]{:S(2)}, u32[]{:S(2)}) collective-permute-start(f32[4,16,768]{2,1,0:T(8,128)S(1)} %pad_maximum_fusion.5), channel_id=1, source_target_pairs={{0,32},{32,0},{64,96},{96,64},{128,160},{160,128},{192,224},{224,1... | collective-permute-start | bytes 589832 | tf_op jit(solution)/shard_map/ppermute | solution.py:157
  121.6 3.5 %collective-permute-start.17 = (f32[4,16,1024]{2,1,0:T(8,128)S(1)}, f32[4,16,1024]{2,1,0:T(8,128)S(1)}, u32[]{:S(2)}, u32[]{:S(2)}) collective-permute-start(f32[4,16,1024]{2,1,0:T(8,128)S(1)} %slice.216), channel_id=1, source_target_pairs={{0,24},{8,0},{16,8},{24,16},{1,25},{9,1},{17,9},{25,17},{2,26},{10... | collective-permute-start | bytes 786440 | tf_op jit(solution)/shard_map/ppermute | solution.py:162
  125.2 6.8 %collective-permute-done.16.refs_3_ = f32[4,16,1024]{2,1,0:T(8,128)S(1)} collective-permute-done((f32[4,16,1024]{2,1,0:T(8,128)S(1)}, f32[4,16,1024]{2,1,0:T(8,128)S(1)}, u32[]{:S(2)}, u32[]{:S(2)}) %collective-permute-start.16) | collective-permute-done | bytes 262176 | tf_op jit(solution)/shard_map/ppermute | solution.py:162
  133.5 7.8 %collective-permute-start.18 = (f32[32,16,256]{2,1,0:T(8,128)S(1)}, f32[32,16,256]{2,1,0:T(8,128)}, u32[]{:S(2)}, u32[]{:S(2)}) collective-permute-start(f32[32,16,256]{2,1,0:T(8,128)S(1)} %slice_dynamic-update-slice_fusion.3.refs_5_), channel_id=1, source_target_pairs={{0,1},{1,0},{2,3},{3,2},{4,5},{5,4},{6,7},{7,6},{8,9},{9,8},{10,11... | collective-permute-start | bytes 1572872 | tf_op jit(solution)/shard_map/ppermute | solution.py:157
  141.4 1.5 collective-permute-start.33
  142.8 9.3 %collective-permute-done.34.refs_2_ = f32[8,16,768]{2,1,0:T(8,128)S(1)} collective-permute-done((f32[8,16,768]{2,1,0:T(8,128)S(1)}, f32[8,16,768]{2,1,0:T(8,128)S(1)}, u32[]{:S(2)}, u32[]{:S(2)}) %collective-permute-start.34) | collective-permute-done | bytes 393248 | tf_op jit(solution)/shard_map/ppermute | solution.py:162
  152.8 1.4 collective-permute-start.36
  157.0 1.6 copy-done.5
  158.6 4.0 %solve.2 = (f32[2,512,384]{2,1,0:T(8,128)S(1)}, f32[512,512]{1,0:T(8,128)S(1)}) custom-call(s32[32]{0:T(128)S(1)} %stack.280.index_ref, s32[1]{0:T(128)} %bitcast.core_ref, f32[2,512,512]{2,1,0:T(8,128)S(1)} %copy-done.5, f32[8,16,1024]{2,1,0:T(8,128)S(1)} %pad_maximum_fusion.refs_0_, f32[8,16,1024]{2,1,0:T(8,128)S(1)} %collective-permute-done.14.refs_1_, ...), custom_call_target="tpu_custom_call" | custom-call | flops 1811939328 | bytes 6291456 | tf_op jit(solution)/shard_map/solve/pallas_call | solution.py:107
  162.6 3.9 %solve.3.own2 = f32[2,512,384]{2,1,0:T(8,128)S(1)} custom-call(s32[32]{0:T(128)S(1)} %stack.280.index_ref, s32[1]{0:T(128)} %bitcast.core_ref, f32[2,512,512]{2,1,0:T(8,128)S(1)} %copy-done.5, f32[8,16,768]{2,1,0:T(8,128)S(1)} %pad_maximum_fusion.1.refs_0_, f32[8,16,768]{2,1,0:T(8,128)S(1)} %collective-permute-done.33.refs_1_, ...), custom_call_target="tpu_custom_call" | custom-call | flops 1811939328 | bytes 6291456 | tf_op jit(solution)/shard_map/solve/pallas_call | solution.py:107
  166.5 1.4 collective-permute-start.38
  168.1 2.9 %collective-permute-done.38.other2 = f32[2,512,384]{2,1,0:T(8,128)S(1)} collective-permute-done((f32[2,512,384]{2,1,0:T(8,128)S(1)}, f32[2,512,384]{2,1,0:T(8,128)S(1)}, u32[]{:S(2)}, u32[]{:S(2)}) %collective-permute-start.38) | collective-permute-done | bytes 1572896 | tf_op jit(solution)/shard_map/ppermute | solution.py:157
  171.0 2.2 %collective-permute-done.37.other1 = f32[2,512,384]{2,1,0:T(8,128)S(1)} collective-permute-done((f32[2,512,384]{2,1,0:T(8,128)S(1)}, f32[2,512,384]{2,1,0:T(8,128)S(1)}, u32[]{:S(2)}, u32[]{:S(2)}) %collective-permute-start.37) | collective-permute-done | bytes 1572896 | tf_op jit(solution)/shard_map/ppermute | solution.py:157
  173.2 4.2 %finish.1 = (f32[2,512,1536]{2,1,0:T(8,128)}, f32[16,1536]{1,0:T(8,128)}) custom-call(s32[1]{0:T(128)} %bitcast.core_ref, f32[2,512,384]{2,1,0:T(8,128)S(1)} %get-tuple-element.17.own1, f32[2,512,384]{2,1,0:T(8,128)S(1)} %solve.3.own2, f32[2,512,384]{2,1,0:T(8,128)S(1)} %collective-permute-done.37.other1, f32[2,512,384]{2,1,0:T(8,128)S(1)} %collective-permute-done.38.other2, ...), custom_call_target="tpu_custom_call" | custom-call | tf_op jit(solution)/shard_map/finish/pallas_call | solution.py:142
  (112 shorter events, 16.6 us)
Async XLA Ops:
  13.2 19.2 %collective-permute-start.2 = (f32[16,16,384]{2,1,0:T(8,128)}, f32[16,16,384]{2,1,0:T(8,128)}, u32[]{:S(2)}, u32[]{:S(2)}) collective-permute-start(f32[16,16,384]{2,1,0:T(8,128)} %slice.154), channel_id=1, source_target_pairs={{0,24},{8,16},{16,8},{24,0},{1,25},{9,17},{17,9},{25,1},{2,26},{10... | collective-permute-start | bytes 1179656 | tf_op jit(solution)/shard_map/ppermute | solution.py:157
  18.6 13.8 %copy-start = (f32[1,1,2,16,512]{4,3,2,1,0:T(8,128)S(1)}, f32[1,1,2,16,512]{4,3,2,1,0:T(8,128)}, u32[]{:S(2)}) copy-start(f32[1,1,2,16,512]{4,3,2,1,0:T(8,128)} %param.8) | copy-start | bytes 196612
  18.6 13.8 %copy-start.9 = (f32[32,16,384]{2,1,0:T(8,128)S(1)}, f32[32,16,384]{2,1,0:T(8,128)}, u32[]{:S(2)}) copy-start(f32[32,16,384]{2,1,0:T(8,128)} %get-tuple-element.16) | copy-start | bytes 2359300
  18.6 15.6 %collective-permute-start = (f32[16,16,384]{2,1,0:T(8,128)}, f32[16,16,384]{2,1,0:T(8,128)}, u32[]{:S(2)}, u32[]{:S(2)}) collective-permute-start(f32[16,16,384]{2,1,0:T(8,128)} %slice.150), channel_id=1, source_target_pairs={{0,8},{8,0},{16,24},{24,16},{1,9},{9,1},{17,25},{25,17},{2,10},{10... | collective-permute-start | bytes 1179656 | tf_op jit(solution)/shard_map/ppermute | solution.py:157
  28.7 5.5 %copy-start.7 = (f32[32,16,384]{2,1,0:T(8,128)S(1)}, f32[32,16,384]{2,1,0:T(8,128)}, u32[]{:S(2)}) copy-start(f32[32,16,384]{2,1,0:T(8,128)} %get-tuple-element.15) | copy-start | bytes 2359300
  29.8 10.9 %copy-start.8 = (f32[32,16,384]{2,1,0:T(8,128)S(1)}, f32[32,16,384]{2,1,0:T(8,128)}, u32[]{:S(2)}) copy-start(f32[32,16,384]{2,1,0:T(8,128)} %get-tuple-element.20) | copy-start | bytes 2359300
  29.8 10.9 %collective-permute-start.21 = (f32[16,16,384]{2,1,0:T(8,128)S(1)}, f32[16,16,384]{2,1,0:T(8,128)}, u32[]{:S(2)}, u32[]{:S(2)}) collective-permute-start(f32[16,16,384]{2,1,0:T(8,128)S(1)} %slice.183), channel_id=1, source_target_pairs={{0,24},{8,16},{16,8},{24,0},{1,25},{9,17},{17,9},{25,1},{2,26},{10... | collective-permute-start | bytes 1179656 | tf_op jit(solution)/shard_map/ppermute | solution.py:157
  31.4 10.5 %collective-permute-start.19 = (f32[16,16,384]{2,1,0:T(8,128)S(1)}, f32[16,16,384]{2,1,0:T(8,128)}, u32[]{:S(2)}, u32[]{:S(2)}) collective-permute-start(f32[16,16,384]{2,1,0:T(8,128)S(1)} %slice.179), channel_id=1, source_target_pairs={{0,8},{8,0},{16,24},{24,16},{1,9},{9,1},{17,25},{25,17},{2,10},{10... | collective-permute-start | bytes 1179656 | tf_op jit(solution)/shard_map/ppermute | solution.py:157
  32.4 9.5 %copy-start.6 = (f32[32,16,384]{2,1,0:T(8,128)S(1)}, f32[32,16,384]{2,1,0:T(8,128)}, u32[]{:S(2)}) copy-start(f32[32,16,384]{2,1,0:T(8,128)} %get-tuple-element.19) | copy-start | bytes 2359300
  33.6 10.6 %collective-permute-start.3 = (f32[8,16,384]{2,1,0:T(8,128)S(1)}, f32[8,16,384]{2,1,0:T(8,128)S(1)}, u32[]{:S(2)}, u32[]{:S(2)}) collective-permute-start(f32[8,16,384]{2,1,0:T(8,128)S(1)} %slice.201), channel_id=1, source_target_pairs={{0,8},{8,0},{16,24},{24,16},{1,9},{9,1},{17,25},{25,17},{2,10},{10... | collective-permute-start | bytes 589832 | tf_op jit(solution)/shard_map/ppermute | solution.py:157
  35.3 9.5 %collective-permute-start.1 = (f32[8,16,384]{2,1,0:T(8,128)S(1)}, f32[8,16,384]{2,1,0:T(8,128)S(1)}, u32[]{:S(2)}, u32[]{:S(2)}) collective-permute-start(f32[8,16,384]{2,1,0:T(8,128)S(1)} %slice.199), channel_id=1, source_target_pairs={{0,24},{8,16},{16,8},{24,0},{1,25},{9,17},{17,9},{25,1},{2,26},{10... | collective-permute-start | bytes 589832 | tf_op jit(solution)/shard_map/ppermute | solution.py:157
  41.8 7.1 %collective-permute-start.22 = (f32[8,16,384]{2,1,0:T(8,128)S(1)}, f32[8,16,384]{2,1,0:T(8,128)S(1)}, u32[]{:S(2)}, u32[]{:S(2)}) collective-permute-start(f32[8,16,384]{2,1,0:T(8,128)S(1)} %slice.226), channel_id=1, source_target_pairs={{0,8},{8,0},{16,24},{24,16},{1,9},{9,1},{17,25},{25,17},{2,10},{10... | collective-permute-start | bytes 589832 | tf_op jit(solution)/shard_map/ppermute | solution.py:157
  43.0 5.9 %collective-permute-start.20 = (f32[8,16,384]{2,1,0:T(8,128)S(1)}, f32[8,16,384]{2,1,0:T(8,128)S(1)}, u32[]{:S(2)}, u32[]{:S(2)}) collective-permute-start(f32[8,16,384]{2,1,0:T(8,128)S(1)} %slice.224), channel_id=1, source_target_pairs={{0,24},{8,16},{16,8},{24,0},{1,25},{9,17},{17,9},{25,1},{2,26},{10... | collective-permute-start | bytes 589832 | tf_op jit(solution)/shard_map/ppermute | solution.py:157
  44.9 6.0 %collective-permute-start.4 = (f32[4,2,16,384]{3,2,1,0:T(8,128)S(1)}, f32[4,2,16,384]{3,2,1,0:T(8,128)S(1)}, u32[]{:S(2)}, u32[]{:S(2)}) collective-permute-start(f32[4,2,16,384]{3,2,1,0:T(8,128)S(1)} %pad_maximum_fusion.4), channel_id=1, source_target_pairs={{0,32},{32,0},{64,96},{96,64},{128,160},{160,128},{192,224},{224,1... | collective-permute-start | bytes 589832 | tf_op jit(solution)/shard_map/ppermute | solution.py:157
  48.9 23.7 %copy-start.10 = (f32[1,1,16,1536]{3,2,1,0:T(8,128)S(1)}, f32[1,1,16,1536]{3,2,1,0:T(8,128)}, u32[]{:S(2)}) copy-start(f32[1,1,16,1536]{3,2,1,0:T(8,128)} %param.7) | copy-start | bytes 294916
  49.0 7.8 %collective-permute-start.23 = (f32[4,2,16,384]{3,2,1,0:T(8,128)S(1)}, f32[4,2,16,384]{3,2,1,0:T(8,128)S(1)}, u32[]{:S(2)}, u32[]{:S(2)}) collective-permute-start(f32[4,2,16,384]{3,2,1,0:T(8,128)S(1)} %pad_maximum_fusion.3), channel_id=1, source_target_pairs={{0,32},{32,0},{64,96},{96,64},{128,160},{160,128},{192,224},{224,1... | collective-permute-start | bytes 589832 | tf_op jit(solution)/shard_map/ppermute | solution.py:157
  50.9 8.2 %collective-permute-start.5 = (f32[2,2,16,384]{3,2,1,0:T(8,128)S(1)}, f32[2,2,16,384]{3,2,1,0:T(8,128)S(1)}, u32[]{:S(2)}, u32[]{:S(2)}) collective-permute-start(f32[2,2,16,384]{3,2,1,0:T(8,128)S(1)} %slice.205), channel_id=1, source_target_pairs={{0,64},{32,96},{64,0},{96,32},{128,192},{160,224},{192,128},{224,1... | collective-permute-start | bytes 294920 | tf_op jit(solution)/shard_map/ppermute | solution.py:157
  56.9 7.0 %collective-permute-start.24 = (f32[2,2,16,384]{3,2,1,0:T(8,128)S(1)}, f32[2,2,16,384]{3,2,1,0:T(8,128)S(1)}, u32[]{:S(2)}, u32[]{:S(2)}) collective-permute-start(f32[2,2,16,384]{3,2,1,0:T(8,128)S(1)} %slice.230), channel_id=1, source_target_pairs={{0,64},{32,96},{64,0},{96,32},{128,192},{160,224},{192,128},{224,1... | collective-permute-start | bytes 294920 | tf_op jit(solution)/shard_map/ppermute | solution.py:157
  59.1 12.0 %collective-permute-start.6 = (f32[1,2,16,384]{3,2,1,0:T(8,128)S(1)}, f32[1,2,16,384]{3,2,1,0:T(8,128)S(1)}, u32[]{:S(2)}, u32[]{:S(2)}) collective-permute-start(f32[1,2,16,384]{3,2,1,0:T(8,128)S(1)} %slice.207), channel_id=1, source_target_pairs={{0,128},{32,160},{64,192},{96,224},{128,0},{160,32},{192,64},{224,... | collective-permute-start | bytes 147464 | tf_op jit(solution)/shard_map/ppermute | solution.py:157
  63.8 8.7 %collective-permute-start.25 = (f32[1,2,16,384]{3,2,1,0:T(8,128)S(1)}, f32[1,2,16,384]{3,2,1,0:T(8,128)S(1)}, u32[]{:S(2)}, u32[]{:S(2)}) collective-permute-start(f32[1,2,16,384]{3,2,1,0:T(8,128)S(1)} %slice.232), channel_id=1, source_target_pairs={{0,128},{32,160},{64,192},{96,224},{128,0},{160,32},{192,64},{224,... | collective-permute-start | bytes 147464 | tf_op jit(solution)/shard_map/ppermute | solution.py:157
  72.6 9.6 %collective-permute-start.7 = (f32[16,640]{1,0:T(8,128)S(1)}, f32[16,640]{1,0:T(8,128)S(1)}, u32[]{:S(2)}, u32[]{:S(2)}) collective-permute-start(f32[16,640]{1,0:T(8,128)S(1)} %pad_maximum_fusion.10), channel_id=1, source_target_pairs={{0,1},{1,0},{2,3},{3,2},{4,5},{5,4},{6,7},{7,6},{8,9},{9,8},{10,11... | collective-permute-start | bytes 122888 | tf_op jit(solution)/shard_map/ppermute | solution.py:157
  82.2 2.7 %collective-permute-start.10 = (f32[16,1024]{1,0:T(8,128)S(1)}, f32[16,1024]{1,0:T(8,128)S(1)}, u32[]{:S(2)}, u32[]{:S(2)}) collective-permute-start(f32[16,1024]{1,0:T(8,128)S(1)} %pad_maximum_fusion.8), channel_id=1, source_target_pairs={{6,4},{7,5},{14,12},{15,13},{22,20},{23,21},{30,28},{31,29},{38,36... | collective-permute-start | bytes 196616 | tf_op jit(solution)/shard_map/ppermute | solution.py:180
  82.9 2.0 %collective-permute-start.9 = (f32[16,1024]{1,0:T(8,128)S(1)}, f32[16,1024]{1,0:T(8,128)S(1)}, u32[]{:S(2)}, u32[]{:S(2)}) collective-permute-start(f32[16,1024]{1,0:T(8,128)S(1)} %pad_maximum_fusion.8), channel_id=1, source_target_pairs={{6,2},{7,3},{14,10},{15,11},{22,18},{23,19},{30,26},{31,27},{38,34... | collective-permute-start | bytes 196616 | tf_op jit(solution)/shard_map/ppermute | solution.py:180
  83.6 7.8 %collective-permute-start.8 = (f32[16,1024]{1,0:T(8,128)S(1)}, f32[16,1024]{1,0:T(8,128)S(1)}, u32[]{:S(2)}, u32[]{:S(2)}) collective-permute-start(f32[16,1024]{1,0:T(8,128)S(1)} %pad_maximum_fusion.8), channel_id=1, source_target_pairs={{6,0},{7,1},{14,8},{15,9},{22,16},{23,17},{30,24},{31,25},{38,32},... | collective-permute-start | bytes 196616 | tf_op jit(solution)/shard_map/ppermute | solution.py:180
  91.4 7.3 %collective-permute-start.11 = (f32[1,16,1024]{2,1,0:T(8,128)S(1)}, f32[1,16,1024]{2,1,0:T(8,128)S(1)}, u32[]{:S(2)}, u32[]{:S(2)}) collective-permute-start(f32[1,16,1024]{2,1,0:T(8,128)S(1)} %select_bitcast_fusion), channel_id=1, source_target_pairs={{0,128},{32,160},{64,192},{96,224},{128,0},{160,32},{192,64},{224,... | collective-permute-start | bytes 196616 | tf_op jit(solution)/shard_map/ppermute | solution.py:157
  93.8 5.0 %collective-permute-start.26 = (f32[16,384]{1,0:T(8,128)S(1)}, f32[16,384]{1,0:T(8,128)S(1)}, u32[]{:S(2)}, u32[]{:S(2)}) collective-permute-start(f32[16,384]{1,0:T(8,128)S(1)} %get-tuple-element.24), channel_id=1, source_target_pairs={{0,1},{1,0},{2,3},{3,2},{4,5},{5,4},{6,7},{7,6},{8,9},{9,8},{10,11... | collective-permute-start | bytes 73736 | tf_op jit(solution)/shard_map/ppermute | solution.py:157
  98.7 5.7 %collective-permute-start.12 = (f32[2,16,1024]{2,1,0:T(8,128)S(1)}, f32[2,16,1024]{2,1,0:T(8,128)S(1)}, u32[]{:S(2)}, u32[]{:S(2)}) collective-permute-start(f32[2,16,1024]{2,1,0:T(8,128)S(1)} %pad_maximum_fusion.6), channel_id=1, source_target_pairs={{0,64},{32,96},{64,0},{96,32},{128,192},{160,224},{192,128},{224,1... | collective-permute-start | bytes 393224 | tf_op jit(solution)/shard_map/ppermute | solution.py:157
  98.9 5.7 %collective-permute-start.29 = (f32[16,768]{1,0:T(8,128)S(1)}, f32[16,768]{1,0:T(8,128)S(1)}, u32[]{:S(2)}, u32[]{:S(2)}) collective-permute-start(f32[16,768]{1,0:T(8,128)S(1)} %pad_maximum_fusion.9), channel_id=1, source_target_pairs={{6,4},{7,5},{14,12},{15,13},{22,20},{23,21},{30,28},{31,29},{38,36... | collective-permute-start | bytes 147464 | tf_op jit(solution)/shard_map/ppermute | solution.py:180
  99.5 5.1 %collective-permute-start.28 = (f32[16,768]{1,0:T(8,128)S(1)}, f32[16,768]{1,0:T(8,128)S(1)}, u32[]{:S(2)}, u32[]{:S(2)}) collective-permute-start(f32[16,768]{1,0:T(8,128)S(1)} %pad_maximum_fusion.9), channel_id=1, source_target_pairs={{6,2},{7,3},{14,10},{15,11},{22,18},{23,19},{30,26},{31,27},{38,34... | collective-permute-start | bytes 147464 | tf_op jit(solution)/shard_map/ppermute | solution.py:180
  100.2 6.4 %collective-permute-start.27 = (f32[16,768]{1,0:T(8,128)S(1)}, f32[16,768]{1,0:T(8,128)S(1)}, u32[]{:S(2)}, u32[]{:S(2)}) collective-permute-start(f32[16,768]{1,0:T(8,128)S(1)} %pad_maximum_fusion.9), channel_id=1, source_target_pairs={{6,0},{7,1},{14,8},{15,9},{22,16},{23,17},{30,24},{31,25},{38,32},... | collective-permute-start | bytes 147464 | tf_op jit(solution)/shard_map/ppermute | solution.py:180
  104.5 5.6 %collective-permute-start.13 = (f32[4,16,1024]{2,1,0:T(8,128)S(1)}, f32[4,16,1024]{2,1,0:T(8,128)S(1)}, u32[]{:S(2)}, u32[]{:S(2)}) collective-permute-start(f32[4,16,1024]{2,1,0:T(8,128)S(1)} %pad_maximum_fusion.2), channel_id=1, source_target_pairs={{0,32},{32,0},{64,96},{96,64},{128,160},{160,128},{192,224},{224,1... | collective-permute-start | bytes 786440 | tf_op jit(solution)/shard_map/ppermute | solution.py:157
  106.7 7.7 %collective-permute-start.30 = (f32[1,16,768]{2,1,0:T(8,128)S(1)}, f32[1,16,768]{2,1,0:T(8,128)S(1)}, u32[]{:S(2)}, u32[]{:S(2)}) collective-permute-start(f32[1,16,768]{2,1,0:T(8,128)S(1)} %select_bitcast_fusion.1), channel_id=1, source_target_pairs={{0,128},{32,160},{64,192},{96,224},{128,0},{160,32},{192,64},{224,... | collective-permute-start | bytes 147464 | tf_op jit(solution)/shard_map/ppermute | solution.py:157
  110.1 11.5 %collective-permute-start.15 = (f32[8,16,1024]{2,1,0:T(8,128)S(1)}, f32[8,16,1024]{2,1,0:T(8,128)S(1)}, u32[]{:S(2)}, u32[]{:S(2)}) collective-permute-start(f32[8,16,1024]{2,1,0:T(8,128)S(1)} %pad_maximum_fusion.refs_0_), channel_id=1, source_target_pairs={{0,24},{8,0},{16,8},{24,16},{1,25},{9,1},{17,9},{25,17},{2,26},{10... | collective-permute-start | bytes 1572872 | tf_op jit(solution)/shard_map/ppermute | solution.py:162
  114.4 10.7 %collective-permute-start.14 = (f32[8,16,1024]{2,1,0:T(8,128)S(1)}, f32[8,16,1024]{2,1,0:T(8,128)S(1)}, u32[]{:S(2)}, u32[]{:S(2)}) collective-permute-start(f32[8,16,1024]{2,1,0:T(8,128)S(1)} %pad_maximum_fusion.refs_0_), channel_id=1, source_target_pairs={{0,8},{8,16},{16,24},{24,0},{1,9},{9,17},{17,25},{25,1},{2,10},{10... | collective-permute-start | bytes 1572872 | tf_op jit(solution)/shard_map/ppermute | solution.py:162
  114.4 4.6 %collective-permute-start.31 = (f32[2,16,768]{2,1,0:T(8,128)S(1)}, f32[2,16,768]{2,1,0:T(8,128)S(1)}, u32[]{:S(2)}, u32[]{:S(2)}) collective-permute-start(f32[2,16,768]{2,1,0:T(8,128)S(1)} %pad_maximum_fusion.7), channel_id=1, source_target_pairs={{0,64},{32,96},{64,0},{96,32},{128,192},{160,224},{192,128},{224,1... | collective-permute-start | bytes 294920 | tf_op jit(solution)/shard_map/ppermute | solution.py:157
  119.0 22.3 %collective-permute-start.32 = (f32[4,16,768]{2,1,0:T(8,128)S(1)}, f32[4,16,768]{2,1,0:T(8,128)S(1)}, u32[]{:S(2)}, u32[]{:S(2)}) collective-permute-start(f32[4,16,768]{2,1,0:T(8,128)S(1)} %pad_maximum_fusion.5), channel_id=1, source_target_pairs={{0,32},{32,0},{64,96},{96,64},{128,160},{160,128},{192,224},{224,1... | collective-permute-start | bytes 589832 | tf_op jit(solution)/shard_map/ppermute | solution.py:157
  121.6 11.2 %collective-permute-start.17 = (f32[4,16,1024]{2,1,0:T(8,128)S(1)}, f32[4,16,1024]{2,1,0:T(8,128)S(1)}, u32[]{:S(2)}, u32[]{:S(2)}) collective-permute-start(f32[4,16,1024]{2,1,0:T(8,128)S(1)} %slice.216), channel_id=1, source_target_pairs={{0,24},{8,0},{16,8},{24,16},{1,25},{9,1},{17,9},{25,17},{2,26},{10... | collective-permute-start | bytes 786440 | tf_op jit(solution)/shard_map/ppermute | solution.py:162
  125.1 6.9 %collective-permute-start.16 = (f32[4,16,1024]{2,1,0:T(8,128)S(1)}, f32[4,16,1024]{2,1,0:T(8,128)S(1)}, u32[]{:S(2)}, u32[]{:S(2)}) collective-permute-start(f32[4,16,1024]{2,1,0:T(8,128)S(1)} %slice.215), channel_id=1, source_target_pairs={{0,8},{8,16},{16,24},{24,0},{1,9},{9,17},{17,25},{25,1},{2,10},{10... | collective-permute-start | bytes 786440 | tf_op jit(solution)/shard_map/ppermute | solution.py:162
  133.5 21.6 %collective-permute-start.18 = (f32[32,16,256]{2,1,0:T(8,128)S(1)}, f32[32,16,256]{2,1,0:T(8,128)}, u32[]{:S(2)}, u32[]{:S(2)}) collective-permute-start(f32[32,16,256]{2,1,0:T(8,128)S(1)} %slice_dynamic-update-slice_fusion.3.refs_5_), channel_id=1, source_target_pairs={{0,1},{1,0},{2,3},{3,2},{4,5},{5,4},{6,7},{7,6},{8,9},{9,8},{10,11... | collective-permute-start | bytes 1572872 | tf_op jit(solution)/shard_map/ppermute | solution.py:157
  141.3 10.8 %collective-permute-start.34 = (f32[8,16,768]{2,1,0:T(8,128)S(1)}, f32[8,16,768]{2,1,0:T(8,128)S(1)}, u32[]{:S(2)}, u32[]{:S(2)}) collective-permute-start(f32[8,16,768]{2,1,0:T(8,128)S(1)} %pad_maximum_fusion.1.refs_0_), channel_id=1, source_target_pairs={{0,24},{8,0},{16,8},{24,16},{1,25},{9,1},{17,9},{25,17},{2,26},{10... | collective-permute-start | bytes 1179656 | tf_op jit(solution)/shard_map/ppermute | solution.py:162
  141.4 12.9 %collective-permute-start.33 = (f32[8,16,768]{2,1,0:T(8,128)S(1)}, f32[8,16,768]{2,1,0:T(8,128)S(1)}, u32[]{:S(2)}, u32[]{:S(2)}) collective-permute-start(f32[8,16,768]{2,1,0:T(8,128)S(1)} %pad_maximum_fusion.1.refs_0_), channel_id=1, source_target_pairs={{0,8},{8,16},{16,24},{24,0},{1,9},{9,17},{17,25},{25,1},{2,10},{10... | collective-permute-start | bytes 1179656 | tf_op jit(solution)/shard_map/ppermute | solution.py:162
  152.8 9.7 %collective-permute-start.36 = (f32[4,16,768]{2,1,0:T(8,128)}, f32[4,16,768]{2,1,0:T(8,128)}, u32[]{:S(2)}, u32[]{:S(2)}) collective-permute-start(f32[4,16,768]{2,1,0:T(8,128)} %slice.237), channel_id=1, source_target_pairs={{0,24},{8,0},{16,8},{24,16},{1,25},{9,1},{17,9},{25,17},{2,26},{10... | collective-permute-start | bytes 589832 | tf_op jit(solution)/shard_map/ppermute | solution.py:162
  155.0 7.6 %collective-permute-start.35 = (f32[4,16,768]{2,1,0:T(8,128)}, f32[4,16,768]{2,1,0:T(8,128)}, u32[]{:S(2)}, u32[]{:S(2)}) collective-permute-start(f32[4,16,768]{2,1,0:T(8,128)} %slice.236), channel_id=1, source_target_pairs={{0,8},{8,16},{16,24},{24,0},{1,9},{9,17},{17,25},{25,1},{2,10},{10... | collective-permute-start | bytes 589832 | tf_op jit(solution)/shard_map/ppermute | solution.py:162
  155.1 1.0 copy-start.2
  156.1 0.9 copy-start.4
  157.0 1.6 copy-start.5
  166.5 4.5 %collective-permute-start.38 = (f32[2,512,384]{2,1,0:T(8,128)S(1)}, f32[2,512,384]{2,1,0:T(8,128)S(1)}, u32[]{:S(2)}, u32[]{:S(2)}) collective-permute-start(f32[2,512,384]{2,1,0:T(8,128)S(1)} %solve.3.own2), channel_id=1, source_target_pairs={{0,1},{1,0},{2,3},{3,2},{4,5},{5,4},{6,7},{7,6},{8,9},{9,8},{10,11... | collective-permute-start | bytes 4718600 | tf_op jit(solution)/shard_map/ppermute | solution.py:157
  168.0 5.3 %collective-permute-start.37 = (f32[2,512,384]{2,1,0:T(8,128)S(1)}, f32[2,512,384]{2,1,0:T(8,128)S(1)}, u32[]{:S(2)}, u32[]{:S(2)}) collective-permute-start(f32[2,512,384]{2,1,0:T(8,128)S(1)} %get-tuple-element.17.own1), channel_id=1, source_target_pairs={{0,1},{1,0},{2,3},{3,2},{4,5},{5,4},{6,7},{7,6},{8,9},{9,8},{10,11... | collective-permute-start | bytes 4718600 | tf_op jit(solution)/shard_map/ppermute | solution.py:157
  (2 other events, 1.4 us)
where the time goes:
time: 178 us
  starting transfers between devices  75.9 us (43%)
  waiting for transfers between devices  50.5 us (28%)
  Pallas kernels  32.2 us (18%)
  local copies, waits for them, and re-layouts  13 us (7%)
  other arithmetic  4.65 us (3%)
    ppermute x25, starting transfers between devices, swap(): lax.ppermute(x, axis, [(i, i ^ bit) for i in range(lax.axis_size(axis))])  59.8 us
    ppermute x25, waiting for transfers between devices, swap(): lax.ppermute(x, axis, [(i, i ^ bit) for i in range(lax.axis_size(axis))])  25.5 us
    pallas_call x2, Pallas kernels, term(): pl.pallas_call(term_kernel, grid_spec=pltpu.PrefetchScalarGridSpec(num_sc...  20.1 us
    ppermute x8, waiting for transfers between devices, step(): return lax.ppermute(x, axis, [(i, (i + by) % n) for i in range(n)])  16.4 us
    ppermute x8, starting transfers between devices, step(): return lax.ppermute(x, axis, [(i, (i + by) % n) for i in range(n)])  10.9 us
    ppermute x6, waiting for transfers between devices, spread_x(): others = [lax.ppermute(v, 'x', [(NX - 1, i)]) for i in range(NX - 1)]  8.53 us
    pallas_call x2, Pallas kernels, solve(): pl.pallas_call(functools.partial(solve_kernel, counts, with_link), in_spe...  7.87 us
    slice x4, local copies, waits for them, and re-layouts, reduce_rows(): s = s[:16] + swap(s[16:], 'y', first)  5.7 us
  transfers between devices with their start and end apart: 39, of which 17 were waited for; matrix products, arithmetic and copies ran while one was open for 6% of the time, Pallas kernels for 8%

commit v1 on v0

--- a/solution.py
+++ b/solution.py
@@ -12,10 +12,6 @@
 SLAB = 16
 HALF = 768
 PART = 384
-BITREV = (0, 4, 2, 6, 1, 5, 3, 7)
-HALVES = (((0, 3, 1, 2), (1, 3)), ((0, 1, 3, 2), (3, 1)))
-
-
 def split(x):
     high = x.astype(jnp.bfloat16)
     return high, (x - high.astype(jnp.float32)).astype(jnp.bfloat16)
@@ -28,7 +24,8 @@
     return mul(ah, bh) + (mul(ah, bl) + mul(al, bh))
 
 
-def term_kernel(index_ref, c_ref, ea_ref, eb_ref, oa_ref, ob_ref, acc):
+def term_kernel(y_ref, c_ref, ea_ref, eb_ref, *refs):
+    outs, acc = refs[:NY], refs[NY]
     k = pl.program_id(0)
     product = dot3(c_ref[0], jnp.concatenate([ea_ref[0], eb_ref[0]], axis=1))
 
@@ -42,14 +39,14 @@
 
     @pl.when(k == pl.num_programs(0) - 1)
     def _():
-        for half, o_ref in enumerate((oa_ref, ob_ref)):
-            for i in range(NZ * NY):
-                row = pl.multiple_of(index_ref[half * NZ * NY + i] * SLAB, SLAB)
-                o_ref[i] = acc[pl.ds(row, SLAB), half * PART : (half + 1) * PART]
-
-
-def term(index, coupling, earlier, chunk):
-    out = pl.BlockSpec((NZ * NY, SLAB, PART), lambda k, i: (0, 0, 0))
+        for ky, o_ref in enumerate(outs):
+            for z in range(NZ):
+                row = pl.multiple_of((z * NY + (y_ref[0] ^ ky)) * SLAB, SLAB)
+                o_ref[z] = acc[pl.ds(row, SLAB), :]
+
+
+def term(y, coupling, earlier, chunk):
+    out = pl.BlockSpec((NZ, SLAB, HALF), lambda k, i: (0, 0, 0))
     return pl.pallas_call(
         term_kernel,
         grid_spec=pltpu.PrefetchScalarGridSpec(
@@ -60,16 +57,16 @@
                 pl.BlockSpec((1, 512, PART), lambda k, i: (k, 0, chunk)),
                 pl.BlockSpec((1, 512, PART), lambda k, i: (k, 0, 2 + chunk)),
             ],
-            out_specs=(out, out),
+            out_specs=(out,) * NY,
             scratch_shapes=[pltpu.VMEM((512, HALF), jnp.float32)],
         ),
-        out_shape=(jax.ShapeDtypeStruct((NZ * NY, SLAB, PART), jnp.float32),) * 2,
+        out_shape=(jax.ShapeDtypeStruct((NZ, SLAB, HALF), jnp.float32),) * NY,
         compiler_params=pltpu.CompilerParams(vmem_limit_bytes=56 * 2**20),
         cost_estimate=pl.CostEstimate(
             flops=6 * 512 * 2048 * HALF, bytes_accessed=12 * 2**20, transcendentals=0
         ),
         name="term",
-    )(index, coupling, earlier, earlier)
+    )(y, coupling, earlier, earlier)
 
 
 def solve_kernel(counts, with_link, index_ref, core_ref, inv_ref, *refs):
@@ -162,18 +159,19 @@
     return lax.ppermute(x, axis, [(i, (i + by) % n) for i in range(n)])
 
 
-def reduce_rows(slabs):
-    near = []
-    for half in (0, 1):
-        first, second = HALVES[half][1]
-        s = slabs[half]
-        s = s[:16] + swap(s[16:], "y", first)
-        near.append(s[:8] + swap(s[8:], "y", second))
-    s = jnp.stack(near, axis=1)
-    s = s[:4] + swap(s[4:], "z", 1)
-    s = s[:2] + swap(s[2:], "z", 2)
-    s = s[:1] + swap(s[1:], "z", 4)
-    return s[0, 0], s[0, 1]
+def after(x, *others):
+    return lax.optimization_barrier((x, *others))[0]
+
+
+def sum_y(slabs):
+    near = slabs[0]
+    for ky in range(1, NY):
+        near = near + swap(slabs[ky], "y", ky)
+    return near
+
+
+def sum_z(near):
+    return jnp.sum(lax.all_to_all(near, "z", 0, 0, tiled=True), axis=0)
 
 
 def spread_x(v):
@@ -181,56 +179,70 @@
     return jnp.where(lax.axis_index("x") == NX - 1, v, others[0] + others[1] + others[2])
 
 
-def gather_rows(v):
-    v = v[None]
-    for bit in (4, 2, 1):
-        v = jnp.concatenate([v, swap(v, "z", bit)])
+def gather_z(v):
+    return lax.all_to_all(jnp.broadcast_to(v, (NZ, *v.shape)), "z", 0, 0, tiled=True)
+
+
+def gather_y_once(v):
+    return [v] + [swap(v, "y", ky) for ky in range(1, NY)]
+
+
+def gather_y_twice(v):
     up, down = step(v, "y", 1), step(v, "y", -1)
-    return [v, up, down, step(up[:4], "y", 1), step(down[4:], "y", -1)]
+    h = v.shape[0] // 2
+    return [v, up, down, step(up[:h], "y", 1), step(down[h:], "y", -1)]
 
 
 def local(coupling, earlier, right_sides, panel_blocks, block_inverses):
-    z, y, core = (lax.axis_index(a) for a in ("z", "y", "core"))
+    y, core = lax.axis_index("y"), lax.axis_index("core")
     coupling, earlier = coupling[0, 0, :, 0], earlier[:, 0]
     right, panel = right_sides[0, 0], panel_blocks[0, 0]
     is_first = core == 0
     core_id = core.astype(jnp.int32).reshape(1)
-
-    slab_order = [(z ^ kz) * NY + (y ^ ky) for order, _ in HALVES for ky in order for kz in BITREV]
-    slab_order = jnp.stack(slab_order).astype(jnp.int32)
-    offsets = ((0, BITREV), (-1, BITREV), (1, BITREV), (2, BITREV[:4]), (2, BITREV[4:]))
-    row_order = [(z ^ kz) * NY + (y + oy) % NY for oy, along in offsets for kz in along]
-    row_order = jnp.stack(row_order).astype(jnp.int32)
-
-    bases, solutions = [], []
-    link = None
-    for chunk in (0, 1):
-        slabs = term(slab_order, coupling, earlier, chunk)
-        if chunk == 0:
-            slabs, coupling = lax.optimization_barrier((slabs, coupling))
-        total = reduce_rows(slabs)
+    y_id = y.astype(jnp.int32).reshape(1)
+    order_a = [z * NY + (y ^ ky) for ky in range(NY) for z in range(NZ)]
+    order_b = [z * NY + (y + oy) % NY for oy in (0, -1, 1, 2) for z in range(NZ)]
+    order_a, order_b = (jnp.stack(order).astype(jnp.int32) for order in (order_a, order_b))
+
+    def halves(total, chunk):
         at = chunk * PART
-        base = right[:, at : at + PART] - total[0], right[:, HALF + at : HALF + at + PART] - total[1]
-        bases += base
+        return (
+            right[:, at : at + PART] - total[:, :PART],
+            right[:, HALF + at : HALF + at + PART] - total[:, PART:],
+        )
+
+    def exchange(base, extra):
         kept = jnp.where(is_first, base[0], base[1])
         given = jnp.where(is_first, base[1], base[0])
-        if chunk == 0:
-            given = jnp.concatenate([given, panel[0, :, 256:]], axis=1)
+        if extra is not None:
+            given = jnp.concatenate([given, extra[:, 256:]], axis=1)
         came = swap(given, "core", 1)
         last = jnp.where(is_first, came[:, :PART], kept)
         other = jnp.where(is_first, kept, came[:, :PART])
         v = [last, other]
-        if chunk == 0:
-            v.append(jnp.where(is_first, panel[0, :, :256], came[:, PART:]))
-        pieces = gather_rows(spread_x(jnp.concatenate(v, axis=1)))
-        if chunk == 0:
-            part = jnp.concatenate([p[:, :, HALF:] for p in pieces])
-            own, link = solve(row_order, core_id, block_inverses, pieces, (part, swap(part, "core", 1)))
-        else:
-            own = solve(row_order, core_id, block_inverses, pieces, (link,))
-        solutions.append((own, swap(own, "core", 1)))
-    (own1, other1), (own2, other2) = solutions
-    solved, pending = finish(core_id, own1, own2, other1, other2, *bases, panel)
+        if extra is not None:
+            v.append(jnp.where(is_first, extra[:, :256], came[:, PART:]))
+        return jnp.concatenate(v, axis=1)
+
+    slabs_a = term(y_id, coupling, earlier, 0)
+    slabs_b = term(y_id, after(coupling, *slabs_a), earlier, 1)
+    base_a = halves(sum_z(sum_y(slabs_a)), 0)
+    v_a = exchange(base_a, panel[0])
+    base_b = halves(sum_z(after(sum_y(slabs_b), v_a)), 1)
+    v_a = gather_z(after(spread_x(v_a), *base_b))
+    v_b = exchange(tuple(after(part, v_a) for part in base_b), None)
+    v_b = gather_z(spread_x(v_b))
+    pieces_a = [after(p, v_b) for p in gather_y_once(v_a)]
+    pieces_b = gather_y_twice(v_b)
+
+    part = jnp.concatenate([p[:, :, HALF:] for p in pieces_a])
+    part = after(part, *pieces_b[1:3])
+    links = part, swap(part, "core", 1)
+    own_a, link = solve(order_a, core_id, block_inverses, pieces_a, links)
+    other_a = swap(own_a, "core", 1)
+    own_b = solve(order_b, core_id, block_inverses, pieces_b, (after(link, other_a),))
+    other_b = swap(own_b, "core", 1)
+    solved, pending = finish(core_id, own_a, own_b, other_a, other_b, *base_a, *base_b, panel)
     return solved, pending[None, None]
 
 

time: 178 us -> 209 us (1.17)
  waiting for transfers between devices: 50.5 us -> 80.8 us
  starting transfers between devices: 75.9 us -> 56.4 us
  blocking collectives: 0 us -> 17.3 us
  local copies, waits for them, and re-layouts: 13 us -> 18.1 us
    ppermute x25 -> x14, starting transfers between devices: 59.8 us -> 28.6 us  [swap(): lax.ppermute(x, axis, [(i, i ^ bit) for i in range(lax.axis_size(axis))])]
    ppermute x25 -> x14, waiting for transfers between devices: 25.5 us -> 43.7 us  [swap(): lax.ppermute(x, axis, [(i, i ^ bit) for i in range(lax.axis_size(axis))])]
    all_to_all x0 -> x3, starting transfers between devices: none -> 18 us  [the longest x2 14.6 us: sum_z(): return jnp.sum(lax.all_to_all(near, 'z', 0, 0, tiled=True), axis=0)]
    all_to_all x0 -> x1, blocking collectives: none -> 17.3 us  [gather_z(): lax.all_to_all(jnp.broadcast_to(v, (NZ, *v.shape)), 'z', 0, 0, tiled=True)]
    all_to_all x0 -> x3, waiting for transfers between devices: none -> 10.8 us  [the longest x1 9.25 us: gather_z(): lax.all_to_all(jnp.broadcast_to(v, (NZ, *v.shape)), 'z', 0, 0, tiled=True)]
    unnamed x26 -> x44, local copies, waits for them, and re-layouts: 4.94 us -> 15.7 us
    ppermute x8 -> x4, starting transfers between devices: 10.9 us -> 4.57 us  [step(): return lax.ppermute(x, axis, [(i, (i + by) % n) for i in range(n)])]
    slice x16 -> x7, local copies, waits for them, and re-layouts: 7.23 us -> 1.44 us  [the longest x2 1.4 us: gather_y_twice(): return [v, up, down, step(up[:h], 'y', 1), step(down[h:], 'y', -1)]]
  transfers between devices with their start and end apart: 39 -> 27, of which waited for: 17 -> 16; matrix products, arithmetic and copies ran while one was open for 6% -> 2% of each run, Pallas kernels for 8% -> 5%
where the time goes in v1:
time: 209 us; the launch traced here: 208 us
  waiting for transfers between devices  80.8 us (39%)
  starting transfers between devices  56.4 us (27%)
  Pallas kernels  30.2 us (14%)
  local copies, waits for them, and re-layouts  18.1 us (9%)
  blocking collectives  17.3 us (8%)
  other arithmetic  3.82 us (2%)
    ppermute x14, waiting for transfers between devices, swap(): lax.ppermute(x, axis, [(i, i ^ bit) for i in range(lax.axis_size(axis))])  43.7 us
    ppermute x14, starting transfers between devices, swap(): lax.ppermute(x, axis, [(i, i ^ bit) for i in range(lax.axis_size(axis))])  28.6 us
    pallas_call x2, Pallas kernels, term(): pl.pallas_call(term_kernel, grid_spec=pltpu.PrefetchScalarGridSpec(num_sc...  18.7 us
    all_to_all x1, blocking collectives, gather_z(): lax.all_to_all(jnp.broadcast_to(v, (NZ, *v.shape)), 'z', 0, 0, tiled=True)  17.3 us
    unnamed x44, local copies, waits for them, and re-layouts  15.7 us
    ppermute x4, waiting for transfers between devices, step(): return lax.ppermute(x, axis, [(i, (i + by) % n) for i in range(n)])  15 us
    all_to_all x2, starting transfers between devices, sum_z(): return jnp.sum(lax.all_to_all(near, 'z', 0, 0, tiled=True), axis=0)  14.6 us
    ppermute x6, waiting for transfers between devices, spread_x(): others = [lax.ppermute(v, 'x', [(NX - 1, i)]) for i in range(NX - 1)]  11.2 us
  transfers between devices with their start and end apart: 27, of which 16 were waited for; matrix products, arithmetic and copies ran while one was open for 2% of the time, Pallas kernels for 5%

profile of v1, /device:TPU:1, one launch (start us, length us, event | category | flops | bytes accessed | tf_op | source)
XLA Modules:
  0.0 207.7 jit_solution(3276632030674872824)
XLA Ops:
  0.6 9.3 %term.2 = (f32[8,16,768]{2,1,0:T(8,128)}, f32[8,16,768]{2,1,0:T(8,128)}, f32[8,16,768]{2,1,0:T(8,128)}, f32[8,16,768]{2,1,0:T(8,128)}) custom-call(s32[1]{0:T(128)} %bitcast.1.y_ref, f32[4,512,512]{2,1,0:T(8,128)} %bitcast.77, f32[4,512,1536]{2,1,0:T(8,128)} %bitcast.73, f32[4,512,1536]{2,1,0:T(8,128)} %bitcast.74), custom_call_target="tpu_custom_call" | custom-call | flops 4831838208 | bytes 12582912 | tf_op jit(solution)/shard_map/term/pallas_call | solution.py:50
  10.0 2.1 %collective-permute-start = (f32[8,16,768]{2,1,0:T(8,128)}, f32[8,16,768]{2,1,0:T(8,128)S(1)}, u32[]{:S(2)}, u32[]{:S(2)}) collective-permute-start(f32[8,16,768]{2,1,0:T(8,128)} %get-tuple-element.26), channel_id=1, source_target_pairs={{0,8},{8,0},{16,24},{24,16},{1,9},{9,1},{17,25},{25,17},{2,10},{10... | collective-permute-start | bytes 1179656 | tf_op jit(solution)/shard_map/ppermute | solution.py:154
  12.1 2.6 %collective-permute-start.1 = (f32[8,16,768]{2,1,0:T(8,128)}, f32[8,16,768]{2,1,0:T(8,128)S(1)}, u32[]{:S(2)}, u32[]{:S(2)}) collective-permute-start(f32[8,16,768]{2,1,0:T(8,128)} %get-tuple-element.27), channel_id=1, source_target_pairs={{0,16},{8,24},{16,0},{24,8},{1,17},{9,25},{17,1},{25,9},{2,18},{10... | collective-permute-start | bytes 1179656 | tf_op jit(solution)/shard_map/ppermute | solution.py:154
  14.7 5.3 %collective-permute-done = f32[8,16,768]{2,1,0:T(8,128)S(1)} collective-permute-done((f32[8,16,768]{2,1,0:T(8,128)}, f32[8,16,768]{2,1,0:T(8,128)S(1)}, u32[]{:S(2)}, u32[]{:S(2)}) %collective-permute-start) | collective-permute-done | bytes 393248 | tf_op jit(solution)/shard_map/ppermute | solution.py:154
  20.0 11.9 %collective-permute-done.1 = f32[8,16,768]{2,1,0:T(8,128)S(1)} collective-permute-done((f32[8,16,768]{2,1,0:T(8,128)}, f32[8,16,768]{2,1,0:T(8,128)S(1)}, u32[]{:S(2)}, u32[]{:S(2)}) %collective-permute-start.1) | collective-permute-done | bytes 393248 | tf_op jit(solution)/shard_map/ppermute | solution.py:154
  31.9 2.0 collective-permute-done.2
  34.0 1.8 add_add_fusion.1
  35.8 8.2 %all-to-all-start = ((f32[8,16,768]{2,1,0:T(8,128)}), f32[8,16,768]{2,1,0:T(8,128)S(1)}, u32[]{:S(2)}, u32[]{:S(2)}) async-start(f32[8,16,768]{2,1,0:T(8,128)} %add_add_fusion.1), calls=%async_computation | async-start | bytes 786432 | tf_op jit(solution)/shard_map/all_to_all | solution.py:174
  44.0 9.4 %term.3 = (f32[8,16,768]{2,1,0:T(8,128)}, f32[8,16,768]{2,1,0:T(8,128)}, f32[8,16,768]{2,1,0:T(8,128)}, f32[8,16,768]{2,1,0:T(8,128)}) custom-call(s32[1]{0:T(128)} %bitcast.1.y_ref, f32[4,512,512]{2,1,0:T(8,128)} %bitcast.78, f32[4,512,1536]{2,1,0:T(8,128)} %bitcast.75, f32[4,512,1536]{2,1,0:T(8,128)} %bitcast.76), custom_call_target="tpu_custom_call" | custom-call | flops 4831838208 | bytes 12582912 | tf_op jit(solution)/shard_map/term/pallas_call | solution.py:50
  53.4 1.2 collective-permute-start.8
  54.6 2.6 %collective-permute-start.9 = (f32[8,16,768]{2,1,0:T(8,128)}, f32[8,16,768]{2,1,0:T(8,128)S(1)}, u32[]{:S(2)}, u32[]{:S(2)}) collective-permute-start(f32[8,16,768]{2,1,0:T(8,128)} %get-tuple-element.33), channel_id=1, source_target_pairs={{0,24},{8,16},{16,8},{24,0},{1,25},{9,17},{17,9},{25,1},{2,26},{10... | collective-permute-start | bytes 1179656 | tf_op jit(solution)/shard_map/ppermute | solution.py:154
  57.3 3.4 %collective-permute-start.3 = (f32[16,640]{1,0:T(8,128)S(1)}, f32[16,640]{1,0:T(8,128)S(1)}, u32[]{:S(2)}, u32[]{:S(2)}) collective-permute-start(f32[16,640]{1,0:T(8,128)S(1)} %pad_maximum_fusion.3), channel_id=1, source_target_pairs={{0,1},{1,0},{2,3},{3,2},{4,5},{5,4},{6,7},{7,6},{8,9},{9,8},{10,11... | collective-permute-start | bytes 122888 | tf_op jit(solution)/shard_map/ppermute | solution.py:154
  60.7 1.0 collective-permute-done.7
  61.7 8.3 %collective-permute-done.8 = f32[8,16,768]{2,1,0:T(8,128)S(1)} collective-permute-done((f32[8,16,768]{2,1,0:T(8,128)}, f32[8,16,768]{2,1,0:T(8,128)S(1)}, u32[]{:S(2)}, u32[]{:S(2)}) %collective-permute-start.8) | collective-permute-done | bytes 393248 | tf_op jit(solution)/shard_map/ppermute | solution.py:154
  70.0 1.8 add_add_fusion
  71.9 6.4 %all-to-all-start.1 = ((f32[8,16,768]{2,1,0:T(8,128)}), f32[8,16,768]{2,1,0:T(8,128)S(1)}, u32[]{:S(2)}, u32[]{:S(2)}) async-start(f32[8,16,768]{2,1,0:T(8,128)} %add_add_fusion), calls=%async_computation.1 | async-start | bytes 786432 | tf_op jit(solution)/shard_map/all_to_all | solution.py:174
  79.6 1.3 collective-permute-start.4
  81.0 6.5 %collective-permute-done.4 = f32[16,1024]{1,0:T(8,128)S(1)} collective-permute-done((f32[16,1024]{1,0:T(8,128)S(1)}, f32[16,1024]{1,0:T(8,128)S(1)}, u32[]{:S(2)}, u32[]{:S(2)}) %collective-permute-start.4) | collective-permute-done | bytes 65568 | tf_op jit(solution)/shard_map/ppermute | solution.py:178
  87.5 1.6 all-to-all-done.1
  89.1 17.3 %all_to_all.20.refs_0_ = f32[8,16,1024]{2,1,0:T(8,128)S(1)} all-to-all(f32[8,16,1024]{2,1,0:T(8,128)S(1)} %broadcast_in_dim.9), channel_id=1, replica_groups=mesh['z'=8,'y'=4,'x'=4,'core'=2] {'z'}, dimensions={0} | all-to-all | bytes 1048576 | tf_op jit(solution)/shard_map/all_to_all | solution.py:183
  106.5 9.1 %collective-permute-start.10 = (f32[16,384]{1,0:T(8,128)S(1)}, f32[16,384]{1,0:T(8,128)S(1)}, u32[]{:S(2)}, u32[]{:S(2)}) collective-permute-start(f32[16,384]{1,0:T(8,128)S(1)} %broadcast_select_fusion.3), channel_id=1, source_target_pairs={{0,1},{1,0},{2,3},{3,2},{4,5},{5,4},{6,7},{7,6},{8,9},{9,8},{10,11... | collective-permute-start | bytes 73736 | tf_op jit(solution)/shard_map/ppermute | solution.py:154
  117.7 1.3 collective-permute-start.11
  119.1 4.7 %collective-permute-done.11 = f32[16,768]{1,0:T(8,128)S(1)} collective-permute-done((f32[16,768]{1,0:T(8,128)S(1)}, f32[16,768]{1,0:T(8,128)S(1)}, u32[]{:S(2)}, u32[]{:S(2)}) %collective-permute-start.11) | collective-permute-done | bytes 49184 | tf_op jit(solution)/shard_map/ppermute | solution.py:178
  124.6 3.5 %all-to-all-start.3 = ((f32[8,16,768]{2,1,0:T(8,128)}), f32[8,16,768]{2,1,0:T(8,128)S(1)}, u32[]{:S(2)}, u32[]{:S(2)}) async-start(f32[8,16,768]{2,1,0:T(8,128)} %broadcast_in_dim.10), calls=%async_computation.3 | async-start | bytes 786432 | tf_op jit(solution)/shard_map/all_to_all | solution.py:183
  128.0 2.7 %collective-permute-start.16 = (f32[8,16,1024]{2,1,0:T(8,128)S(1)}, f32[8,16,1024]{2,1,0:T(8,128)S(1)}, u32[]{:S(2)}, u32[]{:S(2)}) collective-permute-start(f32[8,16,1024]{2,1,0:T(8,128)S(1)} %all_to_all.20.refs_0_), channel_id=1, source_target_pairs={{0,24},{8,16},{16,8},{24,0},{1,25},{9,17},{17,9},{25,1},{2,26},{10... | collective-permute-start | bytes 1572872 | tf_op jit(solution)/shard_map/ppermute | solution.py:154
  131.4 9.2 %all-to-all-done.3.refs_0_ = f32[8,16,768]{2,1,0:T(8,128)S(1)} async-done(((f32[8,16,768]{2,1,0:T(8,128)}), f32[8,16,768]{2,1,0:T(8,128)S(1)}, u32[]{:S(2)}, u32[]{:S(2)}) %all-to-all-start.3) | async-done | bytes 393248 | tf_op jit(solution)/shard_map/all_to_all | solution.py:183
  140.7 2.6 %collective-permute-start.18 = (f32[8,16,768]{2,1,0:T(8,128)S(1)}, f32[8,16,768]{2,1,0:T(8,128)S(1)}, u32[]{:S(2)}, u32[]{:S(2)}) collective-permute-start(f32[8,16,768]{2,1,0:T(8,128)S(1)} %all-to-all-done.3.refs_0_), channel_id=1, source_target_pairs={{0,24},{8,0},{16,8},{24,16},{1,25},{9,1},{17,9},{25,17},{2,26},{10... | collective-permute-start | bytes 1179656 | tf_op jit(solution)/shard_map/ppermute | solution.py:159
  143.3 9.9 %collective-permute-done.16.refs_3_ = f32[8,16,1024]{2,1,0:T(8,128)S(1)} collective-permute-done((f32[8,16,1024]{2,1,0:T(8,128)S(1)}, f32[8,16,1024]{2,1,0:T(8,128)S(1)}, u32[]{:S(2)}, u32[]{:S(2)}) %collective-permute-start.16) | collective-permute-done | bytes 524320 | tf_op jit(solution)/shard_map/ppermute | solution.py:154
  154.1 7.5 %collective-permute-done.18.refs_2_ = f32[8,16,768]{2,1,0:T(8,128)S(1)} collective-permute-done((f32[8,16,768]{2,1,0:T(8,128)S(1)}, f32[8,16,768]{2,1,0:T(8,128)S(1)}, u32[]{:S(2)}, u32[]{:S(2)}) %collective-permute-start.18) | collective-permute-done | bytes 393248 | tf_op jit(solution)/shard_map/ppermute | solution.py:159
  163.1 2.4 %collective-permute-start.19 = (f32[32,16,256]{2,1,0:T(8,128)S(1)}, f32[32,16,256]{2,1,0:T(8,128)S(1)}, u32[]{:S(2)}, u32[]{:S(2)}) collective-permute-start(f32[32,16,256]{2,1,0:T(8,128)S(1)} %pad_maximum_fusion.refs_4_), channel_id=1, source_target_pairs={{0,1},{1,0},{2,3},{3,2},{4,5},{5,4},{6,7},{7,6},{8,9},{9,8},{10,11... | collective-permute-start | bytes 1572872 | tf_op jit(solution)/shard_map/ppermute | solution.py:154
  165.6 1.4 collective-permute-done.19.refs_5_
  167.9 1.0 copy-done.10
  168.9 1.0 copy-done.12
  169.9 1.0 copy-done.14
  171.0 1.6 copy-done.15
  172.6 1.0 copy-done.18
  173.6 3.4 %solve.2 = (f32[2,512,384]{2,1,0:T(8,128)S(1)}, f32[512,512]{1,0:T(8,128)S(1)}) custom-call(s32[32]{0:T(128)S(1)} %stack.230.index_ref, s32[1]{0:T(128)} %bitcast.core_ref, f32[2,512,512]{2,1,0:T(8,128)S(1)} %copy-done.15, f32[8,16,1024]{2,1,0:T(8,128)S(1)} %all_to_all.20.refs_0_, f32[8,16,1024]{2,1,0:T(8,128)S(1)} %copy-done.14, ...), custom_call_target="tpu_custom_call" | custom-call | flops 1811939328 | bytes 6291456 | tf_op jit(solution)/shard_map/solve/pallas_call | solution.py:104
  179.1 1.9 collective-permute-start.21
  181.9 3.8 %collective-permute-done.21.refs_4_ = f32[4,16,768]{2,1,0:T(8,128)S(1)} collective-permute-done((f32[4,16,768]{2,1,0:T(8,128)}, f32[4,16,768]{2,1,0:T(8,128)S(1)}, u32[]{:S(2)}, u32[]{:S(2)}) %collective-permute-start.21) | collective-permute-done | bytes 196640 | tf_op jit(solution)/shard_map/ppermute | solution.py:159
  185.7 3.6 %collective-permute-done.20.refs_3_ = f32[4,16,768]{2,1,0:T(8,128)} collective-permute-done((f32[4,16,768]{2,1,0:T(8,128)}, f32[4,16,768]{2,1,0:T(8,128)}, u32[]{:S(2)}, u32[]{:S(2)}) %collective-permute-start.20) | collective-permute-done | bytes 196640 | tf_op jit(solution)/shard_map/ppermute | solution.py:159
  189.4 1.0 copy-done.1
  190.4 1.0 copy-done.5
  192.4 1.6 copy-done.16
  193.9 1.2 copy-done.20
  195.2 3.8 %solve.3.own2 = f32[2,512,384]{2,1,0:T(8,128)S(1)} custom-call(s32[32]{0:T(128)S(1)} %stack.263.index_ref, s32[1]{0:T(128)} %bitcast.core_ref, f32[2,512,512]{2,1,0:T(8,128)S(1)} %copy-done.16, f32[8,16,768]{2,1,0:T(8,128)S(1)} %copy-done.1, f32[8,16,768]{2,1,0:T(8,128)S(1)} %copy-done.8, f32[8,16,768]{2,1,0:T(8,128)S(1)} %copy-done.5, ...), custom_call_target="tpu_custom_call" | custom-call | flops 1811939328 | bytes 6291456 | tf_op jit(solution)/shard_map/solve/pallas_call | solution.py:104
  199.0 1.4 collective-permute-start.23
  200.4 3.0 %collective-permute-done.23.other2 = f32[2,512,384]{2,1,0:T(8,128)S(1)} collective-permute-done((f32[2,512,384]{2,1,0:T(8,128)S(1)}, f32[2,512,384]{2,1,0:T(8,128)S(1)}, u32[]{:S(2)}, u32[]{:S(2)}) %collective-permute-start.23) | collective-permute-done | bytes 1572896 | tf_op jit(solution)/shard_map/ppermute | solution.py:154
  203.4 4.2 %finish.1 = (f32[2,512,1536]{2,1,0:T(8,128)}, f32[16,1536]{1,0:T(8,128)}) custom-call(s32[1]{0:T(128)} %bitcast.core_ref, f32[2,512,384]{2,1,0:T(8,128)S(1)} %get-tuple-element.43.own1, f32[2,512,384]{2,1,0:T(8,128)S(1)} %solve.3.own2, f32[2,512,384]{2,1,0:T(8,128)S(1)} %collective-permute-done.22.other1, f32[2,512,384]{2,1,0:T(8,128)S(1)} %collective-permute-done.23.other2, ...), custom_call_target="tpu_custom_call" | custom-call | tf_op jit(solution)/shard_map/finish/pallas_call | solution.py:139
  (84 shorter events, 12.4 us)
Async XLA Ops:
  10.0 10.0 %collective-permute-start = (f32[8,16,768]{2,1,0:T(8,128)}, f32[8,16,768]{2,1,0:T(8,128)S(1)}, u32[]{:S(2)}, u32[]{:S(2)}) collective-permute-start(f32[8,16,768]{2,1,0:T(8,128)} %get-tuple-element.26), channel_id=1, source_target_pairs={{0,8},{8,0},{16,24},{24,16},{1,9},{9,1},{17,25},{25,17},{2,10},{10... | collective-permute-start | bytes 1179656 | tf_op jit(solution)/shard_map/ppermute | solution.py:154
  12.1 19.8 %collective-permute-start.1 = (f32[8,16,768]{2,1,0:T(8,128)}, f32[8,16,768]{2,1,0:T(8,128)S(1)}, u32[]{:S(2)}, u32[]{:S(2)}) collective-permute-start(f32[8,16,768]{2,1,0:T(8,128)} %get-tuple-element.27), channel_id=1, source_target_pairs={{0,16},{8,24},{16,0},{24,8},{1,17},{9,25},{17,1},{25,9},{2,18},{10... | collective-permute-start | bytes 1179656 | tf_op jit(solution)/shard_map/ppermute | solution.py:154
  14.7 19.2 %collective-permute-start.2 = (f32[8,16,768]{2,1,0:T(8,128)}, f32[8,16,768]{2,1,0:T(8,128)S(1)}, u32[]{:S(2)}, u32[]{:S(2)}) collective-permute-start(f32[8,16,768]{2,1,0:T(8,128)} %get-tuple-element.28), channel_id=1, source_target_pairs={{0,24},{8,16},{16,8},{24,0},{1,25},{9,17},{17,9},{25,1},{2,26},{10... | collective-permute-start | bytes 1179656 | tf_op jit(solution)/shard_map/ppermute | solution.py:154
  35.8 21.5 %all-to-all-start = ((f32[8,16,768]{2,1,0:T(8,128)}), f32[8,16,768]{2,1,0:T(8,128)S(1)}, u32[]{:S(2)}, u32[]{:S(2)}) async-start(f32[8,16,768]{2,1,0:T(8,128)} %add_add_fusion.1), calls=%async_computation | async-start | bytes 786432 | tf_op jit(solution)/shard_map/all_to_all | solution.py:174
  44.0 13.3 %copy-start.2 = (f32[1,1,2,16,512]{4,3,2,1,0:T(8,128)S(1)}, f32[1,1,2,16,512]{4,3,2,1,0:T(8,128)}, u32[]{:S(2)}) copy-start(f32[1,1,2,16,512]{4,3,2,1,0:T(8,128)} %param.8) | copy-start | bytes 196612
  44.0 13.3 %copy-start.21 = (f32[1,1,16,1536]{3,2,1,0:T(8,128)S(1)}, f32[1,1,16,1536]{3,2,1,0:T(8,128)}, u32[]{:S(2)}) copy-start(f32[1,1,16,1536]{3,2,1,0:T(8,128)} %param.7) | copy-start | bytes 294916
  53.4 8.4 %collective-permute-start.7 = (f32[8,16,768]{2,1,0:T(8,128)}, f32[8,16,768]{2,1,0:T(8,128)S(1)}, u32[]{:S(2)}, u32[]{:S(2)}) collective-permute-start(f32[8,16,768]{2,1,0:T(8,128)} %get-tuple-element.31), channel_id=1, source_target_pairs={{0,8},{8,0},{16,24},{24,16},{1,9},{9,1},{17,25},{25,17},{2,10},{10... | collective-permute-start | bytes 1179656 | tf_op jit(solution)/shard_map/ppermute | solution.py:154
  53.4 16.7 %collective-permute-start.8 = (f32[8,16,768]{2,1,0:T(8,128)}, f32[8,16,768]{2,1,0:T(8,128)S(1)}, u32[]{:S(2)}, u32[]{:S(2)}) collective-permute-start(f32[8,16,768]{2,1,0:T(8,128)} %get-tuple-element.32), channel_id=1, source_target_pairs={{0,16},{8,24},{16,0},{24,8},{1,17},{9,25},{17,1},{25,9},{2,18},{10... | collective-permute-start | bytes 1179656 | tf_op jit(solution)/shard_map/ppermute | solution.py:154
  54.6 15.4 %collective-permute-start.9 = (f32[8,16,768]{2,1,0:T(8,128)}, f32[8,16,768]{2,1,0:T(8,128)S(1)}, u32[]{:S(2)}, u32[]{:S(2)}) collective-permute-start(f32[8,16,768]{2,1,0:T(8,128)} %get-tuple-element.33), channel_id=1, source_target_pairs={{0,24},{8,16},{16,8},{24,0},{1,25},{9,17},{17,9},{25,1},{2,26},{10... | collective-permute-start | bytes 1179656 | tf_op jit(solution)/shard_map/ppermute | solution.py:154
  57.3 14.5 %collective-permute-start.3 = (f32[16,640]{1,0:T(8,128)S(1)}, f32[16,640]{1,0:T(8,128)S(1)}, u32[]{:S(2)}, u32[]{:S(2)}) collective-permute-start(f32[16,640]{1,0:T(8,128)S(1)} %pad_maximum_fusion.3), channel_id=1, source_target_pairs={{0,1},{1,0},{2,3},{3,2},{4,5},{5,4},{6,7},{7,6},{8,9},{9,8},{10,11... | collective-permute-start | bytes 122888 | tf_op jit(solution)/shard_map/ppermute | solution.py:154
  71.9 17.1 %all-to-all-start.1 = ((f32[8,16,768]{2,1,0:T(8,128)}), f32[8,16,768]{2,1,0:T(8,128)S(1)}, u32[]{:S(2)}, u32[]{:S(2)}) async-start(f32[8,16,768]{2,1,0:T(8,128)} %add_add_fusion), calls=%async_computation.1 | async-start | bytes 786432 | tf_op jit(solution)/shard_map/all_to_all | solution.py:174
  78.3 2.6 %collective-permute-start.6 = (f32[16,1024]{1,0:T(8,128)S(1)}, f32[16,1024]{1,0:T(8,128)S(1)}, u32[]{:S(2)}, u32[]{:S(2)}) collective-permute-start(f32[16,1024]{1,0:T(8,128)S(1)} %pad_maximum_fusion.1), channel_id=1, source_target_pairs={{6,4},{7,5},{14,12},{15,13},{22,20},{23,21},{30,28},{31,29},{38,36... | collective-permute-start | bytes 196616 | tf_op jit(solution)/shard_map/ppermute | solution.py:178
  79.0 2.0 collective-permute-start.5
  79.6 7.8 %collective-permute-start.4 = (f32[16,1024]{1,0:T(8,128)S(1)}, f32[16,1024]{1,0:T(8,128)S(1)}, u32[]{:S(2)}, u32[]{:S(2)}) collective-permute-start(f32[16,1024]{1,0:T(8,128)S(1)} %pad_maximum_fusion.1), channel_id=1, source_target_pairs={{6,0},{7,1},{14,8},{15,9},{22,16},{23,17},{30,24},{31,25},{38,32},... | collective-permute-start | bytes 196616 | tf_op jit(solution)/shard_map/ppermute | solution.py:178
  106.5 9.9 %collective-permute-start.10 = (f32[16,384]{1,0:T(8,128)S(1)}, f32[16,384]{1,0:T(8,128)S(1)}, u32[]{:S(2)}, u32[]{:S(2)}) collective-permute-start(f32[16,384]{1,0:T(8,128)S(1)} %broadcast_select_fusion.3), channel_id=1, source_target_pairs={{0,1},{1,0},{2,3},{3,2},{4,5},{5,4},{6,7},{7,6},{8,9},{9,8},{10,11... | collective-permute-start | bytes 73736 | tf_op jit(solution)/shard_map/ppermute | solution.py:154
  116.4 2.6 %collective-permute-start.13 = (f32[16,768]{1,0:T(8,128)S(1)}, f32[16,768]{1,0:T(8,128)S(1)}, u32[]{:S(2)}, u32[]{:S(2)}) collective-permute-start(f32[16,768]{1,0:T(8,128)S(1)} %pad_maximum_fusion.2), channel_id=1, source_target_pairs={{6,4},{7,5},{14,12},{15,13},{22,20},{23,21},{30,28},{31,29},{38,36... | collective-permute-start | bytes 147464 | tf_op jit(solution)/shard_map/ppermute | solution.py:178
  117.1 2.0 collective-permute-start.12
  117.7 6.0 %collective-permute-start.11 = (f32[16,768]{1,0:T(8,128)S(1)}, f32[16,768]{1,0:T(8,128)S(1)}, u32[]{:S(2)}, u32[]{:S(2)}) collective-permute-start(f32[16,768]{1,0:T(8,128)S(1)} %pad_maximum_fusion.2), channel_id=1, source_target_pairs={{6,0},{7,1},{14,8},{15,9},{22,16},{23,17},{30,24},{31,25},{38,32},... | collective-permute-start | bytes 147464 | tf_op jit(solution)/shard_map/ppermute | solution.py:178
  124.6 16.1 %all-to-all-start.3 = ((f32[8,16,768]{2,1,0:T(8,128)}), f32[8,16,768]{2,1,0:T(8,128)S(1)}, u32[]{:S(2)}, u32[]{:S(2)}) async-start(f32[8,16,768]{2,1,0:T(8,128)} %broadcast_in_dim.10), calls=%async_computation.3 | async-start | bytes 786432 | tf_op jit(solution)/shard_map/all_to_all | solution.py:183
  128.0 25.1 %collective-permute-start.16 = (f32[8,16,1024]{2,1,0:T(8,128)S(1)}, f32[8,16,1024]{2,1,0:T(8,128)S(1)}, u32[]{:S(2)}, u32[]{:S(2)}) collective-permute-start(f32[8,16,1024]{2,1,0:T(8,128)S(1)} %all_to_all.20.refs_0_), channel_id=1, source_target_pairs={{0,24},{8,16},{16,8},{24,0},{1,25},{9,17},{17,9},{25,1},{2,26},{10... | collective-permute-start | bytes 1572872 | tf_op jit(solution)/shard_map/ppermute | solution.py:154
  130.7 23.2 %collective-permute-start.15 = (f32[8,16,1024]{2,1,0:T(8,128)S(1)}, f32[8,16,1024]{2,1,0:T(8,128)S(1)}, u32[]{:S(2)}, u32[]{:S(2)}) collective-permute-start(f32[8,16,1024]{2,1,0:T(8,128)S(1)} %all_to_all.20.refs_0_), channel_id=1, source_target_pairs={{0,16},{8,24},{16,0},{24,8},{1,17},{9,25},{17,1},{25,9},{2,18},{10... | collective-permute-start | bytes 1572872 | tf_op jit(solution)/shard_map/ppermute | solution.py:154
  130.7 23.2 %collective-permute-start.14 = (f32[8,16,1024]{2,1,0:T(8,128)S(1)}, f32[8,16,1024]{2,1,0:T(8,128)S(1)}, u32[]{:S(2)}, u32[]{:S(2)}) collective-permute-start(f32[8,16,1024]{2,1,0:T(8,128)S(1)} %all_to_all.20.refs_0_), channel_id=1, source_target_pairs={{0,8},{8,0},{16,24},{24,16},{1,9},{9,1},{17,25},{25,17},{2,10},{10... | collective-permute-start | bytes 1572872 | tf_op jit(solution)/shard_map/ppermute | solution.py:154
  140.7 36.4 %copy-start = (f32[8,16,768]{2,1,0:T(8,128)}, f32[8,16,768]{2,1,0:T(8,128)S(1)}, u32[]{:S(2)}) copy-start(f32[8,16,768]{2,1,0:T(8,128)S(1)} %all-to-all-done.3.refs_0_) | copy-start | bytes 1179652
  140.7 20.9 %collective-permute-start.18 = (f32[8,16,768]{2,1,0:T(8,128)S(1)}, f32[8,16,768]{2,1,0:T(8,128)S(1)}, u32[]{:S(2)}, u32[]{:S(2)}) collective-permute-start(f32[8,16,768]{2,1,0:T(8,128)S(1)} %all-to-all-done.3.refs_0_), channel_id=1, source_target_pairs={{0,24},{8,0},{16,8},{24,16},{1,25},{9,1},{17,9},{25,17},{2,26},{10... | collective-permute-start | bytes 1179656 | tf_op jit(solution)/shard_map/ppermute | solution.py:159
  143.3 18.3 %collective-permute-start.17 = (f32[8,16,768]{2,1,0:T(8,128)S(1)}, f32[8,16,768]{2,1,0:T(8,128)S(1)}, u32[]{:S(2)}, u32[]{:S(2)}) collective-permute-start(f32[8,16,768]{2,1,0:T(8,128)S(1)} %all-to-all-done.3.refs_0_), channel_id=1, source_target_pairs={{0,8},{8,16},{16,24},{24,0},{1,9},{9,17},{17,25},{25,1},{2,10},{10... | collective-permute-start | bytes 1179656 | tf_op jit(solution)/shard_map/ppermute | solution.py:159
  153.2 0.8 copy-start.9
  154.0 13.1 %copy-start.11 = (f32[8,16,1024]{2,1,0:T(8,128)}, f32[8,16,1024]{2,1,0:T(8,128)S(1)}, u32[]{:S(2)}) copy-start(f32[8,16,1024]{2,1,0:T(8,128)S(1)} %collective-permute-done.15.refs_2_) | copy-start | bytes 1572868
  154.0 13.1 %copy-start.13 = (f32[8,16,1024]{2,1,0:T(8,128)}, f32[8,16,1024]{2,1,0:T(8,128)S(1)}, u32[]{:S(2)}) copy-start(f32[8,16,1024]{2,1,0:T(8,128)S(1)} %collective-permute-done.14.refs_1_) | copy-start | bytes 1572868
  162.3 0.8 copy-start.6
  163.1 3.9 %collective-permute-start.19 = (f32[32,16,256]{2,1,0:T(8,128)S(1)}, f32[32,16,256]{2,1,0:T(8,128)S(1)}, u32[]{:S(2)}, u32[]{:S(2)}) collective-permute-start(f32[32,16,256]{2,1,0:T(8,128)S(1)} %pad_maximum_fusion.refs_4_), channel_id=1, source_target_pairs={{0,1},{1,0},{2,3},{3,2},{4,5},{5,4},{6,7},{7,6},{8,9},{9,8},{10,11... | collective-permute-start | bytes 1572872 | tf_op jit(solution)/shard_map/ppermute | solution.py:154
  167.0 0.8 copy-start.17
  167.9 1.0 copy-start.10
  168.9 1.0 copy-start.12
  169.9 1.0 copy-start.14
  171.0 1.6 copy-start.15
  172.6 1.0 copy-start.18
  173.6 4.8 %copy-start.4 = (f32[8,16,768]{2,1,0:T(8,128)S(1)}, f32[8,16,768]{2,1,0:T(8,128)}, u32[]{:S(2)}) copy-start(f32[8,16,768]{2,1,0:T(8,128)} %copy-done.3) | copy-start | bytes 1179652
  173.6 7.5 %copy-start.7 = (f32[8,16,768]{2,1,0:T(8,128)S(1)}, f32[8,16,768]{2,1,0:T(8,128)}, u32[]{:S(2)}) copy-start(f32[8,16,768]{2,1,0:T(8,128)} %copy-done.6) | copy-start | bytes 1179652
  177.1 1.0 copy-start.19
  178.0 3.9 %collective-permute-start.22 = (f32[2,512,384]{2,1,0:T(8,128)S(1)}, f32[2,512,384]{2,1,0:T(8,128)S(1)}, u32[]{:S(2)}, u32[]{:S(2)}) collective-permute-start(f32[2,512,384]{2,1,0:T(8,128)S(1)} %get-tuple-element.43.own1), channel_id=1, source_target_pairs={{0,1},{1,0},{2,3},{3,2},{4,5},{5,4},{6,7},{7,6},{8,9},{9,8},{10,11... | collective-permute-start | bytes 4718600 | tf_op jit(solution)/shard_map/ppermute | solution.py:154
  179.1 6.6 %collective-permute-start.21 = (f32[4,16,768]{2,1,0:T(8,128)}, f32[4,16,768]{2,1,0:T(8,128)S(1)}, u32[]{:S(2)}, u32[]{:S(2)}) collective-permute-start(f32[4,16,768]{2,1,0:T(8,128)} %slice.91), channel_id=1, source_target_pairs={{0,24},{8,0},{16,8},{24,16},{1,25},{9,1},{17,9},{25,17},{2,26},{10... | collective-permute-start | bytes 589832 | tf_op jit(solution)/shard_map/ppermute | solution.py:159
  181.8 7.6 %collective-permute-start.20 = (f32[4,16,768]{2,1,0:T(8,128)}, f32[4,16,768]{2,1,0:T(8,128)}, u32[]{:S(2)}, u32[]{:S(2)}) collective-permute-start(f32[4,16,768]{2,1,0:T(8,128)} %slice.90), channel_id=1, source_target_pairs={{0,8},{8,16},{16,24},{24,0},{1,9},{9,17},{17,25},{25,1},{2,10},{10... | collective-permute-start | bytes 589832 | tf_op jit(solution)/shard_map/ppermute | solution.py:159
  189.4 1.0 copy-start.1
  190.4 1.0 copy-start.5
  191.4 1.0 copy-start.8
  192.4 1.6 copy-start.16
  193.9 1.2 copy-start.20
  199.0 4.4 %collective-permute-start.23 = (f32[2,512,384]{2,1,0:T(8,128)S(1)}, f32[2,512,384]{2,1,0:T(8,128)S(1)}, u32[]{:S(2)}, u32[]{:S(2)}) collective-permute-start(f32[2,512,384]{2,1,0:T(8,128)S(1)} %solve.3.own2), channel_id=1, source_target_pairs={{0,1},{1,0},{2,3},{3,2},{4,5},{5,4},{6,7},{7,6},{8,9},{9,8},{10,11... | collective-permute-start | bytes 4718600 | tf_op jit(solution)/shard_map/ppermute | solution.py:154
  (1 other events, 0.7 us)

commit v2 on v1

v2 whole, which is shorter than its diff:
```python
import functools

import jax
import jax.numpy as jnp
from jax import lax
from jax.experimental import pallas as pl
from jax.experimental.pallas import tpu as pltpu
from jax.sharding import Mesh
from jax.sharding import PartitionSpec as P

NZ, NY, NX, NCORE = 8, 4, 4, 2
SLAB = 16
HALF = 768
PART = 384
BITREV = (0, 4, 2, 6, 1, 5, 3, 7)
SHIFTS = (0, 1)
CUT = 512
BOUNDS = ((0, CUT), (CUT, HALF))


def split(x):
    high = x.astype(jnp.bfloat16)
    return high, (x - high.astype(jnp.float32)).astype(jnp.bfloat16)


def dot3(a, b):
    ah, al = split(a)
    bh, bl = split(b)
    mul = functools.partial(jnp.dot, preferred_element_type=jnp.float32)
    return mul(ah, bh) + (mul(ah, bl) + mul(al, bh))


def term_kernel(shift, z_ref, y_ref, c_ref, ea_ref, eb_ref, *refs):
    outs, acc = refs[:NY], refs[NY]
    k = pl.program_id(0)
    product = dot3(c_ref[0], jnp.concatenate([ea_ref[0], eb_ref[0]], axis=1))

    @pl.when(k == 0)
    def _():
        acc[...] = product

    @pl.when(k > 0)
    def _():
        acc[...] += product

    @pl.when(k == pl.num_programs(0) - 1)
    def _():
        label = (z_ref[0] + shift) % NZ
        for n, kz in enumerate(BITREV):
            z = ((label ^ kz) + NZ - shift) % NZ
            for ky, o_ref in enumerate(outs):
                row = pl.multiple_of((z * NY + (y_ref[0] ^ ky)) * SLAB, SLAB)
                o_ref[n] = acc[pl.ds(row, SLAB), :]


def term(z, y, coupling, earlier, chunk):
    out = pl.BlockSpec((NZ, SLAB, HALF), lambda k, z, y: (0, 0, 0))
    return pl.pallas_call(
        functools.partial(term_kernel, SHIFTS[chunk]),
        grid_spec=pltpu.PrefetchScalarGridSpec(
            num_scalar_prefetch=2,
            grid=(4,),
            in_specs=[
                pl.BlockSpec((1, 512, 512), lambda k, z, y: (k, 0, 0)),
                pl.BlockSpec((1, 512, PART), lambda k, z, y: (k, 0, chunk)),
                pl.BlockSpec((1, 512, PART), lambda k, z, y: (k, 0, 2 + chunk)),
            ],
            out_specs=(out,) * NY,
            scratch_shapes=[pltpu.VMEM((512, HALF), jnp.float32)],
        ),
        out_shape=(jax.ShapeDtypeStruct((NZ, SLAB, HALF), jnp.float32),) * NY,
        compiler_params=pltpu.CompilerParams(vmem_limit_bytes=56 * 2**20),
        cost_estimate=pl.CostEstimate(
            flops=6 * 512 * 2048 * HALF, bytes_accessed=12 * 2**20, transcendentals=0
        ),
        name="term",
    )(z, y, coupling, earlier, earlier)


def copy_in(source, target, sem):
    copy = pltpu.make_async_copy(source, target, sem)
    copy.start()
    return copy


def solve_kernel(n, y_ref, core_ref, inv_hbm, other_hbm, *refs):
    pieces, links, (o_ref, b, inv, link, sems) = refs[: -NY - 5], refs[-NY - 5 : -5], refs[-5:]
    y, core = y_ref[0], core_ref[0]
    begun = [0]

    def begin(source, target):
        begun[0] += 1
        return copy_in(source, target, sems.at[begun[0] - 1])

    def block(k):
        at = pl.ds(k * n, n)
        copies = [begin(inv_hbm.at[k], inv.at[k])]
        for ky in range(NY):
            source = pieces[ky].at[:, :, at] if len(pieces) > 1 else pieces[0].at[:, ky, :, at]
            copies.append(begin(source, b.at[k, :, y ^ ky]))
        return copies

    here = pl.ds(pl.multiple_of(core * 256, 128), 256)
    there = pl.ds(pl.multiple_of((1 - core) * 256, 128), 256)
    copies0, copies1 = block(0), block(1)
    for ky, p in enumerate(links):
        copies1.append(begin(p.at[:, :, pl.ds(p.shape[2] - 256, 256)], link.at[:, y ^ ky, :, here]))
        copies1.append(begin(other_hbm.at[ky], link.at[:, y ^ ky, :, there]))
    for copy in copies0:
        copy.wait()
    first = dot3(inv[0], b[0].reshape(512, n))
    o_ref[0] = first
    for copy in copies1:
        copy.wait()
    middle = b[1].reshape(512, n) - dot3(link[...].reshape(512, 512), first)
    o_ref[1] = dot3(inv[1], middle)


def solve(n, y, core, inverses, other, pieces, links):
    scalar, anywhere = pl.BlockSpec(memory_space=pltpu.SMEM), pl.BlockSpec(memory_space=pl.ANY)
    return pl.pallas_call(
        functools.partial(solve_kernel, n),
        in_specs=[scalar] * 2 + [anywhere] * (2 + len(pieces) + NY),
        out_specs=pl.BlockSpec(memory_space=pltpu.VMEM),
        scratch_shapes=[
            pltpu.VMEM((2, NZ, NY, SLAB, n), jnp.float32),
            pltpu.VMEM((2, 512, 512), jnp.float32),
            pltpu.VMEM((NZ, NY, SLAB, 512), jnp.float32),
            pltpu.SemaphoreType.DMA((2 + 4 * NY,)),
        ],
        out_shape=jax.ShapeDtypeStruct((2, 512, n), jnp.float32),
        compiler_params=pltpu.CompilerParams(vmem_limit_bytes=56 * 2**20),
        cost_estimate=pl.CostEstimate(
            flops=18 * 512 * 512 * n, bytes_accessed=6 * 2**20, transcendentals=0
        ),
        name="solve",
    )(y, core, inverses, other, *pieces, *links)


def columns(part, half):
    return slice(half * HALF + BOUNDS[part][0], half * HALF + BOUNDS[part][1])


def finish_kernel(chunk, core_ref, own, other, base, panel, *refs):
    solved, pending, sems = refs[-3:]
    core = core_ref[0]
    first, last = BOUNDS[chunk]
    places = ((own, core * HALF + first), (other, (1 - core) * HALF + first))
    places = [(ref, pl.ds(pl.multiple_of(at, 128), last - first)) for ref, at in places]
    copies = [copy_in(ref, solved.at[:, :, at], sems.at[i]) for i, (ref, at) in enumerate(places)]
    for half in (0, 1):
        pending[:, columns(chunk, half)] = base[:, columns(chunk, half)]
    for ref, at in places:
        update = dot3(panel[0], ref[0]) + dot3(panel[1], ref[1])
        pending[:, at] = pending[:, at] - update
    if len(refs) > 3:
        for half in (0, 1):
            pending[:, columns(1 - chunk, half)] = refs[1][:, columns(1 - chunk, half)]
    for copy in copies:
        copy.wait()


def finish(chunk, core, own, other, base, panel, *before):
    whole, anywhere = pl.BlockSpec(memory_space=pltpu.VMEM), pl.BlockSpec(memory_space=pl.ANY)
    return pl.pallas_call(
        functools.partial(finish_kernel, chunk),
        in_specs=[pl.BlockSpec(memory_space=pltpu.SMEM)] + [whole] * 4 + [anywhere, whole][: len(before)],
        out_specs=(anywhere, whole),
        scratch_shapes=[pltpu.SemaphoreType.DMA((2,))],
        out_shape=(
            jax.ShapeDtypeStruct((2, 512, 2 * HALF), jnp.float32),
            jax.ShapeDtypeStruct((SLAB, 2 * HALF), jnp.float32),
        ),
        input_output_aliases={5: 0} if before else {},
        compiler_params=pltpu.CompilerParams(vmem_limit_bytes=24 * 2**20),
        cost_estimate=pl.CostEstimate(
            flops=24 * SLAB * 512 * (BOUNDS[chunk][1] - BOUNDS[chunk][0]), bytes_accessed=6 * 2**20, transcendentals=0
        ),
        name="finish",
    )(core, own, other, base, panel, *before)


def swap(x, axis, bit, shift=0):
    n = lax.axis_size(axis)
    return lax.ppermute(x, axis, [(i, (((i + shift) % n ^ bit) - shift) % n) for i in range(n)])


def after(x, *others):
    return lax.optimization_barrier((x, *others))[0]


def sum_y(slabs):
    near = slabs[0]
    for ky in range(1, NY):
        near = near + swap(slabs[ky], "y", ky)
    return near


def sum_z(s, shift):
    for bit in (1, 2, 4):
        n = s.shape[0] // 2
        s = s[:n] + swap(s[n:], "z", bit, shift)
    return s[0]


def spread_x(v):
    others = [lax.ppermute(v, "x", [(NX - 1, i)]) for i in range(NX - 1)]
    return jnp.where(lax.axis_index("x") == NX - 1, v, others[0] + others[1] + others[2])


def gather_z(v):
    return lax.all_to_all(jnp.broadcast_to(v, (NZ, *v.shape)), "z", 0, 0, tiled=True)


def gather_y(v):
    return [v] + [swap(v, "y", ky) for ky in range(1, NY)]


def local(coupling, earlier, right_sides, panel_blocks, block_inverses):
    z, y, core = (lax.axis_index(a) for a in ("z", "y", "core"))
    coupling, earlier = coupling[0, 0, :, 0], earlier[:, 0]
    right, panel = right_sides[0, 0], panel_blocks[0, 0]
    is_first = core == 0
    z_id, y_id, core_id = (i.astype(jnp.int32).reshape(1) for i in (z, y, core))

    slabs_a = term(z_id, y_id, coupling, earlier, 0)
    slabs_b = term(z_id, y_id, after(coupling, *slabs_a), earlier, 1)
    total_a = sum_z(sum_y(slabs_a), SHIFTS[0])
    total_b = sum_z(sum_y(slabs_b), SHIFTS[1])
    base = [
        right[:, half * HALF : (half + 1) * HALF]
        - jnp.concatenate([t[:, half * PART : (half + 1) * PART] for t in (total_a, total_b)], axis=1)
        for half in (0, 1)
    ]

    kept = jnp.where(is_first, base[0], base[1])
    given = jnp.concatenate([jnp.where(is_first, base[1], base[0]), panel[0, :, 256:]], axis=1)
    came = swap(given, "core", 1)
    last = jnp.where(is_first, came[:, :HALF], kept)
    other = jnp.where(is_first, kept, came[:, :HALF])
    link = jnp.where(is_first, panel[0, :, :256], came[:, HALF:])
    v = [last[:, :CUT], other[:, :CUT], link, last[:, CUT:], other[:, CUT:]]
    v = spread_x(jnp.concatenate(v, axis=1))
    split_at = 2 * CUT + 256
    v_b = jnp.stack(gather_y(v[:, split_at:]))
    pieces_a = gather_y(after(gather_z(v[:, :split_at]), v_b))
    pieces_b = gather_z(v_b)

    part = jnp.stack([p[:, :, 2 * CUT :] for p in pieces_a])
    link = swap(part, "core", 1)
    own_a = solve(CUT, y_id, core_id, block_inverses, link, pieces_a, pieces_a)
    other_a = swap(own_a, "core", 1)
    own_b = solve(HALF - CUT, y_id, core_id, block_inverses, link, [pieces_b], pieces_a)
    other_b = swap(own_b, "core", 1)
    base = jnp.concatenate(base, axis=1)
    done_a = finish(0, core_id, own_a, other_a, base, panel)
    solved, pending = finish(1, core_id, own_b, other_b, base, panel, *done_a)
    return solved, pending[None, None]


def solution(mesh):
    inner = Mesh(mesh.devices.reshape(NZ, NY, NX, NCORE), ("z", "y", "x", "core"))
    row, col = ("z", "y"), ("x", "core")
    in_specs = (
        P(None, col, None, row, None, None),
        P(None, row, None, None),
        P(None, col, row, None),
        P(None, col, None, row, None),
        P(),
    )
    out_specs = (P(), P(None, col, row, None))
    return jax.shard_map(local, mesh=inner, in_specs=in_specs, out_specs=out_specs, check_vma=False)
```

time: 209 us -> 174 us (0.83)
  blocking collectives: 17.3 us -> 0 us
  local copies, waits for them, and re-layouts: 18.1 us -> 2.94 us
  starting transfers between devices: 56.4 us -> 50 us
  Pallas kernels: 30.2 us -> 36 us
  other arithmetic: 3.82 us -> 1.35 us
    all_to_all x1 -> x0, blocking collectives: 17.3 us -> none  [gather_z(): lax.all_to_all(jnp.broadcast_to(v, (NZ, *v.shape)), 'z', 0, 0, tiled=True)]
    unnamed x44 -> x27, local copies, waits for them, and re-layouts: 15.7 us -> 0.83 us
    all_to_all x2 -> x0, starting transfers between devices: 14.6 us -> none  [sum_z(): return jnp.sum(lax.all_to_all(near, 'z', 0, 0, tiled=True), axis=0)]
    all_to_all x1 -> x2, starting transfers between devices: 3.45 us -> 11.3 us  [gather_z(): lax.all_to_all(jnp.broadcast_to(v, (NZ, *v.shape)), 'z', 0, 0, tiled=True)]
    all_to_all x1 -> x2, waiting for transfers between devices: 9.25 us -> 15.2 us  [gather_z(): lax.all_to_all(jnp.broadcast_to(v, (NZ, *v.shape)), 'z', 0, 0, tiled=True)]
    pallas_call x5 -> x6, Pallas kernels: 30.2 us -> 36 us  [the longest x2 18.7 us: term(): pl.pallas_call(functools.partial(term_kernel, SHIFTS[chunk]), grid_spec=p...]
    ppermute x6 -> x3, waiting for transfers between devices: 11.2 us -> 7.75 us  [spread_x(): others = [lax.ppermute(v, 'x', [(NX - 1, i)]) for i in range(NX - 1)]]
    ppermute x18 -> x22, starting transfers between devices: 33.1 us -> 36.1 us  [swap(): lax.ppermute(x, axis, [(i, (((i + shift) % n ^ bit) - shift) % n) for i i...]
  transfers between devices with their start and end apart: 27 -> 27, of which waited for: 16 -> 15; matrix products, arithmetic and copies ran while one was open for 2% -> 1% of each run, Pallas kernels for 5% -> 14%
where the time goes in v2:
time: 174 us
  waiting for transfers between devices  82.3 us (47%)
  starting transfers between devices  50 us (29%)
  Pallas kernels  36 us (21%)
  local copies, waits for them, and re-layouts  2.94 us (2%)
    ppermute x22, waiting for transfers between devices, swap(): lax.ppermute(x, axis, [(i, (((i + shift) % n ^ bit) - shift) % n) for i i...  59.4 us
    ppermute x22, starting transfers between devices, swap(): lax.ppermute(x, axis, [(i, (((i + shift) % n ^ bit) - shift) % n) for i i...  36.1 us
    pallas_call x2, Pallas kernels, term(): pl.pallas_call(functools.partial(term_kernel, SHIFTS[chunk]), grid_spec=p...  18.7 us
    all_to_all x2, waiting for transfers between devices, gather_z(): lax.all_to_all(jnp.broadcast_to(v, (NZ, *v.shape)), 'z', 0, 0, tiled=True)  15.2 us
    all_to_all x2, starting transfers between devices, gather_z(): lax.all_to_all(jnp.broadcast_to(v, (NZ, *v.shape)), 'z', 0, 0, tiled=True)  11.3 us
    pallas_call x2, Pallas kernels, solve(): pl.pallas_call(functools.partial(solve_kernel, n), in_specs=[scalar] * 2...  11.1 us
    ppermute x3, waiting for transfers between devices, spread_x(): others = [lax.ppermute(v, 'x', [(NX - 1, i)]) for i in range(NX - 1)]  7.75 us
    pallas_call x2, Pallas kernels, finish(): pl.pallas_call(functools.partial(finish_kernel, chunk), in_specs=[pl.Bloc...  6.11 us
  transfers between devices with their start and end apart: 27, of which 15 were waited for; matrix products, arithmetic and copies ran while one was open for 1% of the time, Pallas kernels for 14%

profile of v2, /device:TPU:1, one launch (start us, length us, event | category | flops | bytes accessed | tf_op | source)
XLA Modules:
  0.0 173.8 jit_solution(2156465469807231177)
XLA Ops:
  0.6 9.3 %term.2 = (f32[8,16,768]{2,1,0:T(8,128)}, f32[8,16,768]{2,1,0:T(8,128)}, f32[8,16,768]{2,1,0:T(8,128)}, f32[8,16,768]{2,1,0:T(8,128)}) custom-call(s32[1]{0:T(128)} %bitcast.3.z_ref, s32[1]{0:T(128)} %bitcast.1.y_ref, f32[4,512,512]{2,1,0:T(8,128)} %bitcast.39, f32[4,512,1536]{2,1,0:T(8,128)} %bitcast.35, f32[4,512,1536]{2,1,0:T(8,128)} %bitcast.36), custom_call_target="tpu_custom_call" | custom-call | flops 4831838208 | bytes 12582912 | tf_op jit(solution)/shard_map/term/pallas_call | solution.py:58
  10.0 2.1 %collective-permute-start = (f32[8,16,768]{2,1,0:T(8,128)}, f32[8,16,768]{2,1,0:T(8,128)S(1)}, u32[]{:S(2)}, u32[]{:S(2)}) collective-permute-start(f32[8,16,768]{2,1,0:T(8,128)} %get-tuple-element.17), channel_id=1, source_target_pairs={{0,8},{8,0},{16,24},{24,16},{1,9},{9,1},{17,25},{25,17},{2,10},{10... | collective-permute-start | bytes 1179656 | tf_op jit(solution)/shard_map/ppermute | solution.py:185
  12.1 2.6 %collective-permute-start.1 = (f32[8,16,768]{2,1,0:T(8,128)}, f32[8,16,768]{2,1,0:T(8,128)S(1)}, u32[]{:S(2)}, u32[]{:S(2)}) collective-permute-start(f32[8,16,768]{2,1,0:T(8,128)} %get-tuple-element.18), channel_id=1, source_target_pairs={{0,16},{8,24},{16,0},{24,8},{1,17},{9,25},{17,1},{25,9},{2,18},{10... | collective-permute-start | bytes 1179656 | tf_op jit(solution)/shard_map/ppermute | solution.py:185
  14.7 9.4 %term.3 = (f32[8,16,768]{2,1,0:T(8,128)}, f32[8,16,768]{2,1,0:T(8,128)}, f32[8,16,768]{2,1,0:T(8,128)}, f32[8,16,768]{2,1,0:T(8,128)}) custom-call(s32[1]{0:T(128)} %bitcast.3.z_ref, s32[1]{0:T(128)} %bitcast.1.y_ref, f32[4,512,512]{2,1,0:T(8,128)} %bitcast.40, f32[4,512,1536]{2,1,0:T(8,128)} %bitcast.37, f32[4,512,1536]{2,1,0:T(8,128)} %bitcast.38), custom_call_target="tpu_custom_call" | custom-call | flops 4831838208 | bytes 12582912 | tf_op jit(solution)/shard_map/term/pallas_call | solution.py:58
  24.1 3.8 %collective-permute-start.7 = (f32[8,16,768]{2,1,0:T(8,128)}, f32[8,16,768]{2,1,0:T(8,128)S(1)}, u32[]{:S(2)}, u32[]{:S(2)}) collective-permute-start(f32[8,16,768]{2,1,0:T(8,128)} %get-tuple-element.23), channel_id=1, source_target_pairs={{0,16},{8,24},{16,0},{24,8},{1,17},{9,25},{17,1},{25,9},{2,18},{10... | collective-permute-start | bytes 1179656 | tf_op jit(solution)/shard_map/ppermute | solution.py:185
  28.0 3.9 %collective-permute-done.1 = f32[8,16,768]{2,1,0:T(8,128)S(1)} collective-permute-done((f32[8,16,768]{2,1,0:T(8,128)}, f32[8,16,768]{2,1,0:T(8,128)S(1)}, u32[]{:S(2)}, u32[]{:S(2)}) %collective-permute-start.1) | collective-permute-done | bytes 393248 | tf_op jit(solution)/shard_map/ppermute | solution.py:185
  31.9 1.7 %collective-permute-done.2 = f32[8,16,768]{2,1,0:T(8,128)S(1)} collective-permute-done((f32[8,16,768]{2,1,0:T(8,128)}, f32[8,16,768]{2,1,0:T(8,128)S(1)}, u32[]{:S(2)}, u32[]{:S(2)}) %collective-permute-start.2) | collective-permute-done | bytes 393248 | tf_op jit(solution)/shard_map/ppermute | solution.py:185
  33.8 1.7 collective-permute-start.3
  35.5 1.4 collective-permute-done.6
  36.9 11.9 %collective-permute-done.7 = f32[8,16,768]{2,1,0:T(8,128)S(1)} collective-permute-done((f32[8,16,768]{2,1,0:T(8,128)}, f32[8,16,768]{2,1,0:T(8,128)S(1)}, u32[]{:S(2)}, u32[]{:S(2)}) %collective-permute-start.7) | collective-permute-done | bytes 393248 | tf_op jit(solution)/shard_map/ppermute | solution.py:185
  48.8 2.0 %collective-permute-done.8 = f32[8,16,768]{2,1,0:T(8,128)S(1)} collective-permute-done((f32[8,16,768]{2,1,0:T(8,128)}, f32[8,16,768]{2,1,0:T(8,128)S(1)}, u32[]{:S(2)}, u32[]{:S(2)}) %collective-permute-start.8) | collective-permute-done | bytes 393248 | tf_op jit(solution)/shard_map/ppermute | solution.py:185
  50.8 1.1 add_add_fusion
  51.9 5.7 %collective-permute-start.9 = (f32[4,16,768]{2,1,0:T(8,128)S(1)}, f32[4,16,768]{2,1,0:T(8,128)S(1)}, u32[]{:S(2)}, u32[]{:S(2)}) collective-permute-start(f32[4,16,768]{2,1,0:T(8,128)S(1)} %slice.138), channel_id=1, source_target_pairs={{0,224},{32,64},{64,32},{96,128},{128,96},{160,192},{192,160},{224... | collective-permute-start | bytes 589832 | tf_op jit(solution)/shard_map/ppermute | solution.py:185
  57.6 0.1 collective-permute-start.4
  57.7 2.9 %collective-permute-done.9 = f32[4,16,768]{2,1,0:T(8,128)S(1)} collective-permute-done((f32[4,16,768]{2,1,0:T(8,128)S(1)}, f32[4,16,768]{2,1,0:T(8,128)S(1)}, u32[]{:S(2)}, u32[]{:S(2)}) %collective-permute-start.9) | collective-permute-done | bytes 196640 | tf_op jit(solution)/shard_map/ppermute | solution.py:185
  60.7 0.1 collective-permute-start.10
  60.8 2.1 %collective-permute-done.4 = f32[2,16,768]{2,1,0:T(8,128)S(1)} collective-permute-done((f32[2,16,768]{2,1,0:T(8,128)S(1)}, f32[2,16,768]{2,1,0:T(8,128)S(1)}, u32[]{:S(2)}, u32[]{:S(2)}) %collective-permute-start.4) | collective-permute-done | bytes 98336 | tf_op jit(solution)/shard_map/ppermute | solution.py:185
  62.9 5.5 %collective-permute-start.5 = (f32[1,16,768]{2,1,0:T(8,128)S(1)}, f32[1,16,768]{2,1,0:T(8,128)S(1)}, u32[]{:S(2)}, u32[]{:S(2)}) collective-permute-start(f32[1,16,768]{2,1,0:T(8,128)S(1)} %slice.135), channel_id=1, source_target_pairs={{0,128},{32,160},{64,192},{96,224},{128,0},{160,32},{192,64},{224,... | collective-permute-start | bytes 147464 | tf_op jit(solution)/shard_map/ppermute | solution.py:185
  68.4 2.4 %collective-permute-start.11 = (f32[1,16,768]{2,1,0:T(8,128)S(1)}, f32[1,16,768]{2,1,0:T(8,128)S(1)}, u32[]{:S(2)}, u32[]{:S(2)}) collective-permute-start(f32[1,16,768]{2,1,0:T(8,128)S(1)} %slice.142), channel_id=1, source_target_pairs={{0,128},{32,160},{64,192},{96,224},{128,0},{160,32},{192,64},{224,... | collective-permute-start | bytes 147464 | tf_op jit(solution)/shard_map/ppermute | solution.py:185
  70.8 6.6 %collective-permute-done.11 = f32[1,16,768]{2,1,0:T(8,128)S(1)} collective-permute-done((f32[1,16,768]{2,1,0:T(8,128)S(1)}, f32[1,16,768]{2,1,0:T(8,128)S(1)}, u32[]{:S(2)}, u32[]{:S(2)}) %collective-permute-start.11) | collective-permute-done | bytes 49184 | tf_op jit(solution)/shard_map/ppermute | solution.py:185
  77.5 3.4 %collective-permute-start.12 = (f32[16,1024]{1,0:T(8,128)S(1)}, f32[16,1024]{1,0:T(8,128)S(1)}, u32[]{:S(2)}, u32[]{:S(2)}) collective-permute-start(f32[16,1024]{1,0:T(8,128)S(1)} %pad_maximum_fusion.3), channel_id=1, source_target_pairs={{0,1},{1,0},{2,3},{3,2},{4,5},{5,4},{6,7},{7,6},{8,9},{9,8},{10,11... | collective-permute-start | bytes 196616 | tf_op jit(solution)/shard_map/ppermute | solution.py:185
  80.8 0.9 collective-permute-done.12
  81.8 0.7 collective-permute-start.15
  82.5 0.7 collective-permute-start.14
  83.2 1.3 collective-permute-start.13
  84.5 7.7 %collective-permute-done.13 = f32[16,1792]{1,0:T(8,128)S(1)} collective-permute-done((f32[16,1792]{1,0:T(8,128)S(1)}, f32[16,1792]{1,0:T(8,128)S(1)}, u32[]{:S(2)}, u32[]{:S(2)}) %collective-permute-start.13) | collective-permute-done | bytes 114720 | tf_op jit(solution)/shard_map/ppermute | solution.py:207
  92.3 0.9 broadcast_in_dim.9
  93.2 7.0 %all-to-all-start = ((f32[8,16,1280]{2,1,0:T(8,128)}), f32[8,16,1280]{2,1,0:T(8,128)S(1)}, u32[]{:S(2)}, u32[]{:S(2)}) async-start(f32[8,16,1280]{2,1,0:T(8,128)} %broadcast_in_dim.9), calls=%async_computation | async-start | bytes 1310720 | tf_op jit(solution)/shard_map/all_to_all | solution.py:212
  100.2 0.1 collective-permute-start.17
  100.3 0.5 collective-permute-start.16
  100.8 2.7 %collective-permute-start.18 = (f32[16,512]{1,0:T(8,128)S(1)}, f32[16,512]{1,0:T(8,128)S(1)}, u32[]{:S(2)}, u32[]{:S(2)}) collective-permute-start(f32[16,512]{1,0:T(8,128)S(1)} %get-tuple-element.36), channel_id=1, source_target_pairs={{0,24},{8,16},{16,8},{24,0},{1,25},{9,17},{17,9},{25,1},{2,26},{10... | collective-permute-start | bytes 98312 | tf_op jit(solution)/shard_map/ppermute | solution.py:185
  103.5 1.0 collective-permute-done.17
  104.6 0.3 collective-permute-done.18
  104.9 15.2 %all-to-all-done.refs_1_.refs_0_.refs_4_ = f32[8,16,1280]{2,1,0:T(8,128)S(1)} async-done(((f32[8,16,1280]{2,1,0:T(8,128)}), f32[8,16,1280]{2,1,0:T(8,128)S(1)}, u32[]{:S(2)}, u32[]{:S(2)}) %all-to-all-start) | async-done | bytes 655392 | tf_op jit(solution)/shard_map/all_to_all | solution.py:212
  120.1 1.0 collective-permute-start.20
  121.1 1.1 broadcast_in_dim.10
  122.2 4.2 %all-to-all-start.1 = ((f32[8,4,16,512]{3,2,1,0:T(8,128)}), f32[8,4,16,512]{3,2,1,0:T(8,128)}, u32[]{:S(2)}, u32[]{:S(2)}) async-start(f32[8,4,16,512]{3,2,1,0:T(8,128)} %broadcast_in_dim.10), calls=%async_computation.1 | async-start | bytes 2097152 | tf_op jit(solution)/shard_map/all_to_all | solution.py:212
  126.5 2.3 %collective-permute-start.19 = (f32[8,16,1280]{2,1,0:T(8,128)S(1)}, f32[8,16,1280]{2,1,0:T(8,128)S(1)}, u32[]{:S(2)}, u32[]{:S(2)}) collective-permute-start(f32[8,16,1280]{2,1,0:T(8,128)S(1)} %all-to-all-done.refs_1_.refs_0_.refs_4_), channel_id=1, source_target_pairs={{0,8},{8,0},{16,24},{24,16},{1,9},{9,1},{17,25},{25,17},{2,10},{10... | collective-permute-start | bytes 1966088 | tf_op jit(solution)/shard_map/ppermute | solution.py:185
  128.8 22.9 %collective-permute-done.21.refs_4_.refs_3_.refs_7_ = f32[8,16,1280]{2,1,0:T(8,128)S(1)} collective-permute-done((f32[8,16,1280]{2,1,0:T(8,128)S(1)}, f32[8,16,1280]{2,1,0:T(8,128)S(1)}, u32[]{:S(2)}, u32[]{:S(2)}) %collective-permute-start.21) | collective-permute-done | bytes 655392 | tf_op jit(solution)/shard_map/ppermute | solution.py:185
  151.9 1.4 collective-permute-start.22
  153.3 1.5 collective-permute-done.22.other_hbm
  154.8 0.8 copy-done.7
  155.6 5.9 %solve.3.own = f32[2,512,512]{2,1,0:T(8,128)} custom-call(s32[1]{0:T(128)} %bitcast.1.y_ref, s32[1]{0:T(128)} %bitcast.core_ref, f32[2,512,512]{2,1,0:T(8,128)} %inv_hbm.3, f32[4,8,16,256]{3,2,1,0:T(8,128)} %copy-done.7, f32[8,16,1280]{2,1,0:T(8,128)} %copy-done.3, f32[8,16,1280]{2,1,0:T(8,128)} %copy-done.6, f32[8,16,1280]{2,1,0:T(8,128)} %copy-done.5, ...), custom_call_target="tpu_custom_call" | custom-call | flops 2415919104 | bytes 6291456 | tf_op jit(solution)/shard_map/solve/pallas_call | solution.py:121
  161.5 0.5 collective-permute-start.24
  162.0 5.3 %solve.2.own = f32[2,512,256]{2,1,0:T(8,128)} custom-call(s32[1]{0:T(128)} %bitcast.1.y_ref, s32[1]{0:T(128)} %bitcast.core_ref, f32[2,512,512]{2,1,0:T(8,128)} %inv_hbm.3, f32[4,8,16,256]{3,2,1,0:T(8,128)} %copy-done.7, f32[8,4,16,512]{3,2,1,0:T(8,128)} %all-to-all-done.1.refs_0_, f32[8,16,1280]{2,1,0:T(8,128)} %copy-done.3, f32[8,16,1280]{2,1,0:T(8,128)} %copy-done.6, ...), custom_call_target="tpu_custom_call" | custom-call | flops 1207959552 | bytes 6291456 | tf_op jit(solution)/shard_map/solve/pallas_call | solution.py:121
  167.2 0.2 collective-permute-start.23
  167.5 3.7 %finish.2 = (f32[2,512,1536]{2,1,0:T(8,128)}, f32[16,1536]{1,0:T(8,128)S(1)}) custom-call(s32[1]{0:T(128)} %bitcast.core_ref, f32[2,512,512]{2,1,0:T(8,128)S(1)} %copy-done, f32[2,512,512]{2,1,0:T(8,128)} %collective-permute-done.24.other, f32[16,1536]{1,0:T(8,128)S(1)} %pad_maximum_fusion.2.base, f32[2,16,512]{2,1,0:T(8,128)S(1)} %bitcast.33), custom_call_target="tpu_custom_call" | custom-call | flops 100663296 | bytes 6291456 | tf_op jit(solution)/shard_map/finish/pallas_call | solution.py:165
  171.2 2.4 %finish.3 = (f32[2,512,1536]{2,1,0:T(8,128)}, f32[16,1536]{1,0:T(8,128)}) custom-call(s32[1]{0:T(128)} %bitcast.core_ref, f32[2,512,256]{2,1,0:T(8,128)S(1)} %copy-done.1, f32[2,512,256]{2,1,0:T(8,128)S(1)} %collective-permute-done.23.other, f32[16,1536]{1,0:T(8,128)S(1)} %pad_maximum_fusion.2.base, ...), custom_call_target="tpu_custom_call", output_to_operand_aliasing={{0}: (5, {})} | custom-call | flops 50331648 | bytes 6291456 | tf_op jit(solution)/shard_map/finish/pallas_call | solution.py:165
  (73 shorter events, 0.5 us)
Async XLA Ops:
  10.0 18.0 %collective-permute-start = (f32[8,16,768]{2,1,0:T(8,128)}, f32[8,16,768]{2,1,0:T(8,128)S(1)}, u32[]{:S(2)}, u32[]{:S(2)}) collective-permute-start(f32[8,16,768]{2,1,0:T(8,128)} %get-tuple-element.17), channel_id=1, source_target_pairs={{0,8},{8,0},{16,24},{24,16},{1,9},{9,1},{17,25},{25,17},{2,10},{10... | collective-permute-start | bytes 1179656 | tf_op jit(solution)/shard_map/ppermute | solution.py:185
  12.1 19.8 %collective-permute-start.1 = (f32[8,16,768]{2,1,0:T(8,128)}, f32[8,16,768]{2,1,0:T(8,128)S(1)}, u32[]{:S(2)}, u32[]{:S(2)}) collective-permute-start(f32[8,16,768]{2,1,0:T(8,128)} %get-tuple-element.18), channel_id=1, source_target_pairs={{0,16},{8,24},{16,0},{24,8},{1,17},{9,25},{17,1},{25,9},{2,18},{10... | collective-permute-start | bytes 1179656 | tf_op jit(solution)/shard_map/ppermute | solution.py:185
  14.7 18.9 %collective-permute-start.2 = (f32[8,16,768]{2,1,0:T(8,128)}, f32[8,16,768]{2,1,0:T(8,128)S(1)}, u32[]{:S(2)}, u32[]{:S(2)}) collective-permute-start(f32[8,16,768]{2,1,0:T(8,128)} %get-tuple-element.19), channel_id=1, source_target_pairs={{0,24},{8,16},{16,8},{24,0},{1,25},{9,17},{17,9},{25,1},{2,26},{10... | collective-permute-start | bytes 1179656 | tf_op jit(solution)/shard_map/ppermute | solution.py:185
  14.7 13.3 %copy-start.2 = (f32[1,1,2,16,512]{4,3,2,1,0:T(8,128)S(1)}, f32[1,1,2,16,512]{4,3,2,1,0:T(8,128)}, u32[]{:S(2)}) copy-start(f32[1,1,2,16,512]{4,3,2,1,0:T(8,128)} %param.8) | copy-start | bytes 196612
  14.7 18.9 %copy-start.10 = (f32[8,16,768]{2,1,0:T(8,128)S(1)}, f32[8,16,768]{2,1,0:T(8,128)}, u32[]{:S(2)}) copy-start(f32[8,16,768]{2,1,0:T(8,128)} %get-tuple-element.16) | copy-start | bytes 1179652
  24.1 53.3 %copy-start.11 = (f32[1,1,16,1536]{3,2,1,0:T(8,128)S(1)}, f32[1,1,16,1536]{3,2,1,0:T(8,128)}, u32[]{:S(2)}) copy-start(f32[1,1,16,1536]{3,2,1,0:T(8,128)} %param.7) | copy-start | bytes 294916
  24.1 12.8 %collective-permute-start.6 = (f32[8,16,768]{2,1,0:T(8,128)}, f32[8,16,768]{2,1,0:T(8,128)S(1)}, u32[]{:S(2)}, u32[]{:S(2)}) collective-permute-start(f32[8,16,768]{2,1,0:T(8,128)} %get-tuple-element.22), channel_id=1, source_target_pairs={{0,8},{8,0},{16,24},{24,16},{1,9},{9,1},{17,25},{25,17},{2,10},{10... | collective-permute-start | bytes 1179656 | tf_op jit(solution)/shard_map/ppermute | solution.py:185
  24.1 24.7 %collective-permute-start.7 = (f32[8,16,768]{2,1,0:T(8,128)}, f32[8,16,768]{2,1,0:T(8,128)S(1)}, u32[]{:S(2)}, u32[]{:S(2)}) collective-permute-start(f32[8,16,768]{2,1,0:T(8,128)} %get-tuple-element.23), channel_id=1, source_target_pairs={{0,16},{8,24},{16,0},{24,8},{1,17},{9,25},{17,1},{25,9},{2,18},{10... | collective-permute-start | bytes 1179656 | tf_op jit(solution)/shard_map/ppermute | solution.py:185
  28.0 22.8 %collective-permute-start.8 = (f32[8,16,768]{2,1,0:T(8,128)}, f32[8,16,768]{2,1,0:T(8,128)S(1)}, u32[]{:S(2)}, u32[]{:S(2)}) collective-permute-start(f32[8,16,768]{2,1,0:T(8,128)} %get-tuple-element.24), channel_id=1, source_target_pairs={{0,24},{8,16},{16,8},{24,0},{1,25},{9,17},{17,9},{25,1},{2,26},{10... | collective-permute-start | bytes 1179656 | tf_op jit(solution)/shard_map/ppermute | solution.py:185
  33.8 23.8 %collective-permute-start.3 = (f32[4,16,768]{2,1,0:T(8,128)S(1)}, f32[4,16,768]{2,1,0:T(8,128)S(1)}, u32[]{:S(2)}, u32[]{:S(2)}) collective-permute-start(f32[4,16,768]{2,1,0:T(8,128)S(1)} %slice.131), channel_id=1, source_target_pairs={{0,32},{32,0},{64,96},{96,64},{128,160},{160,128},{192,224},{224,1... | collective-permute-start | bytes 589832 | tf_op jit(solution)/shard_map/ppermute | solution.py:185
  51.9 8.7 %collective-permute-start.9 = (f32[4,16,768]{2,1,0:T(8,128)S(1)}, f32[4,16,768]{2,1,0:T(8,128)S(1)}, u32[]{:S(2)}, u32[]{:S(2)}) collective-permute-start(f32[4,16,768]{2,1,0:T(8,128)S(1)} %slice.138), channel_id=1, source_target_pairs={{0,224},{32,64},{64,32},{96,128},{128,96},{160,192},{192,160},{224... | collective-permute-start | bytes 589832 | tf_op jit(solution)/shard_map/ppermute | solution.py:185
  57.6 5.3 %collective-permute-start.4 = (f32[2,16,768]{2,1,0:T(8,128)S(1)}, f32[2,16,768]{2,1,0:T(8,128)S(1)}, u32[]{:S(2)}, u32[]{:S(2)}) collective-permute-start(f32[2,16,768]{2,1,0:T(8,128)S(1)} %slice.133), channel_id=1, source_target_pairs={{0,64},{32,96},{64,0},{96,32},{128,192},{160,224},{192,128},{224,1... | collective-permute-start | bytes 294920 | tf_op jit(solution)/shard_map/ppermute | solution.py:185
  60.7 7.7 %collective-permute-start.10 = (f32[2,16,768]{2,1,0:T(8,128)S(1)}, f32[2,16,768]{2,1,0:T(8,128)S(1)}, u32[]{:S(2)}, u32[]{:S(2)}) collective-permute-start(f32[2,16,768]{2,1,0:T(8,128)S(1)} %slice.140), channel_id=1, source_target_pairs={{0,64},{32,224},{64,0},{96,160},{128,192},{160,96},{192,128},{224,... | collective-permute-start | bytes 294920 | tf_op jit(solution)/shard_map/ppermute | solution.py:185
  62.9 7.9 %collective-permute-start.5 = (f32[1,16,768]{2,1,0:T(8,128)S(1)}, f32[1,16,768]{2,1,0:T(8,128)S(1)}, u32[]{:S(2)}, u32[]{:S(2)}) collective-permute-start(f32[1,16,768]{2,1,0:T(8,128)S(1)} %slice.135), channel_id=1, source_target_pairs={{0,128},{32,160},{64,192},{96,224},{128,0},{160,32},{192,64},{224,... | collective-permute-start | bytes 147464 | tf_op jit(solution)/shard_map/ppermute | solution.py:185
  68.4 9.0 %collective-permute-start.11 = (f32[1,16,768]{2,1,0:T(8,128)S(1)}, f32[1,16,768]{2,1,0:T(8,128)S(1)}, u32[]{:S(2)}, u32[]{:S(2)}) collective-permute-start(f32[1,16,768]{2,1,0:T(8,128)S(1)} %slice.142), channel_id=1, source_target_pairs={{0,128},{32,160},{64,192},{96,224},{128,0},{160,32},{192,64},{224,... | collective-permute-start | bytes 147464 | tf_op jit(solution)/shard_map/ppermute | solution.py:185
  77.4 15.7 %copy-start.8 = (f32[16,768]{1,0:T(8,128)}, f32[16,768]{1,0:T(8,128)S(1)}, u32[]{:S(2)}) copy-start(f32[16,768]{1,0:T(8,128)S(1)} %get-tuple-element.32) | copy-start | bytes 147460
  77.5 4.3 %collective-permute-start.12 = (f32[16,1024]{1,0:T(8,128)S(1)}, f32[16,1024]{1,0:T(8,128)S(1)}, u32[]{:S(2)}, u32[]{:S(2)}) collective-permute-start(f32[16,1024]{1,0:T(8,128)S(1)} %pad_maximum_fusion.3), channel_id=1, source_target_pairs={{0,1},{1,0},{2,3},{3,2},{4,5},{5,4},{6,7},{7,6},{8,9},{9,8},{10,11... | collective-permute-start | bytes 196616 | tf_op jit(solution)/shard_map/ppermute | solution.py:185
  81.8 2.7 %collective-permute-start.15 = (f32[16,1792]{1,0:T(8,128)S(1)}, f32[16,1792]{1,0:T(8,128)S(1)}, u32[]{:S(2)}, u32[]{:S(2)}) collective-permute-start(f32[16,1792]{1,0:T(8,128)S(1)} %slice_dynamic-update-slice_fusion.2), channel_id=1, source_target_pairs={{6,4},{7,5},{14,12},{15,13},{22,20},{23,21},{30,28},{31,29},{38,36... | collective-permute-start | bytes 344072 | tf_op jit(solution)/shard_map/ppermute | solution.py:207
  82.5 2.0 %collective-permute-start.14 = (f32[16,1792]{1,0:T(8,128)S(1)}, f32[16,1792]{1,0:T(8,128)S(1)}, u32[]{:S(2)}, u32[]{:S(2)}) collective-permute-start(f32[16,1792]{1,0:T(8,128)S(1)} %slice_dynamic-update-slice_fusion.2), channel_id=1, source_target_pairs={{6,2},{7,3},{14,10},{15,11},{22,18},{23,19},{30,26},{31,27},{38,34... | collective-permute-start | bytes 344072 | tf_op jit(solution)/shard_map/ppermute | solution.py:207
  83.2 9.1 %collective-permute-start.13 = (f32[16,1792]{1,0:T(8,128)S(1)}, f32[16,1792]{1,0:T(8,128)S(1)}, u32[]{:S(2)}, u32[]{:S(2)}) collective-permute-start(f32[16,1792]{1,0:T(8,128)S(1)} %slice_dynamic-update-slice_fusion.2), channel_id=1, source_target_pairs={{6,0},{7,1},{14,8},{15,9},{22,16},{23,17},{30,24},{31,25},{38,32},... | collective-permute-start | bytes 344072 | tf_op jit(solution)/shard_map/ppermute | solution.py:207
  93.2 27.0 %all-to-all-start = ((f32[8,16,1280]{2,1,0:T(8,128)}), f32[8,16,1280]{2,1,0:T(8,128)S(1)}, u32[]{:S(2)}, u32[]{:S(2)}) async-start(f32[8,16,1280]{2,1,0:T(8,128)} %broadcast_in_dim.9), calls=%async_computation | async-start | bytes 1310720 | tf_op jit(solution)/shard_map/all_to_all | solution.py:212
  100.2 4.4 %collective-permute-start.17 = (f32[16,512]{1,0:T(8,128)S(1)}, f32[16,512]{1,0:T(8,128)S(1)}, u32[]{:S(2)}, u32[]{:S(2)}) collective-permute-start(f32[16,512]{1,0:T(8,128)S(1)} %get-tuple-element.36), channel_id=1, source_target_pairs={{0,16},{8,24},{16,0},{24,8},{1,17},{9,25},{17,1},{25,9},{2,18},{10... | collective-permute-start | bytes 98312 | tf_op jit(solution)/shard_map/ppermute | solution.py:185
  100.3 4.3 %collective-permute-start.16 = (f32[16,512]{1,0:T(8,128)S(1)}, f32[16,512]{1,0:T(8,128)S(1)}, u32[]{:S(2)}, u32[]{:S(2)}) collective-permute-start(f32[16,512]{1,0:T(8,128)S(1)} %get-tuple-element.36), channel_id=1, source_target_pairs={{0,8},{8,0},{16,24},{24,16},{1,9},{9,1},{17,25},{25,17},{2,10},{10... | collective-permute-start | bytes 98312 | tf_op jit(solution)/shard_map/ppermute | solution.py:185
  100.8 4.1 %collective-permute-start.18 = (f32[16,512]{1,0:T(8,128)S(1)}, f32[16,512]{1,0:T(8,128)S(1)}, u32[]{:S(2)}, u32[]{:S(2)}) collective-permute-start(f32[16,512]{1,0:T(8,128)S(1)} %get-tuple-element.36), channel_id=1, source_target_pairs={{0,24},{8,16},{16,8},{24,0},{1,25},{9,17},{17,9},{25,1},{2,26},{10... | collective-permute-start | bytes 98312 | tf_op jit(solution)/shard_map/ppermute | solution.py:185
  120.1 34.7 %copy-start.3 = (f32[8,16,1280]{2,1,0:T(8,128)}, f32[8,16,1280]{2,1,0:T(8,128)S(1)}, u32[]{:S(2)}) copy-start(f32[8,16,1280]{2,1,0:T(8,128)S(1)} %all-to-all-done.refs_1_.refs_0_.refs_4_) | copy-start | bytes 1966084
  120.1 31.6 %collective-permute-start.21 = (f32[8,16,1280]{2,1,0:T(8,128)S(1)}, f32[8,16,1280]{2,1,0:T(8,128)S(1)}, u32[]{:S(2)}, u32[]{:S(2)}) collective-permute-start(f32[8,16,1280]{2,1,0:T(8,128)S(1)} %all-to-all-done.refs_1_.refs_0_.refs_4_), channel_id=1, source_target_pairs={{0,24},{8,16},{16,8},{24,0},{1,25},{9,17},{17,9},{25,1},{2,26},{10... | collective-permute-start | bytes 1966088 | tf_op jit(solution)/shard_map/ppermute | solution.py:185
  120.1 31.7 %collective-permute-start.20 = (f32[8,16,1280]{2,1,0:T(8,128)S(1)}, f32[8,16,1280]{2,1,0:T(8,128)S(1)}, u32[]{:S(2)}, u32[]{:S(2)}) collective-permute-start(f32[8,16,1280]{2,1,0:T(8,128)S(1)} %all-to-all-done.refs_1_.refs_0_.refs_4_), channel_id=1, source_target_pairs={{0,16},{8,24},{16,0},{24,8},{1,17},{9,25},{17,1},{25,9},{2,18},{10... | collective-permute-start | bytes 1966088 | tf_op jit(solution)/shard_map/ppermute | solution.py:185
  122.2 39.7 %all-to-all-start.1 = ((f32[8,4,16,512]{3,2,1,0:T(8,128)}), f32[8,4,16,512]{3,2,1,0:T(8,128)}, u32[]{:S(2)}, u32[]{:S(2)}) async-start(f32[8,4,16,512]{3,2,1,0:T(8,128)} %broadcast_in_dim.10), calls=%async_computation.1 | async-start | bytes 2097152 | tf_op jit(solution)/shard_map/all_to_all | solution.py:212
  126.5 25.3 %collective-permute-start.19 = (f32[8,16,1280]{2,1,0:T(8,128)S(1)}, f32[8,16,1280]{2,1,0:T(8,128)S(1)}, u32[]{:S(2)}, u32[]{:S(2)}) collective-permute-start(f32[8,16,1280]{2,1,0:T(8,128)S(1)} %all-to-all-done.refs_1_.refs_0_.refs_4_), channel_id=1, source_target_pairs={{0,8},{8,0},{16,24},{24,16},{1,9},{9,1},{17,25},{25,17},{2,10},{10... | collective-permute-start | bytes 1966088 | tf_op jit(solution)/shard_map/ppermute | solution.py:185
  151.8 3.1 %copy-start.4 = (f32[8,16,1280]{2,1,0:T(8,128)}, f32[8,16,1280]{2,1,0:T(8,128)S(1)}, u32[]{:S(2)}) copy-start(f32[8,16,1280]{2,1,0:T(8,128)S(1)} %collective-permute-done.21.refs_4_.refs_3_.refs_7_) | copy-start | bytes 1966084
  151.8 3.0 %copy-start.5 = (f32[8,16,1280]{2,1,0:T(8,128)}, f32[8,16,1280]{2,1,0:T(8,128)S(1)}, u32[]{:S(2)}) copy-start(f32[8,16,1280]{2,1,0:T(8,128)S(1)} %collective-permute-done.20.refs_3_.refs_2_.refs_6_) | copy-start | bytes 1966084
  151.8 3.0 %copy-start.6 = (f32[8,16,1280]{2,1,0:T(8,128)}, f32[8,16,1280]{2,1,0:T(8,128)S(1)}, u32[]{:S(2)}) copy-start(f32[8,16,1280]{2,1,0:T(8,128)S(1)} %collective-permute-done.19.refs_2_.refs_1_.refs_5_) | copy-start | bytes 1966084
  151.9 2.9 %collective-permute-start.22 = (f32[4,8,16,256]{3,2,1,0:T(8,128)S(1)}, f32[4,8,16,256]{3,2,1,0:T(8,128)S(1)}, u32[]{:S(2)}, u32[]{:S(2)}) collective-permute-start(f32[4,8,16,256]{3,2,1,0:T(8,128)S(1)} %pad_maximum_fusion), channel_id=1, source_target_pairs={{0,1},{1,0},{2,3},{3,2},{4,5},{5,4},{6,7},{7,6},{8,9},{9,8},{10,11... | collective-permute-start | bytes 1572872 | tf_op jit(solution)/shard_map/ppermute | solution.py:185
  154.8 0.8 copy-start.7
  161.5 5.9 %copy-start.9 = (f32[16,768]{1,0:T(8,128)S(1)}, f32[16,768]{1,0:T(8,128)}, u32[]{:S(2)}) copy-start(f32[16,768]{1,0:T(8,128)} %copy-done.8) | copy-start | bytes 147460
  161.5 6.0 %copy-start = (f32[2,512,512]{2,1,0:T(8,128)S(1)}, f32[2,512,512]{2,1,0:T(8,128)}, u32[]{:S(2)}) copy-start(f32[2,512,512]{2,1,0:T(8,128)} %solve.3.own) | copy-start | bytes 6291460
  161.5 5.9 %collective-permute-start.24 = (f32[2,512,512]{2,1,0:T(8,128)}, f32[2,512,512]{2,1,0:T(8,128)}, u32[]{:S(2)}, u32[]{:S(2)}) collective-permute-start(f32[2,512,512]{2,1,0:T(8,128)} %solve.3.own), channel_id=1, source_target_pairs={{0,1},{1,0},{2,3},{3,2},{4,5},{5,4},{6,7},{7,6},{8,9},{9,8},{10,11... | collective-permute-start | bytes 6291464 | tf_op jit(solution)/shard_map/ppermute | solution.py:185
  167.2 4.0 %copy-start.1 = (f32[2,512,256]{2,1,0:T(8,128)S(1)}, f32[2,512,256]{2,1,0:T(8,128)}, u32[]{:S(2)}) copy-start(f32[2,512,256]{2,1,0:T(8,128)} %solve.2.own) | copy-start | bytes 3145732
  167.2 3.9 %collective-permute-start.23 = (f32[2,512,256]{2,1,0:T(8,128)}, f32[2,512,256]{2,1,0:T(8,128)S(1)}, u32[]{:S(2)}, u32[]{:S(2)}) collective-permute-start(f32[2,512,256]{2,1,0:T(8,128)} %solve.2.own), channel_id=1, source_target_pairs={{0,1},{1,0},{2,3},{3,2},{4,5},{5,4},{6,7},{7,6},{8,9},{9,8},{10,11... | collective-permute-start | bytes 3145736 | tf_op jit(solution)/shard_map/ppermute | solution.py:185

commit v3 on v2

--- a/solution.py
+++ b/solution.py
@@ -16,6 +16,7 @@
 SHIFTS = (0, 1)
 CUT = 512
 BOUNDS = ((0, CUT), (CUT, HALF))
+PLACES = ((0, 0, 8), (3, 0, 8), (1, 0, 8), (2, 0, 4), (2, 4, 4))
 
 
 def split(x):
@@ -84,7 +85,7 @@
 
 
 def solve_kernel(n, y_ref, core_ref, inv_hbm, other_hbm, *refs):
-    pieces, links, (o_ref, b, inv, link, sems) = refs[: -NY - 5], refs[-NY - 5 : -5], refs[-5:]
+    pieces, links, (o_ref, b, inv, link, sems) = refs[:-10], refs[-10:-5], refs[-5:]
     y, core = y_ref[0], core_ref[0]
     begun = [0]
 
@@ -95,17 +96,22 @@
     def block(k):
         at = pl.ds(k * n, n)
         copies = [begin(inv_hbm.at[k], inv.at[k])]
-        for ky in range(NY):
-            source = pieces[ky].at[:, :, at] if len(pieces) > 1 else pieces[0].at[:, ky, :, at]
-            copies.append(begin(source, b.at[k, :, y ^ ky]))
+        if len(pieces) > 1:
+            for p, (by, z, count) in zip(pieces, PLACES):
+                copies.append(begin(p.at[:, :, at], b.at[k, pl.ds(z, count), (y + by) % NY]))
+        else:
+            for ky in range(NY):
+                copies.append(begin(pieces[0].at[:, ky, :, at], b.at[k, :, y ^ ky]))
         return copies
 
     here = pl.ds(pl.multiple_of(core * 256, 128), 256)
     there = pl.ds(pl.multiple_of((1 - core) * 256, 128), 256)
     copies0, copies1 = block(0), block(1)
-    for ky, p in enumerate(links):
-        copies1.append(begin(p.at[:, :, pl.ds(p.shape[2] - 256, 256)], link.at[:, y ^ ky, :, here]))
-        copies1.append(begin(other_hbm.at[ky], link.at[:, y ^ ky, :, there]))
+    for p, (by, z, count) in zip(links, PLACES):
+        target = link.at[pl.ds(z, count), (y + by) % NY]
+        copies1.append(begin(p.at[:, :, pl.ds(p.shape[2] - 256, 256)], target.at[:, :, here]))
+    for i, by in enumerate((0, -1, 1, 2)):
+        copies1.append(begin(other_hbm.at[i], link.at[:, (y + by + NY) % NY, :, there]))
     for copy in copies0:
         copy.wait()
     first = dot3(inv[0], b[0].reshape(512, n))
@@ -120,16 +126,16 @@
     scalar, anywhere = pl.BlockSpec(memory_space=pltpu.SMEM), pl.BlockSpec(memory_space=pl.ANY)
     return pl.pallas_call(
         functools.partial(solve_kernel, n),
-        in_specs=[scalar] * 2 + [anywhere] * (2 + len(pieces) + NY),
+        in_specs=[scalar] * 2 + [anywhere] * (2 + len(pieces) + len(links)),
         out_specs=pl.BlockSpec(memory_space=pltpu.VMEM),
         scratch_shapes=[
             pltpu.VMEM((2, NZ, NY, SLAB, n), jnp.float32),
             pltpu.VMEM((2, 512, 512), jnp.float32),
             pltpu.VMEM((NZ, NY, SLAB, 512), jnp.float32),
-            pltpu.SemaphoreType.DMA((2 + 4 * NY,)),
+            pltpu.SemaphoreType.DMA((21,)),
         ],
         out_shape=jax.ShapeDtypeStruct((2, 512, n), jnp.float32),
-        compiler_params=pltpu.CompilerParams(vmem_limit_bytes=56 * 2**20),
+        compiler_params=pltpu.CompilerParams(vmem_limit_bytes=60 * 2**20),
         cost_estimate=pl.CostEstimate(
             flops=18 * 512 * 512 * n, bytes_accessed=6 * 2**20, transcendentals=0
         ),
@@ -196,10 +202,14 @@
     return near
 
 
+def halve(s, bit, shift):
+    n = s.shape[0] // 2
+    return s[:n] + swap(s[n:], "z", bit, shift)
+
+
 def sum_z(s, shift):
     for bit in (1, 2, 4):
-        n = s.shape[0] // 2
-        s = s[:n] + swap(s[n:], "z", bit, shift)
+        s = halve(s, bit, shift)
     return s[0]
 
 
@@ -214,6 +224,17 @@
 
 def gather_y(v):
     return [v] + [swap(v, "y", ky) for ky in range(1, NY)]
+
+
+def step(x, axis, by):
+    n = lax.axis_size(axis)
+    return lax.ppermute(x, axis, [(i, (i + by) % n) for i in range(n)])
+
+
+def gather_y_twice(v):
+    up, down = step(v, "y", 1), step(v, "y", -1)
+    h = NZ // 2
+    return [v, up, down, step(up[:h], "y", 1), step(down[h:], "y", -1)]
 
 
 def local(coupling, earlier, right_sides, panel_blocks, block_inverses):
@@ -225,8 +246,10 @@
 
     slabs_a = term(z_id, y_id, coupling, earlier, 0)
     slabs_b = term(z_id, y_id, after(coupling, *slabs_a), earlier, 1)
-    total_a = sum_z(sum_y(slabs_a), SHIFTS[0])
-    total_b = sum_z(sum_y(slabs_b), SHIFTS[1])
+    near_a = halve(sum_y(slabs_a), 1, SHIFTS[0])
+    near_b = sum_y([after(slabs_b[0], near_a), *slabs_b[1:]])
+    total_a = halve(halve(near_a, 2, SHIFTS[0]), 4, SHIFTS[0])[0]
+    total_b = sum_z(near_b, SHIFTS[1])
     base = [
         right[:, half * HALF : (half + 1) * HALF]
         - jnp.concatenate([t[:, half * PART : (half + 1) * PART] for t in (total_a, total_b)], axis=1)
@@ -243,10 +266,10 @@
     v = spread_x(jnp.concatenate(v, axis=1))
     split_at = 2 * CUT + 256
     v_b = jnp.stack(gather_y(v[:, split_at:]))
-    pieces_a = gather_y(after(gather_z(v[:, :split_at]), v_b))
+    pieces_a = gather_y_twice(after(gather_z(v[:, :split_at]), v_b))
     pieces_b = gather_z(v_b)
 
-    part = jnp.stack([p[:, :, 2 * CUT :] for p in pieces_a])
+    part = jnp.concatenate([p[:, :, 2 * CUT :] for p in pieces_a]).reshape(NY, NZ, SLAB, 256)
     link = swap(part, "core", 1)
     own_a = solve(CUT, y_id, core_id, block_inverses, link, pieces_a, pieces_a)
     other_a = swap(own_a, "core", 1)

time: 174 us -> 167 us (0.960)
  waiting for transfers between devices: 82.3 us -> 72.3 us
  starting transfers between devices: 50 us -> 53 us
    ppermute x22 -> x19, waiting for transfers between devices: 59.4 us -> 33.6 us  [swap(): lax.ppermute(x, axis, [(i, (((i + shift) % n ^ bit) - shift) % n) for i i...]
    ppermute x0 -> x4, waiting for transfers between devices: none -> 15.8 us  [step(): return lax.ppermute(x, axis, [(i, (i + by) % n) for i in range(n)])]
    ppermute x0 -> x4, starting transfers between devices: none -> 3.09 us  [step(): return lax.ppermute(x, axis, [(i, (i + by) % n) for i in range(n)])]
    ppermute x22 -> x19, starting transfers between devices: 36.1 us -> 36.1 us  [swap(): lax.ppermute(x, axis, [(i, (((i + shift) % n ^ bit) - shift) % n) for i i...]
  transfers between devices with their start and end apart: 27 -> 28, of which waited for: 15 -> 17; matrix products, arithmetic and copies ran while one was open for 1% -> 1% of each run, Pallas kernels for 14% -> 15%
where the time goes in v3:
time: 167 us
  waiting for transfers between devices  72.3 us (43%)
  starting transfers between devices  53 us (32%)
  Pallas kernels  36 us (22%)
  local copies, waits for them, and re-layouts  2.99 us (2%)
    ppermute x19, starting transfers between devices, swap(): lax.ppermute(x, axis, [(i, (((i + shift) % n ^ bit) - shift) % n) for i i...  36.1 us
    ppermute x19, waiting for transfers between devices, swap(): lax.ppermute(x, axis, [(i, (((i + shift) % n ^ bit) - shift) % n) for i i...  33.6 us
    pallas_call x2, Pallas kernels, term(): pl.pallas_call(functools.partial(term_kernel, SHIFTS[chunk]), grid_spec=p...  18.7 us
    ppermute x4, waiting for transfers between devices, step(): return lax.ppermute(x, axis, [(i, (i + by) % n) for i in range(n)])  15.8 us
    all_to_all x2, waiting for transfers between devices, gather_z(): lax.all_to_all(jnp.broadcast_to(v, (NZ, *v.shape)), 'z', 0, 0, tiled=True)  15.2 us
    all_to_all x2, starting transfers between devices, gather_z(): lax.all_to_all(jnp.broadcast_to(v, (NZ, *v.shape)), 'z', 0, 0, tiled=True)  11.2 us
    pallas_call x2, Pallas kernels, solve(): pl.pallas_call(functools.partial(solve_kernel, n), in_specs=[scalar] * 2...  11.2 us
    ppermute x3, waiting for transfers between devices, spread_x(): others = [lax.ppermute(v, 'x', [(NX - 1, i)]) for i in range(NX - 1)]  7.76 us
  transfers between devices with their start and end apart: 28, of which 17 were waited for; matrix products, arithmetic and copies ran while one was open for 1% of the time, Pallas kernels for 15%

profile of v3, /device:TPU:1, one launch (start us, length us, event | category | flops | bytes accessed | tf_op | source)
XLA Modules:
  0.0 166.9 jit_solution(15483525968468698470)
XLA Ops:
  0.6 9.3 %term.2 = (f32[8,16,768]{2,1,0:T(8,128)}, f32[8,16,768]{2,1,0:T(8,128)}, f32[8,16,768]{2,1,0:T(8,128)}, f32[8,16,768]{2,1,0:T(8,128)}) custom-call(s32[1]{0:T(128)} %bitcast.3.z_ref, s32[1]{0:T(128)} %bitcast.1.y_ref, f32[4,512,512]{2,1,0:T(8,128)} %bitcast.32, f32[4,512,1536]{2,1,0:T(8,128)} %bitcast.28, f32[4,512,1536]{2,1,0:T(8,128)} %bitcast.29), custom_call_target="tpu_custom_call" | custom-call | flops 4831838208 | bytes 12582912 | tf_op jit(solution)/shard_map/term/pallas_call | solution.py:59
  10.0 2.1 %collective-permute-start = (f32[8,16,768]{2,1,0:T(8,128)}, f32[8,16,768]{2,1,0:T(8,128)S(1)}, u32[]{:S(2)}, u32[]{:S(2)}) collective-permute-start(f32[8,16,768]{2,1,0:T(8,128)} %get-tuple-element.18), channel_id=1, source_target_pairs={{0,8},{8,0},{16,24},{24,16},{1,9},{9,1},{17,25},{25,17},{2,10},{10... | collective-permute-start | bytes 1179656 | tf_op jit(solution)/shard_map/ppermute | solution.py:191
  12.1 2.6 %collective-permute-start.1 = (f32[8,16,768]{2,1,0:T(8,128)}, f32[8,16,768]{2,1,0:T(8,128)S(1)}, u32[]{:S(2)}, u32[]{:S(2)}) collective-permute-start(f32[8,16,768]{2,1,0:T(8,128)} %get-tuple-element.19), channel_id=1, source_target_pairs={{0,16},{8,24},{16,0},{24,8},{1,17},{9,25},{17,1},{25,9},{2,18},{10... | collective-permute-start | bytes 1179656 | tf_op jit(solution)/shard_map/ppermute | solution.py:191
  14.7 9.4 %term.3 = (f32[8,16,768]{2,1,0:T(8,128)}, f32[8,16,768]{2,1,0:T(8,128)}, f32[8,16,768]{2,1,0:T(8,128)}, f32[8,16,768]{2,1,0:T(8,128)}) custom-call(s32[1]{0:T(128)} %bitcast.3.z_ref, s32[1]{0:T(128)} %bitcast.1.y_ref, f32[4,512,512]{2,1,0:T(8,128)} %bitcast.33, f32[4,512,1536]{2,1,0:T(8,128)} %bitcast.30, f32[4,512,1536]{2,1,0:T(8,128)} %bitcast.31), custom_call_target="tpu_custom_call" | custom-call | flops 4831838208 | bytes 12582912 | tf_op jit(solution)/shard_map/term/pallas_call | solution.py:59
  24.1 3.8 %collective-permute-start.7 = (f32[8,16,768]{2,1,0:T(8,128)}, f32[8,16,768]{2,1,0:T(8,128)S(1)}, u32[]{:S(2)}, u32[]{:S(2)}) collective-permute-start(f32[8,16,768]{2,1,0:T(8,128)} %get-tuple-element.25), channel_id=1, source_target_pairs={{0,16},{8,24},{16,0},{24,8},{1,17},{9,25},{17,1},{25,9},{2,18},{10... | collective-permute-start | bytes 1179656 | tf_op jit(solution)/shard_map/ppermute | solution.py:191
  28.0 3.9 %collective-permute-done.1 = f32[8,16,768]{2,1,0:T(8,128)S(1)} collective-permute-done((f32[8,16,768]{2,1,0:T(8,128)}, f32[8,16,768]{2,1,0:T(8,128)S(1)}, u32[]{:S(2)}, u32[]{:S(2)}) %collective-permute-start.1) | collective-permute-done | bytes 393248 | tf_op jit(solution)/shard_map/ppermute | solution.py:191
  31.9 1.7 %collective-permute-done.2 = f32[8,16,768]{2,1,0:T(8,128)S(1)} collective-permute-done((f32[8,16,768]{2,1,0:T(8,128)}, f32[8,16,768]{2,1,0:T(8,128)S(1)}, u32[]{:S(2)}, u32[]{:S(2)}) %collective-permute-start.2) | collective-permute-done | bytes 393248 | tf_op jit(solution)/shard_map/ppermute | solution.py:191
  33.8 1.7 %collective-permute-start.3 = (f32[4,16,768]{2,1,0:T(8,128)S(1)}, f32[4,16,768]{2,1,0:T(8,128)S(1)}, u32[]{:S(2)}, u32[]{:S(2)}) collective-permute-start(f32[4,16,768]{2,1,0:T(8,128)S(1)} %slice.143), channel_id=1, source_target_pairs={{0,32},{32,0},{64,96},{96,64},{128,160},{160,128},{192,224},{224,1... | collective-permute-start | bytes 589832 | tf_op jit(solution)/shard_map/ppermute | solution.py:191
  35.5 3.3 %collective-permute-done.3 = f32[4,16,768]{2,1,0:T(8,128)S(1)} collective-permute-done((f32[4,16,768]{2,1,0:T(8,128)S(1)}, f32[4,16,768]{2,1,0:T(8,128)S(1)}, u32[]{:S(2)}, u32[]{:S(2)}) %collective-permute-start.3) | collective-permute-done | bytes 196640 | tf_op jit(solution)/shard_map/ppermute | solution.py:191
  38.9 3.1 %collective-permute-start.4 = (f32[2,16,768]{2,1,0:T(8,128)S(1)}, f32[2,16,768]{2,1,0:T(8,128)S(1)}, u32[]{:S(2)}, u32[]{:S(2)}) collective-permute-start(f32[2,16,768]{2,1,0:T(8,128)S(1)} %slice.145), channel_id=1, source_target_pairs={{0,64},{32,96},{64,0},{96,32},{128,192},{160,224},{192,128},{224,1... | collective-permute-start | bytes 294920 | tf_op jit(solution)/shard_map/ppermute | solution.py:191
  42.0 6.9 %collective-permute-done.7 = f32[8,16,768]{2,1,0:T(8,128)S(1)} collective-permute-done((f32[8,16,768]{2,1,0:T(8,128)}, f32[8,16,768]{2,1,0:T(8,128)S(1)}, u32[]{:S(2)}, u32[]{:S(2)}) %collective-permute-start.7) | collective-permute-done | bytes 393248 | tf_op jit(solution)/shard_map/ppermute | solution.py:191
  48.8 2.0 %collective-permute-done.8 = f32[8,16,768]{2,1,0:T(8,128)S(1)} collective-permute-done((f32[8,16,768]{2,1,0:T(8,128)}, f32[8,16,768]{2,1,0:T(8,128)S(1)}, u32[]{:S(2)}, u32[]{:S(2)}) %collective-permute-start.8) | collective-permute-done | bytes 393248 | tf_op jit(solution)/shard_map/ppermute | solution.py:191
  50.8 1.1 add_add_fusion
  51.9 5.7 %collective-permute-start.9 = (f32[4,16,768]{2,1,0:T(8,128)S(1)}, f32[4,16,768]{2,1,0:T(8,128)S(1)}, u32[]{:S(2)}, u32[]{:S(2)}) collective-permute-start(f32[4,16,768]{2,1,0:T(8,128)S(1)} %slice.150), channel_id=1, source_target_pairs={{0,224},{32,64},{64,32},{96,128},{128,96},{160,192},{192,160},{224... | collective-permute-start | bytes 589832 | tf_op jit(solution)/shard_map/ppermute | solution.py:191
  57.6 1.5 collective-permute-start.5
  59.0 2.6 %collective-permute-done.9 = f32[4,16,768]{2,1,0:T(8,128)S(1)} collective-permute-done((f32[4,16,768]{2,1,0:T(8,128)S(1)}, f32[4,16,768]{2,1,0:T(8,128)S(1)}, u32[]{:S(2)}, u32[]{:S(2)}) %collective-permute-start.9) | collective-permute-done | bytes 196640 | tf_op jit(solution)/shard_map/ppermute | solution.py:191
  61.8 2.8 %collective-permute-done.5 = f32[1,16,768]{2,1,0:T(8,128)S(1)} collective-permute-done((f32[1,16,768]{2,1,0:T(8,128)S(1)}, f32[1,16,768]{2,1,0:T(8,128)S(1)}, u32[]{:S(2)}, u32[]{:S(2)}) %collective-permute-start.5) | collective-permute-done | bytes 49184 | tf_op jit(solution)/shard_map/ppermute | solution.py:191
  64.6 2.0 %collective-permute-done.10 = f32[2,16,768]{2,1,0:T(8,128)S(1)} collective-permute-done((f32[2,16,768]{2,1,0:T(8,128)S(1)}, f32[2,16,768]{2,1,0:T(8,128)S(1)}, u32[]{:S(2)}, u32[]{:S(2)}) %collective-permute-start.10) | collective-permute-done | bytes 98336 | tf_op jit(solution)/shard_map/ppermute | solution.py:191
  66.7 3.7 %collective-permute-start.11 = (f32[1,16,768]{2,1,0:T(8,128)S(1)}, f32[1,16,768]{2,1,0:T(8,128)S(1)}, u32[]{:S(2)}, u32[]{:S(2)}) collective-permute-start(f32[1,16,768]{2,1,0:T(8,128)S(1)} %slice.154), channel_id=1, source_target_pairs={{0,128},{32,160},{64,192},{96,224},{128,0},{160,32},{192,64},{224,... | collective-permute-start | bytes 147464 | tf_op jit(solution)/shard_map/ppermute | solution.py:191
  70.4 4.5 %collective-permute-done.11 = f32[1,16,768]{2,1,0:T(8,128)S(1)} collective-permute-done((f32[1,16,768]{2,1,0:T(8,128)S(1)}, f32[1,16,768]{2,1,0:T(8,128)S(1)}, u32[]{:S(2)}, u32[]{:S(2)}) %collective-permute-start.11) | collective-permute-done | bytes 49184 | tf_op jit(solution)/shard_map/ppermute | solution.py:191
  75.0 4.4 %collective-permute-start.12 = (f32[16,1024]{1,0:T(8,128)S(1)}, f32[16,1024]{1,0:T(8,128)S(1)}, u32[]{:S(2)}, u32[]{:S(2)}) collective-permute-start(f32[16,1024]{1,0:T(8,128)S(1)} %pad_maximum_fusion.2), channel_id=1, source_target_pairs={{0,1},{1,0},{2,3},{3,2},{4,5},{5,4},{6,7},{7,6},{8,9},{9,8},{10,11... | collective-permute-start | bytes 196616 | tf_op jit(solution)/shard_map/ppermute | solution.py:191
  79.4 0.9 collective-permute-done.12
  80.3 0.7 collective-permute-start.15
  81.0 0.7 collective-permute-start.14
  81.7 1.3 collective-permute-start.13
  83.0 7.8 %collective-permute-done.13 = f32[16,1792]{1,0:T(8,128)S(1)} collective-permute-done((f32[16,1792]{1,0:T(8,128)S(1)}, f32[16,1792]{1,0:T(8,128)S(1)}, u32[]{:S(2)}, u32[]{:S(2)}) %collective-permute-start.13) | collective-permute-done | bytes 114720 | tf_op jit(solution)/shard_map/ppermute | solution.py:217
  90.8 0.9 broadcast_in_dim.9
  91.7 6.9 %all-to-all-start = ((f32[8,16,1280]{2,1,0:T(8,128)}), f32[8,16,1280]{2,1,0:T(8,128)S(1)}, u32[]{:S(2)}, u32[]{:S(2)}) async-start(f32[8,16,1280]{2,1,0:T(8,128)} %broadcast_in_dim.9), calls=%async_computation | async-start | bytes 1310720 | tf_op jit(solution)/shard_map/all_to_all | solution.py:222
  98.8 0.6 collective-permute-start.16
  99.3 2.7 %collective-permute-start.18 = (f32[16,512]{1,0:T(8,128)S(1)}, f32[16,512]{1,0:T(8,128)S(1)}, u32[]{:S(2)}, u32[]{:S(2)}) collective-permute-start(f32[16,512]{1,0:T(8,128)S(1)} %get-tuple-element.38), channel_id=1, source_target_pairs={{0,24},{8,16},{16,8},{24,0},{1,25},{9,17},{17,9},{25,1},{2,26},{10... | collective-permute-start | bytes 98312 | tf_op jit(solution)/shard_map/ppermute | solution.py:191
  102.0 1.0 collective-permute-done.17
  103.0 0.3 collective-permute-done.18
  103.4 15.2 %all-to-all-done.refs_1_.refs_0_.refs_5_ = f32[8,16,1280]{2,1,0:T(8,128)S(1)} async-done(((f32[8,16,1280]{2,1,0:T(8,128)}), f32[8,16,1280]{2,1,0:T(8,128)S(1)}, u32[]{:S(2)}, u32[]{:S(2)}) %all-to-all-start) | async-done | bytes 655392 | tf_op jit(solution)/shard_map/all_to_all | solution.py:222
  118.6 1.5 collective-permute-start.19
  120.1 1.1 broadcast_in_dim.10
  121.2 4.2 %all-to-all-start.1 = ((f32[8,4,16,512]{3,2,1,0:T(8,128)}), f32[8,4,16,512]{3,2,1,0:T(8,128)}, u32[]{:S(2)}, u32[]{:S(2)}) async-start(f32[8,4,16,512]{3,2,1,0:T(8,128)} %broadcast_in_dim.10), calls=%async_computation.1 | async-start | bytes 2097152 | tf_op jit(solution)/shard_map/all_to_all | solution.py:222
  125.4 8.2 %collective-permute-done.20.refs_3_.refs_2_.refs_7_ = f32[8,16,1280]{2,1,0:T(8,128)S(1)} collective-permute-done((f32[8,16,1280]{2,1,0:T(8,128)S(1)}, f32[8,16,1280]{2,1,0:T(8,128)S(1)}, u32[]{:S(2)}, u32[]{:S(2)}) %collective-permute-start.20) | collective-permute-done | bytes 655392 | tf_op jit(solution)/shard_map/ppermute | solution.py:231
  133.6 1.2 collective-permute-start.22
  134.8 0.4 collective-permute-start.21
  135.3 7.6 %collective-permute-done.21.refs_4_.refs_3_.refs_8_ = f32[4,16,1280]{2,1,0:T(8,128)S(1)} collective-permute-done((f32[4,16,1280]{2,1,0:T(8,128)S(1)}, f32[4,16,1280]{2,1,0:T(8,128)S(1)}, u32[]{:S(2)}, u32[]{:S(2)}) %collective-permute-start.21) | collective-permute-done | bytes 327712 | tf_op jit(solution)/shard_map/ppermute | solution.py:231
  143.0 3.4 %collective-permute-start.23 = (f32[4,8,16,256]{3,2,1,0:T(8,128)S(1)}, f32[4,8,16,256]{3,2,1,0:T(8,128)S(1)}, u32[]{:S(2)}, u32[]{:S(2)}) collective-permute-start(f32[4,8,16,256]{3,2,1,0:T(8,128)S(1)} %bitcast.35), channel_id=1, source_target_pairs={{0,1},{1,0},{2,3},{3,2},{4,5},{5,4},{6,7},{7,6},{8,9},{9,8},{10,11... | collective-permute-start | bytes 1572872 | tf_op jit(solution)/shard_map/ppermute | solution.py:191
  146.4 1.5 collective-permute-done.23.other_hbm
  148.0 0.8 copy-done.8
  148.7 5.9 %solve.3.own = f32[2,512,512]{2,1,0:T(8,128)} custom-call(s32[1]{0:T(128)} %bitcast.1.y_ref, s32[1]{0:T(128)} %bitcast.core_ref, f32[2,512,512]{2,1,0:T(8,128)} %inv_hbm.3, f32[4,8,16,256]{3,2,1,0:T(8,128)} %copy-done.8, f32[8,16,1280]{2,1,0:T(8,128)} %copy-done.3, f32[8,16,1280]{2,1,0:T(8,128)} %copy-done.5, f32[8,16,1280]{2,1,0:T(8,128)} %copy-done.4, ...), custom_call_target="tpu_custom_call" | custom-call | flops 2415919104 | bytes 6291456 | tf_op jit(solution)/shard_map/solve/pallas_call | solution.py:127
  154.6 0.5 collective-permute-start.25
  155.1 5.3 %solve.2.own = f32[2,512,256]{2,1,0:T(8,128)} custom-call(s32[1]{0:T(128)} %bitcast.1.y_ref, s32[1]{0:T(128)} %bitcast.core_ref, f32[2,512,512]{2,1,0:T(8,128)} %inv_hbm.3, f32[4,8,16,256]{3,2,1,0:T(8,128)} %copy-done.8, f32[8,4,16,512]{3,2,1,0:T(8,128)} %all-to-all-done.1.refs_0_, f32[8,16,1280]{2,1,0:T(8,128)} %copy-done.3, f32[8,16,1280]{2,1,0:T(8,128)} %copy-done.5, ...), custom_call_target="tpu_custom_call" | custom-call | flops 1207959552 | bytes 6291456 | tf_op jit(solution)/shard_map/solve/pallas_call | solution.py:127
  160.6 3.7 %finish.2 = (f32[2,512,1536]{2,1,0:T(8,128)}, f32[16,1536]{1,0:T(8,128)S(1)}) custom-call(s32[1]{0:T(128)} %bitcast.core_ref, f32[2,512,512]{2,1,0:T(8,128)S(1)} %copy-done, f32[2,512,512]{2,1,0:T(8,128)} %collective-permute-done.25.other, f32[16,1536]{1,0:T(8,128)S(1)} %pad_maximum_fusion.1.base, f32[2,16,512]{2,1,0:T(8,128)S(1)} %bitcast.26), custom_call_target="tpu_custom_call" | custom-call | flops 100663296 | bytes 6291456 | tf_op jit(solution)/shard_map/finish/pallas_call | solution.py:171
  164.4 2.4 %finish.3 = (f32[2,512,1536]{2,1,0:T(8,128)}, f32[16,1536]{1,0:T(8,128)}) custom-call(s32[1]{0:T(128)} %bitcast.core_ref, f32[2,512,256]{2,1,0:T(8,128)S(1)} %copy-done.1, f32[2,512,256]{2,1,0:T(8,128)S(1)} %collective-permute-done.24.other, f32[16,1536]{1,0:T(8,128)S(1)} %pad_maximum_fusion.1.base, ...), custom_call_target="tpu_custom_call", output_to_operand_aliasing={{0}: (5, {})} | custom-call | flops 50331648 | bytes 6291456 | tf_op jit(solution)/shard_map/finish/pallas_call | solution.py:171
  (79 shorter events, 0.9 us)
Async XLA Ops:
  10.0 18.0 %collective-permute-start = (f32[8,16,768]{2,1,0:T(8,128)}, f32[8,16,768]{2,1,0:T(8,128)S(1)}, u32[]{:S(2)}, u32[]{:S(2)}) collective-permute-start(f32[8,16,768]{2,1,0:T(8,128)} %get-tuple-element.18), channel_id=1, source_target_pairs={{0,8},{8,0},{16,24},{24,16},{1,9},{9,1},{17,25},{25,17},{2,10},{10... | collective-permute-start | bytes 1179656 | tf_op jit(solution)/shard_map/ppermute | solution.py:191
  12.1 19.8 %collective-permute-start.1 = (f32[8,16,768]{2,1,0:T(8,128)}, f32[8,16,768]{2,1,0:T(8,128)S(1)}, u32[]{:S(2)}, u32[]{:S(2)}) collective-permute-start(f32[8,16,768]{2,1,0:T(8,128)} %get-tuple-element.19), channel_id=1, source_target_pairs={{0,16},{8,24},{16,0},{24,8},{1,17},{9,25},{17,1},{25,9},{2,18},{10... | collective-permute-start | bytes 1179656 | tf_op jit(solution)/shard_map/ppermute | solution.py:191
  14.7 18.9 %collective-permute-start.2 = (f32[8,16,768]{2,1,0:T(8,128)}, f32[8,16,768]{2,1,0:T(8,128)S(1)}, u32[]{:S(2)}, u32[]{:S(2)}) collective-permute-start(f32[8,16,768]{2,1,0:T(8,128)} %get-tuple-element.20), channel_id=1, source_target_pairs={{0,24},{8,16},{16,8},{24,0},{1,25},{9,17},{17,9},{25,1},{2,26},{10... | collective-permute-start | bytes 1179656 | tf_op jit(solution)/shard_map/ppermute | solution.py:191
  14.7 18.9 %copy-start.11 = (f32[8,16,768]{2,1,0:T(8,128)S(1)}, f32[8,16,768]{2,1,0:T(8,128)}, u32[]{:S(2)}) copy-start(f32[8,16,768]{2,1,0:T(8,128)} %get-tuple-element.17) | copy-start | bytes 1179652
  14.7 20.8 %copy-start.2 = (f32[1,1,2,16,512]{4,3,2,1,0:T(8,128)S(1)}, f32[1,1,2,16,512]{4,3,2,1,0:T(8,128)}, u32[]{:S(2)}) copy-start(f32[1,1,2,16,512]{4,3,2,1,0:T(8,128)} %param.8) | copy-start | bytes 196612
  24.1 50.8 %copy-start.12 = (f32[1,1,16,1536]{3,2,1,0:T(8,128)S(1)}, f32[1,1,16,1536]{3,2,1,0:T(8,128)}, u32[]{:S(2)}) copy-start(f32[1,1,16,1536]{3,2,1,0:T(8,128)} %param.7) | copy-start | bytes 294916
  24.1 17.8 %collective-permute-start.6 = (f32[8,16,768]{2,1,0:T(8,128)}, f32[8,16,768]{2,1,0:T(8,128)S(1)}, u32[]{:S(2)}, u32[]{:S(2)}) collective-permute-start(f32[8,16,768]{2,1,0:T(8,128)} %get-tuple-element.24), channel_id=1, source_target_pairs={{0,8},{8,0},{16,24},{24,16},{1,9},{9,1},{17,25},{25,17},{2,10},{10... | collective-permute-start | bytes 1179656 | tf_op jit(solution)/shard_map/ppermute | solution.py:191
  24.1 24.7 %collective-permute-start.7 = (f32[8,16,768]{2,1,0:T(8,128)}, f32[8,16,768]{2,1,0:T(8,128)S(1)}, u32[]{:S(2)}, u32[]{:S(2)}) collective-permute-start(f32[8,16,768]{2,1,0:T(8,128)} %get-tuple-element.25), channel_id=1, source_target_pairs={{0,16},{8,24},{16,0},{24,8},{1,17},{9,25},{17,1},{25,9},{2,18},{10... | collective-permute-start | bytes 1179656 | tf_op jit(solution)/shard_map/ppermute | solution.py:191
  28.0 22.8 %collective-permute-start.8 = (f32[8,16,768]{2,1,0:T(8,128)}, f32[8,16,768]{2,1,0:T(8,128)S(1)}, u32[]{:S(2)}, u32[]{:S(2)}) collective-permute-start(f32[8,16,768]{2,1,0:T(8,128)} %get-tuple-element.26), channel_id=1, source_target_pairs={{0,24},{8,16},{16,8},{24,0},{1,25},{9,17},{17,9},{25,1},{2,26},{10... | collective-permute-start | bytes 1179656 | tf_op jit(solution)/shard_map/ppermute | solution.py:191
  33.8 5.1 %collective-permute-start.3 = (f32[4,16,768]{2,1,0:T(8,128)S(1)}, f32[4,16,768]{2,1,0:T(8,128)S(1)}, u32[]{:S(2)}, u32[]{:S(2)}) collective-permute-start(f32[4,16,768]{2,1,0:T(8,128)S(1)} %slice.143), channel_id=1, source_target_pairs={{0,32},{32,0},{64,96},{96,64},{128,160},{160,128},{192,224},{224,1... | collective-permute-start | bytes 589832 | tf_op jit(solution)/shard_map/ppermute | solution.py:191
  38.9 18.7 %collective-permute-start.4 = (f32[2,16,768]{2,1,0:T(8,128)S(1)}, f32[2,16,768]{2,1,0:T(8,128)S(1)}, u32[]{:S(2)}, u32[]{:S(2)}) collective-permute-start(f32[2,16,768]{2,1,0:T(8,128)S(1)} %slice.145), channel_id=1, source_target_pairs={{0,64},{32,96},{64,0},{96,32},{128,192},{160,224},{192,128},{224,1... | collective-permute-start | bytes 294920 | tf_op jit(solution)/shard_map/ppermute | solution.py:191
  51.9 9.8 %collective-permute-start.9 = (f32[4,16,768]{2,1,0:T(8,128)S(1)}, f32[4,16,768]{2,1,0:T(8,128)S(1)}, u32[]{:S(2)}, u32[]{:S(2)}) collective-permute-start(f32[4,16,768]{2,1,0:T(8,128)S(1)} %slice.150), channel_id=1, source_target_pairs={{0,224},{32,64},{64,32},{96,128},{128,96},{160,192},{192,160},{224... | collective-permute-start | bytes 589832 | tf_op jit(solution)/shard_map/ppermute | solution.py:191
  57.6 7.0 %collective-permute-start.5 = (f32[1,16,768]{2,1,0:T(8,128)S(1)}, f32[1,16,768]{2,1,0:T(8,128)S(1)}, u32[]{:S(2)}, u32[]{:S(2)}) collective-permute-start(f32[1,16,768]{2,1,0:T(8,128)S(1)} %slice.147), channel_id=1, source_target_pairs={{0,128},{32,160},{64,192},{96,224},{128,0},{160,32},{192,64},{224,... | collective-permute-start | bytes 147464 | tf_op jit(solution)/shard_map/ppermute | solution.py:191
  61.7 4.9 %collective-permute-start.10 = (f32[2,16,768]{2,1,0:T(8,128)S(1)}, f32[2,16,768]{2,1,0:T(8,128)S(1)}, u32[]{:S(2)}, u32[]{:S(2)}) collective-permute-start(f32[2,16,768]{2,1,0:T(8,128)S(1)} %slice.152), channel_id=1, source_target_pairs={{0,64},{32,224},{64,0},{96,160},{128,192},{160,96},{192,128},{224,... | collective-permute-start | bytes 294920 | tf_op jit(solution)/shard_map/ppermute | solution.py:191
  66.7 8.2 %collective-permute-start.11 = (f32[1,16,768]{2,1,0:T(8,128)S(1)}, f32[1,16,768]{2,1,0:T(8,128)S(1)}, u32[]{:S(2)}, u32[]{:S(2)}) collective-permute-start(f32[1,16,768]{2,1,0:T(8,128)S(1)} %slice.154), channel_id=1, source_target_pairs={{0,128},{32,160},{64,192},{96,224},{128,0},{160,32},{192,64},{224,... | collective-permute-start | bytes 147464 | tf_op jit(solution)/shard_map/ppermute | solution.py:191
  75.0 16.8 %copy-start.9 = (f32[16,768]{1,0:T(8,128)}, f32[16,768]{1,0:T(8,128)S(1)}, u32[]{:S(2)}) copy-start(f32[16,768]{1,0:T(8,128)S(1)} %get-tuple-element.34) | copy-start | bytes 147460
  75.0 5.3 %collective-permute-start.12 = (f32[16,1024]{1,0:T(8,128)S(1)}, f32[16,1024]{1,0:T(8,128)S(1)}, u32[]{:S(2)}, u32[]{:S(2)}) collective-permute-start(f32[16,1024]{1,0:T(8,128)S(1)} %pad_maximum_fusion.2), channel_id=1, source_target_pairs={{0,1},{1,0},{2,3},{3,2},{4,5},{5,4},{6,7},{7,6},{8,9},{9,8},{10,11... | collective-permute-start | bytes 196616 | tf_op jit(solution)/shard_map/ppermute | solution.py:191
  80.3 2.7 %collective-permute-start.15 = (f32[16,1792]{1,0:T(8,128)S(1)}, f32[16,1792]{1,0:T(8,128)S(1)}, u32[]{:S(2)}, u32[]{:S(2)}) collective-permute-start(f32[16,1792]{1,0:T(8,128)S(1)} %constant_dynamic-update-slice_fusion), channel_id=1, source_target_pairs={{6,4},{7,5},{14,12},{15,13},{22,20},{23,21},{30,28},{31,29},{38,36... | collective-permute-start | bytes 344072 | tf_op jit(solution)/shard_map/ppermute | solution.py:217
  81.0 2.0 %collective-permute-start.14 = (f32[16,1792]{1,0:T(8,128)S(1)}, f32[16,1792]{1,0:T(8,128)S(1)}, u32[]{:S(2)}, u32[]{:S(2)}) collective-permute-start(f32[16,1792]{1,0:T(8,128)S(1)} %constant_dynamic-update-slice_fusion), channel_id=1, source_target_pairs={{6,2},{7,3},{14,10},{15,11},{22,18},{23,19},{30,26},{31,27},{38,34... | collective-permute-start | bytes 344072 | tf_op jit(solution)/shard_map/ppermute | solution.py:217
  81.7 9.1 %collective-permute-start.13 = (f32[16,1792]{1,0:T(8,128)S(1)}, f32[16,1792]{1,0:T(8,128)S(1)}, u32[]{:S(2)}, u32[]{:S(2)}) collective-permute-start(f32[16,1792]{1,0:T(8,128)S(1)} %constant_dynamic-update-slice_fusion), channel_id=1, source_target_pairs={{6,0},{7,1},{14,8},{15,9},{22,16},{23,17},{30,24},{31,25},{38,32},... | collective-permute-start | bytes 344072 | tf_op jit(solution)/shard_map/ppermute | solution.py:217
  91.7 26.9 %all-to-all-start = ((f32[8,16,1280]{2,1,0:T(8,128)}), f32[8,16,1280]{2,1,0:T(8,128)S(1)}, u32[]{:S(2)}, u32[]{:S(2)}) async-start(f32[8,16,1280]{2,1,0:T(8,128)} %broadcast_in_dim.9), calls=%async_computation | async-start | bytes 1310720 | tf_op jit(solution)/shard_map/all_to_all | solution.py:222
  98.7 4.4 %collective-permute-start.17 = (f32[16,512]{1,0:T(8,128)S(1)}, f32[16,512]{1,0:T(8,128)S(1)}, u32[]{:S(2)}, u32[]{:S(2)}) collective-permute-start(f32[16,512]{1,0:T(8,128)S(1)} %get-tuple-element.38), channel_id=1, source_target_pairs={{0,16},{8,24},{16,0},{24,8},{1,17},{9,25},{17,1},{25,9},{2,18},{10... | collective-permute-start | bytes 98312 | tf_op jit(solution)/shard_map/ppermute | solution.py:191
  98.8 4.3 %collective-permute-start.16 = (f32[16,512]{1,0:T(8,128)S(1)}, f32[16,512]{1,0:T(8,128)S(1)}, u32[]{:S(2)}, u32[]{:S(2)}) collective-permute-start(f32[16,512]{1,0:T(8,128)S(1)} %get-tuple-element.38), channel_id=1, source_target_pairs={{0,8},{8,0},{16,24},{24,16},{1,9},{9,1},{17,25},{25,17},{2,10},{10... | collective-permute-start | bytes 98312 | tf_op jit(solution)/shard_map/ppermute | solution.py:191
  99.3 4.0 %collective-permute-start.18 = (f32[16,512]{1,0:T(8,128)S(1)}, f32[16,512]{1,0:T(8,128)S(1)}, u32[]{:S(2)}, u32[]{:S(2)}) collective-permute-start(f32[16,512]{1,0:T(8,128)S(1)} %get-tuple-element.38), channel_id=1, source_target_pairs={{0,24},{8,16},{16,8},{24,0},{1,25},{9,17},{17,9},{25,1},{2,26},{10... | collective-permute-start | bytes 98312 | tf_op jit(solution)/shard_map/ppermute | solution.py:191
  118.6 29.3 %copy-start.3 = (f32[8,16,1280]{2,1,0:T(8,128)}, f32[8,16,1280]{2,1,0:T(8,128)S(1)}, u32[]{:S(2)}) copy-start(f32[8,16,1280]{2,1,0:T(8,128)S(1)} %all-to-all-done.refs_1_.refs_0_.refs_5_) | copy-start | bytes 1966084
  118.6 15.0 %collective-permute-start.20 = (f32[8,16,1280]{2,1,0:T(8,128)S(1)}, f32[8,16,1280]{2,1,0:T(8,128)S(1)}, u32[]{:S(2)}, u32[]{:S(2)}) collective-permute-start(f32[8,16,1280]{2,1,0:T(8,128)S(1)} %all-to-all-done.refs_1_.refs_0_.refs_5_), channel_id=1, source_target_pairs={{0,24},{8,0},{16,8},{24,16},{1,25},{9,1},{17,9},{25,17},{2,26},{10... | collective-permute-start | bytes 1966088 | tf_op jit(solution)/shard_map/ppermute | solution.py:231
  118.6 16.2 %collective-permute-start.19 = (f32[8,16,1280]{2,1,0:T(8,128)S(1)}, f32[8,16,1280]{2,1,0:T(8,128)S(1)}, u32[]{:S(2)}, u32[]{:S(2)}) collective-permute-start(f32[8,16,1280]{2,1,0:T(8,128)S(1)} %all-to-all-done.refs_1_.refs_0_.refs_5_), channel_id=1, source_target_pairs={{0,8},{8,16},{16,24},{24,0},{1,9},{9,17},{17,25},{25,1},{2,10},{10... | collective-permute-start | bytes 1966088 | tf_op jit(solution)/shard_map/ppermute | solution.py:231
  121.2 33.9 %all-to-all-start.1 = ((f32[8,4,16,512]{3,2,1,0:T(8,128)}), f32[8,4,16,512]{3,2,1,0:T(8,128)}, u32[]{:S(2)}, u32[]{:S(2)}) async-start(f32[8,4,16,512]{3,2,1,0:T(8,128)} %broadcast_in_dim.10), calls=%async_computation.1 | async-start | bytes 2097152 | tf_op jit(solution)/shard_map/all_to_all | solution.py:222
  133.6 14.3 %copy-start.4 = (f32[8,16,1280]{2,1,0:T(8,128)}, f32[8,16,1280]{2,1,0:T(8,128)S(1)}, u32[]{:S(2)}) copy-start(f32[8,16,1280]{2,1,0:T(8,128)S(1)} %collective-permute-done.20.refs_3_.refs_2_.refs_7_) | copy-start | bytes 1966084
  133.6 9.3 %collective-permute-start.22 = (f32[4,16,1280]{2,1,0:T(8,128)S(1)}, f32[4,16,1280]{2,1,0:T(8,128)S(1)}, u32[]{:S(2)}, u32[]{:S(2)}) collective-permute-start(f32[4,16,1280]{2,1,0:T(8,128)S(1)} %slice.173), channel_id=1, source_target_pairs={{0,24},{8,0},{16,8},{24,16},{1,25},{9,1},{17,9},{25,17},{2,26},{10... | collective-permute-start | bytes 983048 | tf_op jit(solution)/shard_map/ppermute | solution.py:231
  134.8 13.1 %copy-start.5 = (f32[8,16,1280]{2,1,0:T(8,128)}, f32[8,16,1280]{2,1,0:T(8,128)S(1)}, u32[]{:S(2)}) copy-start(f32[8,16,1280]{2,1,0:T(8,128)S(1)} %collective-permute-done.19.refs_2_.refs_1_.refs_6_) | copy-start | bytes 1966084
  134.8 8.1 %collective-permute-start.21 = (f32[4,16,1280]{2,1,0:T(8,128)S(1)}, f32[4,16,1280]{2,1,0:T(8,128)S(1)}, u32[]{:S(2)}, u32[]{:S(2)}) collective-permute-start(f32[4,16,1280]{2,1,0:T(8,128)S(1)} %slice.171), channel_id=1, source_target_pairs={{0,8},{8,16},{16,24},{24,0},{1,9},{9,17},{17,25},{25,1},{2,10},{10... | collective-permute-start | bytes 983048 | tf_op jit(solution)/shard_map/ppermute | solution.py:231
  142.9 5.0 %copy-start.7 = (f32[4,16,1280]{2,1,0:T(8,128)}, f32[4,16,1280]{2,1,0:T(8,128)S(1)}, u32[]{:S(2)}) copy-start(f32[4,16,1280]{2,1,0:T(8,128)S(1)} %collective-permute-done.21.refs_4_.refs_3_.refs_8_) | copy-start | bytes 983044
  142.9 5.0 %copy-start.6 = (f32[4,16,1280]{2,1,0:T(8,128)}, f32[4,16,1280]{2,1,0:T(8,128)S(1)}, u32[]{:S(2)}) copy-start(f32[4,16,1280]{2,1,0:T(8,128)S(1)} %collective-permute-done.22.refs_5_.refs_4_.refs_9_) | copy-start | bytes 983044
  143.0 5.0 %collective-permute-start.23 = (f32[4,8,16,256]{3,2,1,0:T(8,128)S(1)}, f32[4,8,16,256]{3,2,1,0:T(8,128)S(1)}, u32[]{:S(2)}, u32[]{:S(2)}) collective-permute-start(f32[4,8,16,256]{3,2,1,0:T(8,128)S(1)} %bitcast.35), channel_id=1, source_target_pairs={{0,1},{1,0},{2,3},{3,2},{4,5},{5,4},{6,7},{7,6},{8,9},{9,8},{10,11... | collective-permute-start | bytes 1572872 | tf_op jit(solution)/shard_map/ppermute | solution.py:191
  147.9 0.8 copy-start.8
  154.6 6.0 %copy-start.10 = (f32[16,768]{1,0:T(8,128)S(1)}, f32[16,768]{1,0:T(8,128)}, u32[]{:S(2)}) copy-start(f32[16,768]{1,0:T(8,128)} %copy-done.9) | copy-start | bytes 147460
  154.6 6.0 %copy-start = (f32[2,512,512]{2,1,0:T(8,128)S(1)}, f32[2,512,512]{2,1,0:T(8,128)}, u32[]{:S(2)}) copy-start(f32[2,512,512]{2,1,0:T(8,128)} %solve.3.own) | copy-start | bytes 6291460
  154.6 6.0 %collective-permute-start.25 = (f32[2,512,512]{2,1,0:T(8,128)}, f32[2,512,512]{2,1,0:T(8,128)}, u32[]{:S(2)}, u32[]{:S(2)}) collective-permute-start(f32[2,512,512]{2,1,0:T(8,128)} %solve.3.own), channel_id=1, source_target_pairs={{0,1},{1,0},{2,3},{3,2},{4,5},{5,4},{6,7},{7,6},{8,9},{9,8},{10,11... | collective-permute-start | bytes 6291464 | tf_op jit(solution)/shard_map/ppermute | solution.py:191
  160.4 4.0 %copy-start.1 = (f32[2,512,256]{2,1,0:T(8,128)S(1)}, f32[2,512,256]{2,1,0:T(8,128)}, u32[]{:S(2)}) copy-start(f32[2,512,256]{2,1,0:T(8,128)} %solve.2.own) | copy-start | bytes 3145732
  160.4 3.9 %collective-permute-start.24 = (f32[2,512,256]{2,1,0:T(8,128)}, f32[2,512,256]{2,1,0:T(8,128)S(1)}, u32[]{:S(2)}, u32[]{:S(2)}) collective-permute-start(f32[2,512,256]{2,1,0:T(8,128)} %solve.2.own), channel_id=1, source_target_pairs={{0,1},{1,0},{2,3},{3,2},{4,5},{5,4},{6,7},{7,6},{8,9},{9,8},{10,11... | collective-permute-start | bytes 3145736 | tf_op jit(solution)/shard_map/ppermute | solution.py:191

commit v4 on v3

--- a/solution.py
+++ b/solution.py
@@ -11,9 +11,9 @@
 NZ, NY, NX, NCORE = 8, 4, 4, 2
 SLAB = 16
 HALF = 768
-PART = 384
 BITREV = (0, 4, 2, 6, 1, 5, 3, 7)
 SHIFTS = (0, 1)
+STRIP = 256
 CUT = 512
 BOUNDS = ((0, CUT), (CUT, HALF))
 PLACES = ((0, 0, 8), (3, 0, 8), (1, 0, 8), (2, 0, 4), (2, 4, 4))
@@ -31,10 +31,14 @@
     return mul(ah, bh) + (mul(ah, bl) + mul(al, bh))
 
 
-def term_kernel(shift, z_ref, y_ref, c_ref, ea_ref, eb_ref, *refs):
-    outs, acc = refs[:NY], refs[NY]
+def width(part):
+    return BOUNDS[part][1] - BOUNDS[part][0]
+
+
+def term_kernel(part, z_ref, y_ref, c_ref, *refs):
+    strips, outs, acc = refs[: -NY - 1], refs[-NY - 1 : -1], refs[-1]
     k = pl.program_id(0)
-    product = dot3(c_ref[0], jnp.concatenate([ea_ref[0], eb_ref[0]], axis=1))
+    product = dot3(c_ref[0], jnp.concatenate([e[0] for e in strips], axis=1))
 
     @pl.when(k == 0)
     def _():
@@ -46,6 +50,7 @@
 
     @pl.when(k == pl.num_programs(0) - 1)
     def _():
+        shift = SHIFTS[part]
         label = (z_ref[0] + shift) % NZ
         for n, kz in enumerate(BITREV):
             z = ((label ^ kz) + NZ - shift) % NZ
@@ -54,28 +59,28 @@
                 o_ref[n] = acc[pl.ds(row, SLAB), :]
 
 
-def term(z, y, coupling, earlier, chunk):
-    out = pl.BlockSpec((NZ, SLAB, HALF), lambda k, z, y: (0, 0, 0))
+def term(z, y, coupling, earlier, part):
+    n = 2 * width(part)
+    at = BOUNDS[part][0] // STRIP
+    strips = [half * (HALF // STRIP) + at + i for half in (0, 1) for i in range(width(part) // STRIP)]
+    out = pl.BlockSpec((NZ, SLAB, n), lambda k, z, y: (0, 0, 0))
     return pl.pallas_call(
-        functools.partial(term_kernel, SHIFTS[chunk]),
+        functools.partial(term_kernel, part),
         grid_spec=pltpu.PrefetchScalarGridSpec(
             num_scalar_prefetch=2,
             grid=(4,),
-            in_specs=[
-                pl.BlockSpec((1, 512, 512), lambda k, z, y: (k, 0, 0)),
-                pl.BlockSpec((1, 512, PART), lambda k, z, y: (k, 0, chunk)),
-                pl.BlockSpec((1, 512, PART), lambda k, z, y: (k, 0, 2 + chunk)),
-            ],
+            in_specs=[pl.BlockSpec((1, 512, 512), lambda k, z, y: (k, 0, 0))]
+            + [pl.BlockSpec((1, 512, STRIP), lambda k, z, y, i=i: (k, 0, i)) for i in strips],
             out_specs=(out,) * NY,
-            scratch_shapes=[pltpu.VMEM((512, HALF), jnp.float32)],
-        ),
-        out_shape=(jax.ShapeDtypeStruct((NZ, SLAB, HALF), jnp.float32),) * NY,
+            scratch_shapes=[pltpu.VMEM((512, n), jnp.float32)],
+        ),
+        out_shape=(jax.ShapeDtypeStruct((NZ, SLAB, n), jnp.float32),) * NY,
         compiler_params=pltpu.CompilerParams(vmem_limit_bytes=56 * 2**20),
         cost_estimate=pl.CostEstimate(
-            flops=6 * 512 * 2048 * HALF, bytes_accessed=12 * 2**20, transcendentals=0
+            flops=6 * 512 * 2048 * n, bytes_accessed=2**22 + 2**13 * n, transcendentals=0
         ),
         name="term",
-    )(z, y, coupling, earlier, earlier)
+    )(z, y, coupling, *[earlier] * len(strips))
 
 
 def copy_in(source, target, sem):
@@ -155,7 +160,7 @@
     places = [(ref, pl.ds(pl.multiple_of(at, 128), last - first)) for ref, at in places]
     copies = [copy_in(ref, solved.at[:, :, at], sems.at[i]) for i, (ref, at) in enumerate(places)]
     for half in (0, 1):
-        pending[:, columns(chunk, half)] = base[:, columns(chunk, half)]
+        pending[:, columns(chunk, half)] = base[:, half * (last - first) : (half + 1) * (last - first)]
     for ref, at in places:
         update = dot3(panel[0], ref[0]) + dot3(panel[1], ref[1])
         pending[:, at] = pending[:, at] - update
@@ -250,23 +255,25 @@
     near_b = sum_y([after(slabs_b[0], near_a), *slabs_b[1:]])
     total_a = halve(halve(near_a, 2, SHIFTS[0]), 4, SHIFTS[0])[0]
     total_b = sum_z(near_b, SHIFTS[1])
-    base = [
-        right[:, half * HALF : (half + 1) * HALF]
-        - jnp.concatenate([t[:, half * PART : (half + 1) * PART] for t in (total_a, total_b)], axis=1)
-        for half in (0, 1)
-    ]
-
-    kept = jnp.where(is_first, base[0], base[1])
-    given = jnp.concatenate([jnp.where(is_first, base[1], base[0]), panel[0, :, 256:]], axis=1)
-    came = swap(given, "core", 1)
-    last = jnp.where(is_first, came[:, :HALF], kept)
-    other = jnp.where(is_first, kept, came[:, :HALF])
-    link = jnp.where(is_first, panel[0, :, :256], came[:, HALF:])
-    v = [last[:, :CUT], other[:, :CUT], link, last[:, CUT:], other[:, CUT:]]
-    v = spread_x(jnp.concatenate(v, axis=1))
-    split_at = 2 * CUT + 256
-    v_b = jnp.stack(gather_y(v[:, split_at:]))
-    pieces_a = gather_y_twice(after(gather_z(v[:, :split_at]), v_b))
+    def subtract(total, part):
+        return jnp.concatenate([right[:, columns(part, half)] for half in (0, 1)], axis=1) - total
+
+    def exchange(base, extra):
+        n = base.shape[1] // 2
+        kept = jnp.where(is_first, base[:, :n], base[:, n:])
+        given = jnp.where(is_first, base[:, n:], base[:, :n])
+        if extra is not None:
+            given = jnp.concatenate([given, extra[:, 256:]], axis=1)
+        came = swap(given, "core", 1)
+        v = [jnp.where(is_first, came[:, :n], kept), jnp.where(is_first, kept, came[:, :n])]
+        if extra is not None:
+            v.append(jnp.where(is_first, extra[:, :256], came[:, n:]))
+        return jnp.concatenate(v, axis=1)
+
+    base_a, base_b = subtract(total_a, 0), subtract(total_b, 1)
+    v_a = gather_z(spread_x(exchange(base_a, panel[0])))
+    v_b = jnp.stack(gather_y(spread_x(exchange(base_b, None))))
+    pieces_a = gather_y_twice(after(v_a, v_b))
     pieces_b = gather_z(v_b)
 
     part = jnp.concatenate([p[:, :, 2 * CUT :] for p in pieces_a]).reshape(NY, NZ, SLAB, 256)
@@ -275,9 +282,8 @@
     other_a = swap(own_a, "core", 1)
     own_b = solve(HALF - CUT, y_id, core_id, block_inverses, link, [pieces_b], pieces_a)
     other_b = swap(own_b, "core", 1)
-    base = jnp.concatenate(base, axis=1)
-    done_a = finish(0, core_id, own_a, other_a, base, panel)
-    solved, pending = finish(1, core_id, own_b, other_b, base, panel, *done_a)
+    done_a = finish(0, core_id, own_a, other_a, base_a, panel)
+    solved, pending = finish(1, core_id, own_b, other_b, base_b, panel, *done_a)
     return solved, pending[None, None]
 
 

time: 167 us -> 161 us (0.964)
  waiting for transfers between devices: 72.3 us -> 49.5 us
  starting transfers between devices: 53 us -> 68.4 us
    ppermute x19 -> x20, starting transfers between devices: 36.1 us -> 48.9 us  [swap(): lax.ppermute(x, axis, [(i, (((i + shift) % n ^ bit) - shift) % n) for i i...]
    all_to_all x2, waiting for transfers between devices: 15.2 us -> 3.47 us  [gather_z(): lax.all_to_all(jnp.broadcast_to(v, (NZ, *v.shape)), 'z', 0, 0, tiled=True)]
    ppermute x19 -> x20, waiting for transfers between devices: 33.6 us -> 26.5 us  [swap(): lax.ppermute(x, axis, [(i, (((i + shift) % n ^ bit) - shift) % n) for i i...]
    ppermute x3 -> x6, waiting for transfers between devices: 7.76 us -> 4.86 us  [spread_x(): others = [lax.ppermute(v, 'x', [(NX - 1, i)]) for i in range(NX - 1)]]
    ppermute x3 -> x6, starting transfers between devices: 2.63 us -> 5.24 us  [spread_x(): others = [lax.ppermute(v, 'x', [(NX - 1, i)]) for i in range(NX - 1)]]
  transfers between devices with their start and end apart: 28 -> 32, of which waited for: 17 -> 16; matrix products, arithmetic and copies ran while one was open for 1% -> 2% of each run, Pallas kernels for 15% -> 14%
where the time goes in v4:
time: 161 us; the launch traced here: 159 us
  starting transfers between devices  68.4 us (42%)
  waiting for transfers between devices  49.5 us (31%)
  Pallas kernels  36 us (22%)
  local copies, waits for them, and re-layouts  3.85 us (2%)
    ppermute x20, starting transfers between devices, swap(): lax.ppermute(x, axis, [(i, (((i + shift) % n ^ bit) - shift) % n) for i i...  48.9 us
    ppermute x20, waiting for transfers between devices, swap(): lax.ppermute(x, axis, [(i, (((i + shift) % n ^ bit) - shift) % n) for i i...  26.5 us
    pallas_call x2, Pallas kernels, term(): pl.pallas_call(functools.partial(term_kernel, part), grid_spec=pltpu.Pref...  19 us
    ppermute x4, waiting for transfers between devices, step(): return lax.ppermute(x, axis, [(i, (i + by) % n) for i in range(n)])  14.6 us
    all_to_all x2, starting transfers between devices, gather_z(): lax.all_to_all(jnp.broadcast_to(v, (NZ, *v.shape)), 'z', 0, 0, tiled=True)  11.2 us
    pallas_call x2, Pallas kernels, solve(): pl.pallas_call(functools.partial(solve_kernel, n), in_specs=[scalar] * 2...  11 us
    pallas_call x2, Pallas kernels, finish(): pl.pallas_call(functools.partial(finish_kernel, chunk), in_specs=[pl.Bloc...  5.98 us
    ppermute x6, starting transfers between devices, spread_x(): others = [lax.ppermute(v, 'x', [(NX - 1, i)]) for i in range(NX - 1)]  5.24 us
  transfers between devices with their start and end apart: 32, of which 16 were waited for; matrix products, arithmetic and copies ran while one was open for 2% of the time, Pallas kernels for 14%

profile of v4, /device:TPU:1, one launch (start us, length us, event | category | flops | bytes accessed | tf_op | source)
XLA Modules:
  0.0 159.3 jit_solution(16194084735922576678)
XLA Ops:
  0.6 11.4 %term.2 = (f32[8,16,1024]{2,1,0:T(8,128)}, f32[8,16,1024]{2,1,0:T(8,128)}, f32[8,16,1024]{2,1,0:T(8,128)}, f32[8,16,1024]{2,1,0:T(8,128)}) custom-call(s32[1]{0:T(128)} %bitcast.3.z_ref, s32[1]{0:T(128)} %bitcast.1.y_ref, f32[4,512,512]{2,1,0:T(8,128)} %bitcast.31, f32[4,512,1536]{2,1,0:T(8,128)} %bitcast.25, f32[4,512,1536]{2,1,0:T(8,128)} %bitcast.26, ...), custom_call_target="tpu_custom_call" | custom-call | flops 6442450944 | bytes 12582912 | tf_op jit(solution)/shard_map/term/pallas_call | solution.py:67
  12.0 2.1 %collective-permute-start = (f32[8,16,1024]{2,1,0:T(8,128)}, f32[8,16,1024]{2,1,0:T(8,128)S(1)}, u32[]{:S(2)}, u32[]{:S(2)}) collective-permute-start(f32[8,16,1024]{2,1,0:T(8,128)} %get-tuple-element.18), channel_id=1, source_target_pairs={{0,8},{8,0},{16,24},{24,16},{1,9},{9,1},{17,25},{25,17},{2,10},{10... | collective-permute-start | bytes 1572872 | tf_op jit(solution)/shard_map/ppermute | solution.py:196
  14.1 2.6 %collective-permute-start.1 = (f32[8,16,1024]{2,1,0:T(8,128)}, f32[8,16,1024]{2,1,0:T(8,128)S(1)}, u32[]{:S(2)}, u32[]{:S(2)}) collective-permute-start(f32[8,16,1024]{2,1,0:T(8,128)} %get-tuple-element.19), channel_id=1, source_target_pairs={{0,16},{8,24},{16,0},{24,8},{1,17},{9,25},{17,1},{25,9},{2,18},{10... | collective-permute-start | bytes 1572872 | tf_op jit(solution)/shard_map/ppermute | solution.py:196
  16.8 7.6 %term.3 = (f32[8,16,512]{2,1,0:T(8,128)}, f32[8,16,512]{2,1,0:T(8,128)}, f32[8,16,512]{2,1,0:T(8,128)}, f32[8,16,512]{2,1,0:T(8,128)}) custom-call(s32[1]{0:T(128)} %bitcast.3.z_ref, s32[1]{0:T(128)} %bitcast.1.y_ref, f32[4,512,512]{2,1,0:T(8,128)} %bitcast.32, f32[4,512,1536]{2,1,0:T(8,128)} %bitcast.29, f32[4,512,1536]{2,1,0:T(8,128)} %bitcast.30), custom_call_target="tpu_custom_call" | custom-call | flops 3221225472 | bytes 8388608 | tf_op jit(solution)/shard_map/term/pallas_call | solution.py:67
  24.4 3.8 %collective-permute-start.11 = (f32[8,16,512]{2,1,0:T(8,128)}, f32[8,16,512]{2,1,0:T(8,128)S(1)}, u32[]{:S(2)}, u32[]{:S(2)}) collective-permute-start(f32[8,16,512]{2,1,0:T(8,128)} %get-tuple-element.25), channel_id=1, source_target_pairs={{0,16},{8,24},{16,0},{24,8},{1,17},{9,25},{17,1},{25,9},{2,18},{10... | collective-permute-start | bytes 786440 | tf_op jit(solution)/shard_map/ppermute | solution.py:196
  28.6 11.0 %collective-permute-done.1 = f32[8,16,1024]{2,1,0:T(8,128)S(1)} collective-permute-done((f32[8,16,1024]{2,1,0:T(8,128)}, f32[8,16,1024]{2,1,0:T(8,128)S(1)}, u32[]{:S(2)}, u32[]{:S(2)}) %collective-permute-start.1) | collective-permute-done | bytes 524320 | tf_op jit(solution)/shard_map/ppermute | solution.py:196
  39.6 1.7 %collective-permute-done.2 = f32[8,16,1024]{2,1,0:T(8,128)S(1)} collective-permute-done((f32[8,16,1024]{2,1,0:T(8,128)}, f32[8,16,1024]{2,1,0:T(8,128)S(1)}, u32[]{:S(2)}, u32[]{:S(2)}) %collective-permute-start.2) | collective-permute-done | bytes 524320 | tf_op jit(solution)/shard_map/ppermute | solution.py:196
  41.5 1.7 %collective-permute-start.3 = (f32[4,16,1024]{2,1,0:T(8,128)S(1)}, f32[4,16,1024]{2,1,0:T(8,128)S(1)}, u32[]{:S(2)}, u32[]{:S(2)}) collective-permute-start(f32[4,16,1024]{2,1,0:T(8,128)S(1)} %slice.137), channel_id=1, source_target_pairs={{0,32},{32,0},{64,96},{96,64},{128,160},{160,128},{192,224},{224,1... | collective-permute-start | bytes 786440 | tf_op jit(solution)/shard_map/ppermute | solution.py:196
  43.3 4.0 %collective-permute-done.3 = f32[4,16,1024]{2,1,0:T(8,128)S(1)} collective-permute-done((f32[4,16,1024]{2,1,0:T(8,128)S(1)}, f32[4,16,1024]{2,1,0:T(8,128)S(1)}, u32[]{:S(2)}, u32[]{:S(2)}) %collective-permute-start.3) | collective-permute-done | bytes 262176 | tf_op jit(solution)/shard_map/ppermute | solution.py:196
  47.3 3.1 %collective-permute-start.4 = (f32[2,16,1024]{2,1,0:T(8,128)S(1)}, f32[2,16,1024]{2,1,0:T(8,128)S(1)}, u32[]{:S(2)}, u32[]{:S(2)}) collective-permute-start(f32[2,16,1024]{2,1,0:T(8,128)S(1)} %slice.139), channel_id=1, source_target_pairs={{0,64},{32,96},{64,0},{96,32},{128,192},{160,224},{192,128},{224,1... | collective-permute-start | bytes 393224 | tf_op jit(solution)/shard_map/ppermute | solution.py:196
  50.4 2.9 %collective-permute-done.4 = f32[2,16,1024]{2,1,0:T(8,128)S(1)} collective-permute-done((f32[2,16,1024]{2,1,0:T(8,128)S(1)}, f32[2,16,1024]{2,1,0:T(8,128)S(1)}, u32[]{:S(2)}, u32[]{:S(2)}) %collective-permute-start.4) | collective-permute-done | bytes 131104 | tf_op jit(solution)/shard_map/ppermute | solution.py:196
  53.4 6.8 %collective-permute-start.5 = (f32[1,16,1024]{2,1,0:T(8,128)S(1)}, f32[1,16,1024]{2,1,0:T(8,128)S(1)}, u32[]{:S(2)}, u32[]{:S(2)}) collective-permute-start(f32[1,16,1024]{2,1,0:T(8,128)S(1)} %slice.141), channel_id=1, source_target_pairs={{0,128},{32,160},{64,192},{96,224},{128,0},{160,32},{192,64},{224,... | collective-permute-start | bytes 196616 | tf_op jit(solution)/shard_map/ppermute | solution.py:196
  60.6 1.3 collective-permute-done.5
  62.0 11.0 %collective-permute-start.6 = (f32[16,768]{1,0:T(8,128)S(1)}, f32[16,768]{1,0:T(8,128)S(1)}, u32[]{:S(2)}, u32[]{:S(2)}) collective-permute-start(f32[16,768]{1,0:T(8,128)S(1)} %pad_maximum_fusion.2), channel_id=1, source_target_pairs={{0,1},{1,0},{2,3},{3,2},{4,5},{5,4},{6,7},{7,6},{8,9},{9,8},{10,11... | collective-permute-start | bytes 147464 | tf_op jit(solution)/shard_map/ppermute | solution.py:196
  73.1 0.7 collective-permute-done.6
  73.9 0.7 collective-permute-start.9
  74.6 0.7 collective-permute-start.8
  75.3 1.3 collective-permute-start.7
  76.6 0.6 collective-permute-done.14
  77.2 6.3 %collective-permute-start.15 = (f32[1,16,512]{2,1,0:T(8,128)S(1)}, f32[1,16,512]{2,1,0:T(8,128)S(1)}, u32[]{:S(2)}, u32[]{:S(2)}) collective-permute-start(f32[1,16,512]{2,1,0:T(8,128)S(1)} %slice.155), channel_id=1, source_target_pairs={{0,128},{32,160},{64,192},{96,224},{128,0},{160,32},{192,64},{224,... | collective-permute-start | bytes 98312 | tf_op jit(solution)/shard_map/ppermute | solution.py:196
  83.5 0.9 broadcast_in_dim.9
  84.4 7.1 %all-to-all-start = ((f32[8,16,1280]{2,1,0:T(8,128)}), f32[8,16,1280]{2,1,0:T(8,128)S(1)}, u32[]{:S(2)}, u32[]{:S(2)}) async-start(f32[8,16,1280]{2,1,0:T(8,128)} %broadcast_in_dim.9), calls=%async_computation | async-start | bytes 1310720 | tf_op jit(solution)/shard_map/all_to_all | solution.py:227
  91.5 2.0 %collective-permute-start.16 = (f32[16,256]{1,0:T(8,128)S(1)}, f32[16,256]{1,0:T(8,128)S(1)}, u32[]{:S(2)}, u32[]{:S(2)}) collective-permute-start(f32[16,256]{1,0:T(8,128)S(1)} %slice_select_fusion.6), channel_id=1, source_target_pairs={{0,1},{1,0},{2,3},{3,2},{4,5},{5,4},{6,7},{7,6},{8,9},{9,8},{10,11... | collective-permute-start | bytes 49160 | tf_op jit(solution)/shard_map/ppermute | solution.py:196
  93.5 0.8 collective-permute-done.16
  94.4 0.7 collective-permute-start.19
  95.0 0.7 collective-permute-start.18
  95.7 1.3 collective-permute-start.17
  97.0 4.8 %collective-permute-done.17 = f32[16,512]{1,0:T(8,128)S(1)} collective-permute-done((f32[16,512]{1,0:T(8,128)S(1)}, f32[16,512]{1,0:T(8,128)S(1)}, u32[]{:S(2)}, u32[]{:S(2)}) %collective-permute-start.17) | collective-permute-done | bytes 32800 | tf_op jit(solution)/shard_map/ppermute | solution.py:222
  101.9 0.4 collective-permute-start.22
  102.3 3.1 %collective-permute-start.20 = (f32[16,512]{1,0:T(8,128)S(1)}, f32[16,512]{1,0:T(8,128)S(1)}, u32[]{:S(2)}, u32[]{:S(2)}) collective-permute-start(f32[16,512]{1,0:T(8,128)S(1)} %add_select_fusion.1), channel_id=1, source_target_pairs={{0,8},{8,0},{16,24},{24,16},{1,9},{9,1},{17,25},{25,17},{2,10},{10... | collective-permute-start | bytes 98312 | tf_op jit(solution)/shard_map/ppermute | solution.py:196
  105.4 1.0 collective-permute-done.22
  106.6 0.5 collective-permute-done.20
  107.1 3.5 %all-to-all-done.refs_1_.refs_0_.refs_5_ = f32[8,16,1280]{2,1,0:T(8,128)S(1)} async-done(((f32[8,16,1280]{2,1,0:T(8,128)}), f32[8,16,1280]{2,1,0:T(8,128)S(1)}, u32[]{:S(2)}, u32[]{:S(2)}) %all-to-all-start) | async-done | bytes 655392 | tf_op jit(solution)/shard_map/all_to_all | solution.py:227
  110.7 1.3 collective-permute-start.23
  112.0 1.1 broadcast_in_dim.10
  113.1 4.1 %all-to-all-start.1 = ((f32[8,4,16,512]{3,2,1,0:T(8,128)}), f32[8,4,16,512]{3,2,1,0:T(8,128)S(1)}, u32[]{:S(2)}, u32[]{:S(2)}) async-start(f32[8,4,16,512]{3,2,1,0:T(8,128)} %broadcast_in_dim.10), calls=%async_computation.1 | async-start | bytes 2097152 | tf_op jit(solution)/shard_map/all_to_all | solution.py:227
  117.3 7.3 %collective-permute-done.24.refs_3_.refs_2_.refs_7_ = f32[8,16,1280]{2,1,0:T(8,128)S(1)} collective-permute-done((f32[8,16,1280]{2,1,0:T(8,128)S(1)}, f32[8,16,1280]{2,1,0:T(8,128)S(1)}, u32[]{:S(2)}, u32[]{:S(2)}) %collective-permute-start.24) | collective-permute-done | bytes 655392 | tf_op jit(solution)/shard_map/ppermute | solution.py:236
  124.6 1.4 collective-permute-start.26
  126.3 7.3 %collective-permute-done.25.refs_4_.refs_3_.refs_8_ = f32[4,16,1280]{2,1,0:T(8,128)S(1)} collective-permute-done((f32[4,16,1280]{2,1,0:T(8,128)S(1)}, f32[4,16,1280]{2,1,0:T(8,128)S(1)}, u32[]{:S(2)}, u32[]{:S(2)}) %collective-permute-start.25) | collective-permute-done | bytes 327712 | tf_op jit(solution)/shard_map/ppermute | solution.py:236
  133.6 0.7 copy-done.8
  134.3 4.3 %collective-permute-start.27 = (f32[4,8,16,256]{3,2,1,0:T(8,128)S(1)}, f32[4,8,16,256]{3,2,1,0:T(8,128)}, u32[]{:S(2)}, u32[]{:S(2)}) collective-permute-start(f32[4,8,16,256]{3,2,1,0:T(8,128)S(1)} %bitcast.36), channel_id=1, source_target_pairs={{0,1},{1,0},{2,3},{3,2},{4,5},{5,4},{6,7},{7,6},{8,9},{9,8},{10,11... | collective-permute-start | bytes 1572872 | tf_op jit(solution)/shard_map/ppermute | solution.py:196
  138.7 1.7 %collective-permute-done.27.other_hbm = f32[4,8,16,256]{3,2,1,0:T(8,128)} collective-permute-done((f32[4,8,16,256]{3,2,1,0:T(8,128)S(1)}, f32[4,8,16,256]{3,2,1,0:T(8,128)}, u32[]{:S(2)}, u32[]{:S(2)}) %collective-permute-start.27) | collective-permute-done | bytes 524320 | tf_op jit(solution)/shard_map/ppermute | solution.py:196
  140.3 5.9 %solve.3.own = f32[2,512,512]{2,1,0:T(8,128)} custom-call(s32[1]{0:T(128)} %bitcast.1.y_ref, s32[1]{0:T(128)} %bitcast.core_ref, f32[2,512,512]{2,1,0:T(8,128)} %inv_hbm.3, f32[4,8,16,256]{3,2,1,0:T(8,128)} %collective-permute-done.27.other_hbm, f32[8,16,1280]{2,1,0:T(8,128)} %copy-done.3, f32[8,16,1280]{2,1,0:T(8,128)} %copy-done.5, ...), custom_call_target="tpu_custom_call" | custom-call | flops 2415919104 | bytes 6291456 | tf_op jit(solution)/shard_map/solve/pallas_call | solution.py:132
  146.3 0.5 collective-permute-start.29
  146.7 1.0 copy-done.6
  147.7 5.1 %solve.2.own = f32[2,512,256]{2,1,0:T(8,128)} custom-call(s32[1]{0:T(128)} %bitcast.1.y_ref, s32[1]{0:T(128)} %bitcast.core_ref, f32[2,512,512]{2,1,0:T(8,128)} %inv_hbm.3, f32[4,8,16,256]{3,2,1,0:T(8,128)} %collective-permute-done.27.other_hbm, f32[8,4,16,512]{3,2,1,0:T(8,128)} %copy-done.6, f32[8,16,1280]{2,1,0:T(8,128)} %copy-done.3, ...), custom_call_target="tpu_custom_call" | custom-call | flops 1207959552 | bytes 6291456 | tf_op jit(solution)/shard_map/solve/pallas_call | solution.py:132
  153.2 3.6 %finish.2 = (f32[2,512,1536]{2,1,0:T(8,128)}, f32[16,1536]{1,0:T(8,128)S(1)}) custom-call(s32[1]{0:T(128)} %bitcast.core_ref, f32[2,512,512]{2,1,0:T(8,128)S(1)} %copy-done, f32[2,512,512]{2,1,0:T(8,128)} %collective-permute-done.29.other, f32[16,1024]{1,0:T(8,128)S(1)} %fusion.1.base, f32[2,16,512]{2,1,0:T(8,128)S(1)} %bitcast.23), custom_call_target="tpu_custom_call" | custom-call | flops 100663296 | bytes 6291456 | tf_op jit(solution)/shard_map/finish/pallas_call | solution.py:176
  156.8 2.3 %finish.3 = (f32[2,512,1536]{2,1,0:T(8,128)}, f32[16,1536]{1,0:T(8,128)}) custom-call(s32[1]{0:T(128)} %bitcast.core_ref, f32[2,512,256]{2,1,0:T(8,128)S(1)} %copy-done.1, f32[2,512,256]{2,1,0:T(8,128)S(1)} %collective-permute-done.28.other, f32[16,512]{1,0:T(8,128)S(1)} %fusion.3.base, f32[2,16,512]{2,1,0:T(8,128)S(1)} %bitcast.24, ...), custom_call_target="tpu_custom_call", output_to_operand_aliasing={{0}: (5, {})} | custom-call | flops 50331648 | bytes 6291456 | tf_op jit(solution)/shard_map/finish/pallas_call | solution.py:176
  (84 shorter events, 2.2 us)
Async XLA Ops:
  12.0 16.2 %collective-permute-start = (f32[8,16,1024]{2,1,0:T(8,128)}, f32[8,16,1024]{2,1,0:T(8,128)S(1)}, u32[]{:S(2)}, u32[]{:S(2)}) collective-permute-start(f32[8,16,1024]{2,1,0:T(8,128)} %get-tuple-element.18), channel_id=1, source_target_pairs={{0,8},{8,0},{16,24},{24,16},{1,9},{9,1},{17,25},{25,17},{2,10},{10... | collective-permute-start | bytes 1572872 | tf_op jit(solution)/shard_map/ppermute | solution.py:196
  14.1 25.4 %collective-permute-start.1 = (f32[8,16,1024]{2,1,0:T(8,128)}, f32[8,16,1024]{2,1,0:T(8,128)S(1)}, u32[]{:S(2)}, u32[]{:S(2)}) collective-permute-start(f32[8,16,1024]{2,1,0:T(8,128)} %get-tuple-element.19), channel_id=1, source_target_pairs={{0,16},{8,24},{16,0},{24,8},{1,17},{9,25},{17,1},{25,9},{2,18},{10... | collective-permute-start | bytes 1572872 | tf_op jit(solution)/shard_map/ppermute | solution.py:196
  16.8 24.5 %collective-permute-start.2 = (f32[8,16,1024]{2,1,0:T(8,128)}, f32[8,16,1024]{2,1,0:T(8,128)S(1)}, u32[]{:S(2)}, u32[]{:S(2)}) collective-permute-start(f32[8,16,1024]{2,1,0:T(8,128)} %get-tuple-element.20), channel_id=1, source_target_pairs={{0,24},{8,16},{16,8},{24,0},{1,25},{9,17},{17,9},{25,1},{2,26},{10... | collective-permute-start | bytes 1572872 | tf_op jit(solution)/shard_map/ppermute | solution.py:196
  16.8 24.5 %copy-start.9 = (f32[8,16,1024]{2,1,0:T(8,128)S(1)}, f32[8,16,1024]{2,1,0:T(8,128)}, u32[]{:S(2)}) copy-start(f32[8,16,1024]{2,1,0:T(8,128)} %get-tuple-element.17) | copy-start | bytes 1572868
  16.8 26.5 %copy-start.2 = (f32[1,1,2,16,512]{4,3,2,1,0:T(8,128)S(1)}, f32[1,1,2,16,512]{4,3,2,1,0:T(8,128)}, u32[]{:S(2)}) copy-start(f32[1,1,2,16,512]{4,3,2,1,0:T(8,128)} %param.8) | copy-start | bytes 196612
  16.8 26.5 %copy-start.11 = (f32[1,1,16,1536]{3,2,1,0:T(8,128)S(1)}, f32[1,1,16,1536]{3,2,1,0:T(8,128)}, u32[]{:S(2)}) copy-start(f32[1,1,16,1536]{3,2,1,0:T(8,128)} %param.7) | copy-start | bytes 294916
  24.4 35.8 %copy-start.10 = (f32[8,16,512]{2,1,0:T(8,128)S(1)}, f32[8,16,512]{2,1,0:T(8,128)}, u32[]{:S(2)}) copy-start(f32[8,16,512]{2,1,0:T(8,128)} %get-tuple-element.23) | copy-start | bytes 786436
  24.4 35.8 %collective-permute-start.10 = (f32[8,16,512]{2,1,0:T(8,128)}, f32[8,16,512]{2,1,0:T(8,128)S(1)}, u32[]{:S(2)}, u32[]{:S(2)}) collective-permute-start(f32[8,16,512]{2,1,0:T(8,128)} %get-tuple-element.24), channel_id=1, source_target_pairs={{0,8},{8,0},{16,24},{24,16},{1,9},{9,1},{17,25},{25,17},{2,10},{10... | collective-permute-start | bytes 786440 | tf_op jit(solution)/shard_map/ppermute | solution.py:196
  24.4 35.8 %collective-permute-start.11 = (f32[8,16,512]{2,1,0:T(8,128)}, f32[8,16,512]{2,1,0:T(8,128)S(1)}, u32[]{:S(2)}, u32[]{:S(2)}) collective-permute-start(f32[8,16,512]{2,1,0:T(8,128)} %get-tuple-element.25), channel_id=1, source_target_pairs={{0,16},{8,24},{16,0},{24,8},{1,17},{9,25},{17,1},{25,9},{2,18},{10... | collective-permute-start | bytes 786440 | tf_op jit(solution)/shard_map/ppermute | solution.py:196
  28.2 32.0 %collective-permute-start.12 = (f32[8,16,512]{2,1,0:T(8,128)}, f32[8,16,512]{2,1,0:T(8,128)S(1)}, u32[]{:S(2)}, u32[]{:S(2)}) collective-permute-start(f32[8,16,512]{2,1,0:T(8,128)} %get-tuple-element.26), channel_id=1, source_target_pairs={{0,24},{8,16},{16,8},{24,0},{1,25},{9,17},{17,9},{25,1},{2,26},{10... | collective-permute-start | bytes 786440 | tf_op jit(solution)/shard_map/ppermute | solution.py:196
  41.5 5.8 %collective-permute-start.3 = (f32[4,16,1024]{2,1,0:T(8,128)S(1)}, f32[4,16,1024]{2,1,0:T(8,128)S(1)}, u32[]{:S(2)}, u32[]{:S(2)}) collective-permute-start(f32[4,16,1024]{2,1,0:T(8,128)S(1)} %slice.137), channel_id=1, source_target_pairs={{0,32},{32,0},{64,96},{96,64},{128,160},{160,128},{192,224},{224,1... | collective-permute-start | bytes 786440 | tf_op jit(solution)/shard_map/ppermute | solution.py:196
  47.3 6.0 %collective-permute-start.4 = (f32[2,16,1024]{2,1,0:T(8,128)S(1)}, f32[2,16,1024]{2,1,0:T(8,128)S(1)}, u32[]{:S(2)}, u32[]{:S(2)}) collective-permute-start(f32[2,16,1024]{2,1,0:T(8,128)S(1)} %slice.139), channel_id=1, source_target_pairs={{0,64},{32,96},{64,0},{96,32},{128,192},{160,224},{192,128},{224,1... | collective-permute-start | bytes 393224 | tf_op jit(solution)/shard_map/ppermute | solution.py:196
  53.4 8.6 %collective-permute-start.5 = (f32[1,16,1024]{2,1,0:T(8,128)S(1)}, f32[1,16,1024]{2,1,0:T(8,128)S(1)}, u32[]{:S(2)}, u32[]{:S(2)}) collective-permute-start(f32[1,16,1024]{2,1,0:T(8,128)S(1)} %slice.141), channel_id=1, source_target_pairs={{0,128},{32,160},{64,192},{96,224},{128,0},{160,32},{192,64},{224,... | collective-permute-start | bytes 196616 | tf_op jit(solution)/shard_map/ppermute | solution.py:196
  60.3 12.7 %collective-permute-start.13 = (f32[4,16,512]{2,1,0:T(8,128)S(1)}, f32[4,16,512]{2,1,0:T(8,128)S(1)}, u32[]{:S(2)}, u32[]{:S(2)}) collective-permute-start(f32[4,16,512]{2,1,0:T(8,128)S(1)} %slice.151), channel_id=1, source_target_pairs={{0,224},{32,64},{64,32},{96,128},{128,96},{160,192},{192,160},{224... | collective-permute-start | bytes 393224 | tf_op jit(solution)/shard_map/ppermute | solution.py:196
  62.0 11.9 %collective-permute-start.6 = (f32[16,768]{1,0:T(8,128)S(1)}, f32[16,768]{1,0:T(8,128)S(1)}, u32[]{:S(2)}, u32[]{:S(2)}) collective-permute-start(f32[16,768]{1,0:T(8,128)S(1)} %pad_maximum_fusion.2), channel_id=1, source_target_pairs={{0,1},{1,0},{2,3},{3,2},{4,5},{5,4},{6,7},{7,6},{8,9},{9,8},{10,11... | collective-permute-start | bytes 147464 | tf_op jit(solution)/shard_map/ppermute | solution.py:196
  73.0 4.1 %collective-permute-start.14 = (f32[2,16,512]{2,1,0:T(8,128)S(1)}, f32[2,16,512]{2,1,0:T(8,128)S(1)}, u32[]{:S(2)}, u32[]{:S(2)}) collective-permute-start(f32[2,16,512]{2,1,0:T(8,128)S(1)} %slice.153), channel_id=1, source_target_pairs={{0,64},{32,224},{64,0},{96,160},{128,192},{160,96},{192,128},{224,... | collective-permute-start | bytes 196616 | tf_op jit(solution)/shard_map/ppermute | solution.py:196
  73.9 9.6 %collective-permute-start.9 = (f32[16,1280]{1,0:T(8,128)S(1)}, f32[16,1280]{1,0:T(8,128)S(1)}, u32[]{:S(2)}, u32[]{:S(2)}) collective-permute-start(f32[16,1280]{1,0:T(8,128)S(1)} %pad_maximum_fusion.1), channel_id=1, source_target_pairs={{6,4},{7,5},{14,12},{15,13},{22,20},{23,21},{30,28},{31,29},{38,36... | collective-permute-start | bytes 245768 | tf_op jit(solution)/shard_map/ppermute | solution.py:222
  74.6 8.9 %collective-permute-start.8 = (f32[16,1280]{1,0:T(8,128)S(1)}, f32[16,1280]{1,0:T(8,128)S(1)}, u32[]{:S(2)}, u32[]{:S(2)}) collective-permute-start(f32[16,1280]{1,0:T(8,128)S(1)} %pad_maximum_fusion.1), channel_id=1, source_target_pairs={{6,2},{7,3},{14,10},{15,11},{22,18},{23,19},{30,26},{31,27},{38,34... | collective-permute-start | bytes 245768 | tf_op jit(solution)/shard_map/ppermute | solution.py:222
  75.3 8.2 %collective-permute-start.7 = (f32[16,1280]{1,0:T(8,128)S(1)}, f32[16,1280]{1,0:T(8,128)S(1)}, u32[]{:S(2)}, u32[]{:S(2)}) collective-permute-start(f32[16,1280]{1,0:T(8,128)S(1)} %pad_maximum_fusion.1), channel_id=1, source_target_pairs={{6,0},{7,1},{14,8},{15,9},{22,16},{23,17},{30,24},{31,25},{38,32},... | collective-permute-start | bytes 245768 | tf_op jit(solution)/shard_map/ppermute | solution.py:222
  77.2 14.3 %collective-permute-start.15 = (f32[1,16,512]{2,1,0:T(8,128)S(1)}, f32[1,16,512]{2,1,0:T(8,128)S(1)}, u32[]{:S(2)}, u32[]{:S(2)}) collective-permute-start(f32[1,16,512]{2,1,0:T(8,128)S(1)} %slice.155), channel_id=1, source_target_pairs={{0,128},{32,160},{64,192},{96,224},{128,0},{160,32},{192,64},{224,... | collective-permute-start | bytes 98312 | tf_op jit(solution)/shard_map/ppermute | solution.py:196
  84.4 26.1 %all-to-all-start = ((f32[8,16,1280]{2,1,0:T(8,128)}), f32[8,16,1280]{2,1,0:T(8,128)S(1)}, u32[]{:S(2)}, u32[]{:S(2)}) async-start(f32[8,16,1280]{2,1,0:T(8,128)} %broadcast_in_dim.9), calls=%async_computation | async-start | bytes 1310720 | tf_op jit(solution)/shard_map/all_to_all | solution.py:227
  91.5 2.8 %collective-permute-start.16 = (f32[16,256]{1,0:T(8,128)S(1)}, f32[16,256]{1,0:T(8,128)S(1)}, u32[]{:S(2)}, u32[]{:S(2)}) collective-permute-start(f32[16,256]{1,0:T(8,128)S(1)} %slice_select_fusion.6), channel_id=1, source_target_pairs={{0,1},{1,0},{2,3},{3,2},{4,5},{5,4},{6,7},{7,6},{8,9},{9,8},{10,11... | collective-permute-start | bytes 49160 | tf_op jit(solution)/shard_map/ppermute | solution.py:196
  94.4 2.6 %collective-permute-start.19 = (f32[16,512]{1,0:T(8,128)S(1)}, f32[16,512]{1,0:T(8,128)S(1)}, u32[]{:S(2)}, u32[]{:S(2)}) collective-permute-start(f32[16,512]{1,0:T(8,128)S(1)} %pad_maximum_fusion.3), channel_id=1, source_target_pairs={{6,4},{7,5},{14,12},{15,13},{22,20},{23,21},{30,28},{31,29},{38,36... | collective-permute-start | bytes 98312 | tf_op jit(solution)/shard_map/ppermute | solution.py:222
  95.0 2.0 %collective-permute-start.18 = (f32[16,512]{1,0:T(8,128)S(1)}, f32[16,512]{1,0:T(8,128)S(1)}, u32[]{:S(2)}, u32[]{:S(2)}) collective-permute-start(f32[16,512]{1,0:T(8,128)S(1)} %pad_maximum_fusion.3), channel_id=1, source_target_pairs={{6,2},{7,3},{14,10},{15,11},{22,18},{23,19},{30,26},{31,27},{38,34... | collective-permute-start | bytes 98312 | tf_op jit(solution)/shard_map/ppermute | solution.py:222
  95.7 6.2 %collective-permute-start.17 = (f32[16,512]{1,0:T(8,128)S(1)}, f32[16,512]{1,0:T(8,128)S(1)}, u32[]{:S(2)}, u32[]{:S(2)}) collective-permute-start(f32[16,512]{1,0:T(8,128)S(1)} %pad_maximum_fusion.3), channel_id=1, source_target_pairs={{6,0},{7,1},{14,8},{15,9},{22,16},{23,17},{30,24},{31,25},{38,32},... | collective-permute-start | bytes 98312 | tf_op jit(solution)/shard_map/ppermute | solution.py:222
  101.9 4.5 %collective-permute-start.22 = (f32[16,512]{1,0:T(8,128)S(1)}, f32[16,512]{1,0:T(8,128)S(1)}, u32[]{:S(2)}, u32[]{:S(2)}) collective-permute-start(f32[16,512]{1,0:T(8,128)S(1)} %add_select_fusion.1), channel_id=1, source_target_pairs={{0,24},{8,16},{16,8},{24,0},{1,25},{9,17},{17,9},{25,1},{2,26},{10... | collective-permute-start | bytes 98312 | tf_op jit(solution)/shard_map/ppermute | solution.py:196
  102.3 4.3 %collective-permute-start.21 = (f32[16,512]{1,0:T(8,128)S(1)}, f32[16,512]{1,0:T(8,128)S(1)}, u32[]{:S(2)}, u32[]{:S(2)}) collective-permute-start(f32[16,512]{1,0:T(8,128)S(1)} %add_select_fusion.1), channel_id=1, source_target_pairs={{0,16},{8,24},{16,0},{24,8},{1,17},{9,25},{17,1},{25,9},{2,18},{10... | collective-permute-start | bytes 98312 | tf_op jit(solution)/shard_map/ppermute | solution.py:196
  102.3 4.8 %collective-permute-start.20 = (f32[16,512]{1,0:T(8,128)S(1)}, f32[16,512]{1,0:T(8,128)S(1)}, u32[]{:S(2)}, u32[]{:S(2)}) collective-permute-start(f32[16,512]{1,0:T(8,128)S(1)} %add_select_fusion.1), channel_id=1, source_target_pairs={{0,8},{8,0},{16,24},{24,16},{1,9},{9,1},{17,25},{25,17},{2,10},{10... | collective-permute-start | bytes 98312 | tf_op jit(solution)/shard_map/ppermute | solution.py:196
  110.5 29.8 %copy-start.3 = (f32[8,16,1280]{2,1,0:T(8,128)}, f32[8,16,1280]{2,1,0:T(8,128)S(1)}, u32[]{:S(2)}) copy-start(f32[8,16,1280]{2,1,0:T(8,128)S(1)} %all-to-all-done.refs_1_.refs_0_.refs_5_) | copy-start | bytes 1966084
  110.5 14.0 %collective-permute-start.24 = (f32[8,16,1280]{2,1,0:T(8,128)S(1)}, f32[8,16,1280]{2,1,0:T(8,128)S(1)}, u32[]{:S(2)}, u32[]{:S(2)}) collective-permute-start(f32[8,16,1280]{2,1,0:T(8,128)S(1)} %all-to-all-done.refs_1_.refs_0_.refs_5_), channel_id=1, source_target_pairs={{0,24},{8,0},{16,8},{24,16},{1,25},{9,1},{17,9},{25,17},{2,26},{10... | collective-permute-start | bytes 1966088 | tf_op jit(solution)/shard_map/ppermute | solution.py:236
  110.7 15.4 %collective-permute-start.23 = (f32[8,16,1280]{2,1,0:T(8,128)S(1)}, f32[8,16,1280]{2,1,0:T(8,128)S(1)}, u32[]{:S(2)}, u32[]{:S(2)}) collective-permute-start(f32[8,16,1280]{2,1,0:T(8,128)S(1)} %all-to-all-done.refs_1_.refs_0_.refs_5_), channel_id=1, source_target_pairs={{0,8},{8,16},{16,24},{24,0},{1,9},{9,17},{17,25},{25,1},{2,10},{10... | collective-permute-start | bytes 1966088 | tf_op jit(solution)/shard_map/ppermute | solution.py:236
  113.1 33.6 %all-to-all-start.1 = ((f32[8,4,16,512]{3,2,1,0:T(8,128)}), f32[8,4,16,512]{3,2,1,0:T(8,128)S(1)}, u32[]{:S(2)}, u32[]{:S(2)}) async-start(f32[8,4,16,512]{3,2,1,0:T(8,128)} %broadcast_in_dim.10), calls=%async_computation.1 | async-start | bytes 2097152 | tf_op jit(solution)/shard_map/all_to_all | solution.py:227
  124.6 15.7 %copy-start.4 = (f32[8,16,1280]{2,1,0:T(8,128)}, f32[8,16,1280]{2,1,0:T(8,128)S(1)}, u32[]{:S(2)}) copy-start(f32[8,16,1280]{2,1,0:T(8,128)S(1)} %collective-permute-done.24.refs_3_.refs_2_.refs_7_) | copy-start | bytes 1966084
  124.6 9.0 %collective-permute-start.26 = (f32[4,16,1280]{2,1,0:T(8,128)S(1)}, f32[4,16,1280]{2,1,0:T(8,128)S(1)}, u32[]{:S(2)}, u32[]{:S(2)}) collective-permute-start(f32[4,16,1280]{2,1,0:T(8,128)S(1)} %slice.162), channel_id=1, source_target_pairs={{0,24},{8,0},{16,8},{24,16},{1,25},{9,1},{17,9},{25,17},{2,26},{10... | collective-permute-start | bytes 983048 | tf_op jit(solution)/shard_map/ppermute | solution.py:236
  126.1 14.3 %copy-start.5 = (f32[8,16,1280]{2,1,0:T(8,128)}, f32[8,16,1280]{2,1,0:T(8,128)S(1)}, u32[]{:S(2)}) copy-start(f32[8,16,1280]{2,1,0:T(8,128)S(1)} %collective-permute-done.23.refs_2_.refs_1_.refs_6_) | copy-start | bytes 1966084
  126.1 7.5 %collective-permute-start.25 = (f32[4,16,1280]{2,1,0:T(8,128)S(1)}, f32[4,16,1280]{2,1,0:T(8,128)S(1)}, u32[]{:S(2)}, u32[]{:S(2)}) collective-permute-start(f32[4,16,1280]{2,1,0:T(8,128)S(1)} %slice.160), channel_id=1, source_target_pairs={{0,8},{8,16},{16,24},{24,0},{1,9},{9,17},{17,25},{25,1},{2,10},{10... | collective-permute-start | bytes 983048 | tf_op jit(solution)/shard_map/ppermute | solution.py:236
  133.6 0.7 copy-start.8
  134.3 6.0 %copy-start.7 = (f32[4,16,1280]{2,1,0:T(8,128)}, f32[4,16,1280]{2,1,0:T(8,128)S(1)}, u32[]{:S(2)}) copy-start(f32[4,16,1280]{2,1,0:T(8,128)S(1)} %collective-permute-done.26.refs_5_.refs_4_.refs_9_) | copy-start | bytes 983044
  134.3 6.0 %collective-permute-start.27 = (f32[4,8,16,256]{3,2,1,0:T(8,128)S(1)}, f32[4,8,16,256]{3,2,1,0:T(8,128)}, u32[]{:S(2)}, u32[]{:S(2)}) collective-permute-start(f32[4,8,16,256]{3,2,1,0:T(8,128)S(1)} %bitcast.36), channel_id=1, source_target_pairs={{0,1},{1,0},{2,3},{3,2},{4,5},{5,4},{6,7},{7,6},{8,9},{9,8},{10,11... | collective-permute-start | bytes 1572872 | tf_op jit(solution)/shard_map/ppermute | solution.py:196
  146.3 6.9 %copy-start = (f32[2,512,512]{2,1,0:T(8,128)S(1)}, f32[2,512,512]{2,1,0:T(8,128)}, u32[]{:S(2)}) copy-start(f32[2,512,512]{2,1,0:T(8,128)} %solve.3.own) | copy-start | bytes 6291460
  146.3 6.9 %collective-permute-start.29 = (f32[2,512,512]{2,1,0:T(8,128)}, f32[2,512,512]{2,1,0:T(8,128)}, u32[]{:S(2)}, u32[]{:S(2)}) collective-permute-start(f32[2,512,512]{2,1,0:T(8,128)} %solve.3.own), channel_id=1, source_target_pairs={{0,1},{1,0},{2,3},{3,2},{4,5},{5,4},{6,7},{7,6},{8,9},{9,8},{10,11... | collective-permute-start | bytes 6291464 | tf_op jit(solution)/shard_map/ppermute | solution.py:196
  146.7 1.0 copy-start.6
  152.8 4.0 %copy-start.1 = (f32[2,512,256]{2,1,0:T(8,128)S(1)}, f32[2,512,256]{2,1,0:T(8,128)}, u32[]{:S(2)}) copy-start(f32[2,512,256]{2,1,0:T(8,128)} %solve.2.own) | copy-start | bytes 3145732
  152.8 4.0 %collective-permute-start.28 = (f32[2,512,256]{2,1,0:T(8,128)}, f32[2,512,256]{2,1,0:T(8,128)S(1)}, u32[]{:S(2)}, u32[]{:S(2)}) collective-permute-start(f32[2,512,256]{2,1,0:T(8,128)} %solve.2.own), channel_id=1, source_target_pairs={{0,1},{1,0},{2,3},{3,2},{4,5},{5,4},{6,7},{7,6},{8,9},{9,8},{10,11... | collective-permute-start | bytes 3145736 | tf_op jit(solution)/shard_map/ppermute | solution.py:196

commit v5 on v4

--- a/solution.py
+++ b/solution.py
@@ -219,7 +219,7 @@
 
 
 def spread_x(v):
-    others = [lax.ppermute(v, "x", [(NX - 1, i)]) for i in range(NX - 1)]
+    others = [lax.ppermute(v, "x", [(NX - 1, i)]) for i in (2, 0, 1)]
     return jnp.where(lax.axis_index("x") == NX - 1, v, others[0] + others[1] + others[2])
 
 

time: 161 us -> 159 us (0.988)
  no operation moved by 1% of the time
where the time goes in v5:
time: 159 us
  starting transfers between devices  67 us (42%)
  waiting for transfers between devices  50 us (31%)
  Pallas kernels  36.1 us (23%)
  local copies, waits for them, and re-layouts  3.86 us (2%)
    ppermute x20, starting transfers between devices, swap(): lax.ppermute(x, axis, [(i, (((i + shift) % n ^ bit) - shift) % n) for i i...  48.8 us
    ppermute x20, waiting for transfers between devices, swap(): lax.ppermute(x, axis, [(i, (((i + shift) % n ^ bit) - shift) % n) for i i...  26.8 us
    pallas_call x2, Pallas kernels, term(): pl.pallas_call(functools.partial(term_kernel, part), grid_spec=pltpu.Pref...  19 us
    ppermute x4, waiting for transfers between devices, step(): return lax.ppermute(x, axis, [(i, (i + by) % n) for i in range(n)])  15.2 us
    pallas_call x2, Pallas kernels, solve(): pl.pallas_call(functools.partial(solve_kernel, n), in_specs=[scalar] * 2...  11 us
    all_to_all x2, starting transfers between devices, gather_z(): lax.all_to_all(jnp.broadcast_to(v, (NZ, *v.shape)), 'z', 0, 0, tiled=True)  9.91 us
    pallas_call x2, Pallas kernels, finish(): pl.pallas_call(functools.partial(finish_kernel, chunk), in_specs=[pl.Bloc...  6.07 us
    ppermute x6, starting transfers between devices, spread_x(): others = [lax.ppermute(v, 'x', [(NX - 1, i)]) for i in (2, 0, 1)]  5.24 us
  transfers between devices with their start and end apart: 32, of which 16 were waited for; matrix products, arithmetic and copies ran while one was open for 2% of the time, Pallas kernels for 14%

profile of v5, /device:TPU:1, one launch (start us, length us, event | category | flops | bytes accessed | tf_op | source)
XLA Modules:
  0.0 158.6 jit_solution(16111730880553522082)
XLA Ops:
  0.6 11.4 %term.2 = (f32[8,16,1024]{2,1,0:T(8,128)}, f32[8,16,1024]{2,1,0:T(8,128)}, f32[8,16,1024]{2,1,0:T(8,128)}, f32[8,16,1024]{2,1,0:T(8,128)}) custom-call(s32[1]{0:T(128)} %bitcast.3.z_ref, s32[1]{0:T(128)} %bitcast.1.y_ref, f32[4,512,512]{2,1,0:T(8,128)} %bitcast.31, f32[4,512,1536]{2,1,0:T(8,128)} %bitcast.25, f32[4,512,1536]{2,1,0:T(8,128)} %bitcast.26, ...), custom_call_target="tpu_custom_call" | custom-call | flops 6442450944 | bytes 12582912 | tf_op jit(solution)/shard_map/term/pallas_call | solution.py:67
  12.0 2.1 %collective-permute-start = (f32[8,16,1024]{2,1,0:T(8,128)}, f32[8,16,1024]{2,1,0:T(8,128)S(1)}, u32[]{:S(2)}, u32[]{:S(2)}) collective-permute-start(f32[8,16,1024]{2,1,0:T(8,128)} %get-tuple-element.18), channel_id=1, source_target_pairs={{0,8},{8,0},{16,24},{24,16},{1,9},{9,1},{17,25},{25,17},{2,10},{10... | collective-permute-start | bytes 1572872 | tf_op jit(solution)/shard_map/ppermute | solution.py:196
  14.1 2.6 %collective-permute-start.1 = (f32[8,16,1024]{2,1,0:T(8,128)}, f32[8,16,1024]{2,1,0:T(8,128)S(1)}, u32[]{:S(2)}, u32[]{:S(2)}) collective-permute-start(f32[8,16,1024]{2,1,0:T(8,128)} %get-tuple-element.19), channel_id=1, source_target_pairs={{0,16},{8,24},{16,0},{24,8},{1,17},{9,25},{17,1},{25,9},{2,18},{10... | collective-permute-start | bytes 1572872 | tf_op jit(solution)/shard_map/ppermute | solution.py:196
  16.8 7.6 %term.3 = (f32[8,16,512]{2,1,0:T(8,128)}, f32[8,16,512]{2,1,0:T(8,128)}, f32[8,16,512]{2,1,0:T(8,128)}, f32[8,16,512]{2,1,0:T(8,128)}) custom-call(s32[1]{0:T(128)} %bitcast.3.z_ref, s32[1]{0:T(128)} %bitcast.1.y_ref, f32[4,512,512]{2,1,0:T(8,128)} %bitcast.32, f32[4,512,1536]{2,1,0:T(8,128)} %bitcast.29, f32[4,512,1536]{2,1,0:T(8,128)} %bitcast.30), custom_call_target="tpu_custom_call" | custom-call | flops 3221225472 | bytes 8388608 | tf_op jit(solution)/shard_map/term/pallas_call | solution.py:67
  24.4 3.8 %collective-permute-start.11 = (f32[8,16,512]{2,1,0:T(8,128)}, f32[8,16,512]{2,1,0:T(8,128)S(1)}, u32[]{:S(2)}, u32[]{:S(2)}) collective-permute-start(f32[8,16,512]{2,1,0:T(8,128)} %get-tuple-element.25), channel_id=1, source_target_pairs={{0,16},{8,24},{16,0},{24,8},{1,17},{9,25},{17,1},{25,9},{2,18},{10... | collective-permute-start | bytes 786440 | tf_op jit(solution)/shard_map/ppermute | solution.py:196
  28.6 11.0 %collective-permute-done.1 = f32[8,16,1024]{2,1,0:T(8,128)S(1)} collective-permute-done((f32[8,16,1024]{2,1,0:T(8,128)}, f32[8,16,1024]{2,1,0:T(8,128)S(1)}, u32[]{:S(2)}, u32[]{:S(2)}) %collective-permute-start.1) | collective-permute-done | bytes 524320 | tf_op jit(solution)/shard_map/ppermute | solution.py:196
  39.6 1.7 %collective-permute-done.2 = f32[8,16,1024]{2,1,0:T(8,128)S(1)} collective-permute-done((f32[8,16,1024]{2,1,0:T(8,128)}, f32[8,16,1024]{2,1,0:T(8,128)S(1)}, u32[]{:S(2)}, u32[]{:S(2)}) %collective-permute-start.2) | collective-permute-done | bytes 524320 | tf_op jit(solution)/shard_map/ppermute | solution.py:196
  41.5 1.7 %collective-permute-start.3 = (f32[4,16,1024]{2,1,0:T(8,128)S(1)}, f32[4,16,1024]{2,1,0:T(8,128)S(1)}, u32[]{:S(2)}, u32[]{:S(2)}) collective-permute-start(f32[4,16,1024]{2,1,0:T(8,128)S(1)} %slice.137), channel_id=1, source_target_pairs={{0,32},{32,0},{64,96},{96,64},{128,160},{160,128},{192,224},{224,1... | collective-permute-start | bytes 786440 | tf_op jit(solution)/shard_map/ppermute | solution.py:196
  43.3 4.0 %collective-permute-done.3 = f32[4,16,1024]{2,1,0:T(8,128)S(1)} collective-permute-done((f32[4,16,1024]{2,1,0:T(8,128)S(1)}, f32[4,16,1024]{2,1,0:T(8,128)S(1)}, u32[]{:S(2)}, u32[]{:S(2)}) %collective-permute-start.3) | collective-permute-done | bytes 262176 | tf_op jit(solution)/shard_map/ppermute | solution.py:196
  47.3 3.1 %collective-permute-start.4 = (f32[2,16,1024]{2,1,0:T(8,128)S(1)}, f32[2,16,1024]{2,1,0:T(8,128)S(1)}, u32[]{:S(2)}, u32[]{:S(2)}) collective-permute-start(f32[2,16,1024]{2,1,0:T(8,128)S(1)} %slice.139), channel_id=1, source_target_pairs={{0,64},{32,96},{64,0},{96,32},{128,192},{160,224},{192,128},{224,1... | collective-permute-start | bytes 393224 | tf_op jit(solution)/shard_map/ppermute | solution.py:196
  50.4 2.9 %collective-permute-done.4 = f32[2,16,1024]{2,1,0:T(8,128)S(1)} collective-permute-done((f32[2,16,1024]{2,1,0:T(8,128)S(1)}, f32[2,16,1024]{2,1,0:T(8,128)S(1)}, u32[]{:S(2)}, u32[]{:S(2)}) %collective-permute-start.4) | collective-permute-done | bytes 131104 | tf_op jit(solution)/shard_map/ppermute | solution.py:196
  53.4 6.8 %collective-permute-start.5 = (f32[1,16,1024]{2,1,0:T(8,128)S(1)}, f32[1,16,1024]{2,1,0:T(8,128)S(1)}, u32[]{:S(2)}, u32[]{:S(2)}) collective-permute-start(f32[1,16,1024]{2,1,0:T(8,128)S(1)} %slice.141), channel_id=1, source_target_pairs={{0,128},{32,160},{64,192},{96,224},{128,0},{160,32},{192,64},{224,... | collective-permute-start | bytes 196616 | tf_op jit(solution)/shard_map/ppermute | solution.py:196
  60.6 1.3 collective-permute-done.5
  62.0 11.0 %collective-permute-start.6 = (f32[16,768]{1,0:T(8,128)S(1)}, f32[16,768]{1,0:T(8,128)S(1)}, u32[]{:S(2)}, u32[]{:S(2)}) collective-permute-start(f32[16,768]{1,0:T(8,128)S(1)} %pad_maximum_fusion.2), channel_id=1, source_target_pairs={{0,1},{1,0},{2,3},{3,2},{4,5},{5,4},{6,7},{7,6},{8,9},{9,8},{10,11... | collective-permute-start | bytes 147464 | tf_op jit(solution)/shard_map/ppermute | solution.py:196
  73.1 0.7 collective-permute-done.6
  73.9 0.7 collective-permute-start.9
  74.6 1.3 collective-permute-start.8
  75.9 0.7 collective-permute-start.7
  76.6 0.6 collective-permute-done.14
  77.2 6.3 %collective-permute-start.15 = (f32[1,16,512]{2,1,0:T(8,128)S(1)}, f32[1,16,512]{2,1,0:T(8,128)S(1)}, u32[]{:S(2)}, u32[]{:S(2)}) collective-permute-start(f32[1,16,512]{2,1,0:T(8,128)S(1)} %slice.155), channel_id=1, source_target_pairs={{0,128},{32,160},{64,192},{96,224},{128,0},{160,32},{192,64},{224,... | collective-permute-start | bytes 98312 | tf_op jit(solution)/shard_map/ppermute | solution.py:196
  83.5 0.9 broadcast_in_dim.9
  84.4 6.4 %all-to-all-start = ((f32[8,16,1280]{2,1,0:T(8,128)}), f32[8,16,1280]{2,1,0:T(8,128)S(1)}, u32[]{:S(2)}, u32[]{:S(2)}) async-start(f32[8,16,1280]{2,1,0:T(8,128)} %broadcast_in_dim.9), calls=%async_computation | async-start | bytes 1310720 | tf_op jit(solution)/shard_map/all_to_all | solution.py:227
  90.8 2.0 %collective-permute-start.16 = (f32[16,256]{1,0:T(8,128)S(1)}, f32[16,256]{1,0:T(8,128)S(1)}, u32[]{:S(2)}, u32[]{:S(2)}) collective-permute-start(f32[16,256]{1,0:T(8,128)S(1)} %slice_select_fusion.6), channel_id=1, source_target_pairs={{0,1},{1,0},{2,3},{3,2},{4,5},{5,4},{6,7},{7,6},{8,9},{9,8},{10,11... | collective-permute-start | bytes 49160 | tf_op jit(solution)/shard_map/ppermute | solution.py:196
  92.8 0.8 collective-permute-done.16
  93.7 0.7 collective-permute-start.19
  94.3 1.3 collective-permute-start.18
  95.6 0.7 collective-permute-start.17
  96.3 4.2 %collective-permute-done.18 = f32[16,512]{1,0:T(8,128)S(1)} collective-permute-done((f32[16,512]{1,0:T(8,128)S(1)}, f32[16,512]{1,0:T(8,128)S(1)}, u32[]{:S(2)}, u32[]{:S(2)}) %collective-permute-start.18) | collective-permute-done | bytes 32800 | tf_op jit(solution)/shard_map/ppermute | solution.py:222
  100.9 3.1 %collective-permute-start.20 = (f32[16,512]{1,0:T(8,128)S(1)}, f32[16,512]{1,0:T(8,128)S(1)}, u32[]{:S(2)}, u32[]{:S(2)}) collective-permute-start(f32[16,512]{1,0:T(8,128)S(1)} %add_select_fusion.1), channel_id=1, source_target_pairs={{0,8},{8,0},{16,24},{24,16},{1,9},{9,1},{17,25},{25,17},{2,10},{10... | collective-permute-start | bytes 98312 | tf_op jit(solution)/shard_map/ppermute | solution.py:196
  104.1 1.0 collective-permute-done.22
  105.1 0.4 collective-permute-done.21
  105.5 0.5 collective-permute-done.20
  106.0 3.9 %all-to-all-done.refs_1_.refs_0_.refs_5_ = f32[8,16,1280]{2,1,0:T(8,128)S(1)} async-done(((f32[8,16,1280]{2,1,0:T(8,128)}), f32[8,16,1280]{2,1,0:T(8,128)S(1)}, u32[]{:S(2)}, u32[]{:S(2)}) %all-to-all-start) | async-done | bytes 655392 | tf_op jit(solution)/shard_map/all_to_all | solution.py:227
  110.0 1.3 collective-permute-start.23
  111.3 1.1 broadcast_in_dim.10
  112.4 3.6 %all-to-all-start.1 = ((f32[8,4,16,512]{3,2,1,0:T(8,128)}), f32[8,4,16,512]{3,2,1,0:T(8,128)S(1)}, u32[]{:S(2)}, u32[]{:S(2)}) async-start(f32[8,4,16,512]{3,2,1,0:T(8,128)} %broadcast_in_dim.10), calls=%async_computation.1 | async-start | bytes 2097152 | tf_op jit(solution)/shard_map/all_to_all | solution.py:227
  116.0 7.9 %collective-permute-done.24.refs_3_.refs_2_.refs_7_ = f32[8,16,1280]{2,1,0:T(8,128)S(1)} collective-permute-done((f32[8,16,1280]{2,1,0:T(8,128)S(1)}, f32[8,16,1280]{2,1,0:T(8,128)S(1)}, u32[]{:S(2)}, u32[]{:S(2)}) %collective-permute-start.24) | collective-permute-done | bytes 655392 | tf_op jit(solution)/shard_map/ppermute | solution.py:236
  123.9 1.5 collective-permute-start.26
  125.6 7.3 %collective-permute-done.25.refs_4_.refs_3_.refs_8_ = f32[4,16,1280]{2,1,0:T(8,128)S(1)} collective-permute-done((f32[4,16,1280]{2,1,0:T(8,128)S(1)}, f32[4,16,1280]{2,1,0:T(8,128)S(1)}, u32[]{:S(2)}, u32[]{:S(2)}) %collective-permute-start.25) | collective-permute-done | bytes 327712 | tf_op jit(solution)/shard_map/ppermute | solution.py:236
  132.9 0.7 copy-done.8
  133.6 4.3 %collective-permute-start.27 = (f32[4,8,16,256]{3,2,1,0:T(8,128)S(1)}, f32[4,8,16,256]{3,2,1,0:T(8,128)}, u32[]{:S(2)}, u32[]{:S(2)}) collective-permute-start(f32[4,8,16,256]{3,2,1,0:T(8,128)S(1)} %bitcast.36), channel_id=1, source_target_pairs={{0,1},{1,0},{2,3},{3,2},{4,5},{5,4},{6,7},{7,6},{8,9},{9,8},{10,11... | collective-permute-start | bytes 1572872 | tf_op jit(solution)/shard_map/ppermute | solution.py:196
  137.9 1.7 %collective-permute-done.27.other_hbm = f32[4,8,16,256]{3,2,1,0:T(8,128)} collective-permute-done((f32[4,8,16,256]{3,2,1,0:T(8,128)S(1)}, f32[4,8,16,256]{3,2,1,0:T(8,128)}, u32[]{:S(2)}, u32[]{:S(2)}) %collective-permute-start.27) | collective-permute-done | bytes 524320 | tf_op jit(solution)/shard_map/ppermute | solution.py:196
  139.6 5.9 %solve.3.own = f32[2,512,512]{2,1,0:T(8,128)} custom-call(s32[1]{0:T(128)} %bitcast.1.y_ref, s32[1]{0:T(128)} %bitcast.core_ref, f32[2,512,512]{2,1,0:T(8,128)} %inv_hbm.3, f32[4,8,16,256]{3,2,1,0:T(8,128)} %collective-permute-done.27.other_hbm, f32[8,16,1280]{2,1,0:T(8,128)} %copy-done.3, f32[8,16,1280]{2,1,0:T(8,128)} %copy-done.5, ...), custom_call_target="tpu_custom_call" | custom-call | flops 2415919104 | bytes 6291456 | tf_op jit(solution)/shard_map/solve/pallas_call | solution.py:132
  145.6 0.5 collective-permute-start.29
  146.0 1.0 copy-done.6
  147.0 5.1 %solve.2.own = f32[2,512,256]{2,1,0:T(8,128)} custom-call(s32[1]{0:T(128)} %bitcast.1.y_ref, s32[1]{0:T(128)} %bitcast.core_ref, f32[2,512,512]{2,1,0:T(8,128)} %inv_hbm.3, f32[4,8,16,256]{3,2,1,0:T(8,128)} %collective-permute-done.27.other_hbm, f32[8,4,16,512]{3,2,1,0:T(8,128)} %copy-done.6, f32[8,16,1280]{2,1,0:T(8,128)} %copy-done.3, ...), custom_call_target="tpu_custom_call" | custom-call | flops 1207959552 | bytes 6291456 | tf_op jit(solution)/shard_map/solve/pallas_call | solution.py:132
  152.4 3.7 %finish.2 = (f32[2,512,1536]{2,1,0:T(8,128)}, f32[16,1536]{1,0:T(8,128)S(1)}) custom-call(s32[1]{0:T(128)} %bitcast.core_ref, f32[2,512,512]{2,1,0:T(8,128)S(1)} %copy-done, f32[2,512,512]{2,1,0:T(8,128)} %collective-permute-done.29.other, f32[16,1024]{1,0:T(8,128)S(1)} %fusion.1.base, f32[2,16,512]{2,1,0:T(8,128)S(1)} %bitcast.23), custom_call_target="tpu_custom_call" | custom-call | flops 100663296 | bytes 6291456 | tf_op jit(solution)/shard_map/finish/pallas_call | solution.py:176
  156.1 2.3 %finish.3 = (f32[2,512,1536]{2,1,0:T(8,128)}, f32[16,1536]{1,0:T(8,128)}) custom-call(s32[1]{0:T(128)} %bitcast.core_ref, f32[2,512,256]{2,1,0:T(8,128)S(1)} %copy-done.1, f32[2,512,256]{2,1,0:T(8,128)S(1)} %collective-permute-done.28.other, f32[16,512]{1,0:T(8,128)S(1)} %fusion.3.base, f32[2,16,512]{2,1,0:T(8,128)S(1)} %bitcast.24, ...), custom_call_target="tpu_custom_call", output_to_operand_aliasing={{0}: (5, {})} | custom-call | flops 50331648 | bytes 6291456 | tf_op jit(solution)/shard_map/finish/pallas_call | solution.py:176
  (84 shorter events, 2.3 us)
Async XLA Ops:
  12.0 16.2 %collective-permute-start = (f32[8,16,1024]{2,1,0:T(8,128)}, f32[8,16,1024]{2,1,0:T(8,128)S(1)}, u32[]{:S(2)}, u32[]{:S(2)}) collective-permute-start(f32[8,16,1024]{2,1,0:T(8,128)} %get-tuple-element.18), channel_id=1, source_target_pairs={{0,8},{8,0},{16,24},{24,16},{1,9},{9,1},{17,25},{25,17},{2,10},{10... | collective-permute-start | bytes 1572872 | tf_op jit(solution)/shard_map/ppermute | solution.py:196
  14.1 25.4 %collective-permute-start.1 = (f32[8,16,1024]{2,1,0:T(8,128)}, f32[8,16,1024]{2,1,0:T(8,128)S(1)}, u32[]{:S(2)}, u32[]{:S(2)}) collective-permute-start(f32[8,16,1024]{2,1,0:T(8,128)} %get-tuple-element.19), channel_id=1, source_target_pairs={{0,16},{8,24},{16,0},{24,8},{1,17},{9,25},{17,1},{25,9},{2,18},{10... | collective-permute-start | bytes 1572872 | tf_op jit(solution)/shard_map/ppermute | solution.py:196
  16.8 24.5 %collective-permute-start.2 = (f32[8,16,1024]{2,1,0:T(8,128)}, f32[8,16,1024]{2,1,0:T(8,128)S(1)}, u32[]{:S(2)}, u32[]{:S(2)}) collective-permute-start(f32[8,16,1024]{2,1,0:T(8,128)} %get-tuple-element.20), channel_id=1, source_target_pairs={{0,24},{8,16},{16,8},{24,0},{1,25},{9,17},{17,9},{25,1},{2,26},{10... | collective-permute-start | bytes 1572872 | tf_op jit(solution)/shard_map/ppermute | solution.py:196
  16.8 24.5 %copy-start.9 = (f32[8,16,1024]{2,1,0:T(8,128)S(1)}, f32[8,16,1024]{2,1,0:T(8,128)}, u32[]{:S(2)}) copy-start(f32[8,16,1024]{2,1,0:T(8,128)} %get-tuple-element.17) | copy-start | bytes 1572868
  16.8 26.5 %copy-start.2 = (f32[1,1,2,16,512]{4,3,2,1,0:T(8,128)S(1)}, f32[1,1,2,16,512]{4,3,2,1,0:T(8,128)}, u32[]{:S(2)}) copy-start(f32[1,1,2,16,512]{4,3,2,1,0:T(8,128)} %param.8) | copy-start | bytes 196612
  16.8 26.5 %copy-start.11 = (f32[1,1,16,1536]{3,2,1,0:T(8,128)S(1)}, f32[1,1,16,1536]{3,2,1,0:T(8,128)}, u32[]{:S(2)}) copy-start(f32[1,1,16,1536]{3,2,1,0:T(8,128)} %param.7) | copy-start | bytes 294916
  24.4 35.8 %copy-start.10 = (f32[8,16,512]{2,1,0:T(8,128)S(1)}, f32[8,16,512]{2,1,0:T(8,128)}, u32[]{:S(2)}) copy-start(f32[8,16,512]{2,1,0:T(8,128)} %get-tuple-element.23) | copy-start | bytes 786436
  24.4 35.8 %collective-permute-start.10 = (f32[8,16,512]{2,1,0:T(8,128)}, f32[8,16,512]{2,1,0:T(8,128)S(1)}, u32[]{:S(2)}, u32[]{:S(2)}) collective-permute-start(f32[8,16,512]{2,1,0:T(8,128)} %get-tuple-element.24), channel_id=1, source_target_pairs={{0,8},{8,0},{16,24},{24,16},{1,9},{9,1},{17,25},{25,17},{2,10},{10... | collective-permute-start | bytes 786440 | tf_op jit(solution)/shard_map/ppermute | solution.py:196
  24.4 35.8 %collective-permute-start.11 = (f32[8,16,512]{2,1,0:T(8,128)}, f32[8,16,512]{2,1,0:T(8,128)S(1)}, u32[]{:S(2)}, u32[]{:S(2)}) collective-permute-start(f32[8,16,512]{2,1,0:T(8,128)} %get-tuple-element.25), channel_id=1, source_target_pairs={{0,16},{8,24},{16,0},{24,8},{1,17},{9,25},{17,1},{25,9},{2,18},{10... | collective-permute-start | bytes 786440 | tf_op jit(solution)/shard_map/ppermute | solution.py:196
  28.2 32.0 %collective-permute-start.12 = (f32[8,16,512]{2,1,0:T(8,128)}, f32[8,16,512]{2,1,0:T(8,128)S(1)}, u32[]{:S(2)}, u32[]{:S(2)}) collective-permute-start(f32[8,16,512]{2,1,0:T(8,128)} %get-tuple-element.26), channel_id=1, source_target_pairs={{0,24},{8,16},{16,8},{24,0},{1,25},{9,17},{17,9},{25,1},{2,26},{10... | collective-permute-start | bytes 786440 | tf_op jit(solution)/shard_map/ppermute | solution.py:196
  41.5 5.8 %collective-permute-start.3 = (f32[4,16,1024]{2,1,0:T(8,128)S(1)}, f32[4,16,1024]{2,1,0:T(8,128)S(1)}, u32[]{:S(2)}, u32[]{:S(2)}) collective-permute-start(f32[4,16,1024]{2,1,0:T(8,128)S(1)} %slice.137), channel_id=1, source_target_pairs={{0,32},{32,0},{64,96},{96,64},{128,160},{160,128},{192,224},{224,1... | collective-permute-start | bytes 786440 | tf_op jit(solution)/shard_map/ppermute | solution.py:196
  47.3 6.0 %collective-permute-start.4 = (f32[2,16,1024]{2,1,0:T(8,128)S(1)}, f32[2,16,1024]{2,1,0:T(8,128)S(1)}, u32[]{:S(2)}, u32[]{:S(2)}) collective-permute-start(f32[2,16,1024]{2,1,0:T(8,128)S(1)} %slice.139), channel_id=1, source_target_pairs={{0,64},{32,96},{64,0},{96,32},{128,192},{160,224},{192,128},{224,1... | collective-permute-start | bytes 393224 | tf_op jit(solution)/shard_map/ppermute | solution.py:196
  53.4 8.6 %collective-permute-start.5 = (f32[1,16,1024]{2,1,0:T(8,128)S(1)}, f32[1,16,1024]{2,1,0:T(8,128)S(1)}, u32[]{:S(2)}, u32[]{:S(2)}) collective-permute-start(f32[1,16,1024]{2,1,0:T(8,128)S(1)} %slice.141), channel_id=1, source_target_pairs={{0,128},{32,160},{64,192},{96,224},{128,0},{160,32},{192,64},{224,... | collective-permute-start | bytes 196616 | tf_op jit(solution)/shard_map/ppermute | solution.py:196
  60.3 12.7 %collective-permute-start.13 = (f32[4,16,512]{2,1,0:T(8,128)S(1)}, f32[4,16,512]{2,1,0:T(8,128)S(1)}, u32[]{:S(2)}, u32[]{:S(2)}) collective-permute-start(f32[4,16,512]{2,1,0:T(8,128)S(1)} %slice.151), channel_id=1, source_target_pairs={{0,224},{32,64},{64,32},{96,128},{128,96},{160,192},{192,160},{224... | collective-permute-start | bytes 393224 | tf_op jit(solution)/shard_map/ppermute | solution.py:196
  62.0 11.9 %collective-permute-start.6 = (f32[16,768]{1,0:T(8,128)S(1)}, f32[16,768]{1,0:T(8,128)S(1)}, u32[]{:S(2)}, u32[]{:S(2)}) collective-permute-start(f32[16,768]{1,0:T(8,128)S(1)} %pad_maximum_fusion.2), channel_id=1, source_target_pairs={{0,1},{1,0},{2,3},{3,2},{4,5},{5,4},{6,7},{7,6},{8,9},{9,8},{10,11... | collective-permute-start | bytes 147464 | tf_op jit(solution)/shard_map/ppermute | solution.py:196
  73.0 4.1 %collective-permute-start.14 = (f32[2,16,512]{2,1,0:T(8,128)S(1)}, f32[2,16,512]{2,1,0:T(8,128)S(1)}, u32[]{:S(2)}, u32[]{:S(2)}) collective-permute-start(f32[2,16,512]{2,1,0:T(8,128)S(1)} %slice.153), channel_id=1, source_target_pairs={{0,64},{32,224},{64,0},{96,160},{128,192},{160,96},{192,128},{224,... | collective-permute-start | bytes 196616 | tf_op jit(solution)/shard_map/ppermute | solution.py:196
  73.9 9.6 %collective-permute-start.9 = (f32[16,1280]{1,0:T(8,128)S(1)}, f32[16,1280]{1,0:T(8,128)S(1)}, u32[]{:S(2)}, u32[]{:S(2)}) collective-permute-start(f32[16,1280]{1,0:T(8,128)S(1)} %pad_maximum_fusion.1), channel_id=1, source_target_pairs={{6,2},{7,3},{14,10},{15,11},{22,18},{23,19},{30,26},{31,27},{38,34... | collective-permute-start | bytes 245768 | tf_op jit(solution)/shard_map/ppermute | solution.py:222
  74.6 8.9 %collective-permute-start.8 = (f32[16,1280]{1,0:T(8,128)S(1)}, f32[16,1280]{1,0:T(8,128)S(1)}, u32[]{:S(2)}, u32[]{:S(2)}) collective-permute-start(f32[16,1280]{1,0:T(8,128)S(1)} %pad_maximum_fusion.1), channel_id=1, source_target_pairs={{6,0},{7,1},{14,8},{15,9},{22,16},{23,17},{30,24},{31,25},{38,32},... | collective-permute-start | bytes 245768 | tf_op jit(solution)/shard_map/ppermute | solution.py:222
  75.9 7.6 %collective-permute-start.7 = (f32[16,1280]{1,0:T(8,128)S(1)}, f32[16,1280]{1,0:T(8,128)S(1)}, u32[]{:S(2)}, u32[]{:S(2)}) collective-permute-start(f32[16,1280]{1,0:T(8,128)S(1)} %pad_maximum_fusion.1), channel_id=1, source_target_pairs={{6,4},{7,5},{14,12},{15,13},{22,20},{23,21},{30,28},{31,29},{38,36... | collective-permute-start | bytes 245768 | tf_op jit(solution)/shard_map/ppermute | solution.py:222
  77.2 13.6 %collective-permute-start.15 = (f32[1,16,512]{2,1,0:T(8,128)S(1)}, f32[1,16,512]{2,1,0:T(8,128)S(1)}, u32[]{:S(2)}, u32[]{:S(2)}) collective-permute-start(f32[1,16,512]{2,1,0:T(8,128)S(1)} %slice.155), channel_id=1, source_target_pairs={{0,128},{32,160},{64,192},{96,224},{128,0},{160,32},{192,64},{224,... | collective-permute-start | bytes 98312 | tf_op jit(solution)/shard_map/ppermute | solution.py:196
  84.4 25.4 %all-to-all-start = ((f32[8,16,1280]{2,1,0:T(8,128)}), f32[8,16,1280]{2,1,0:T(8,128)S(1)}, u32[]{:S(2)}, u32[]{:S(2)}) async-start(f32[8,16,1280]{2,1,0:T(8,128)} %broadcast_in_dim.9), calls=%async_computation | async-start | bytes 1310720 | tf_op jit(solution)/shard_map/all_to_all | solution.py:227
  90.8 2.9 %collective-permute-start.16 = (f32[16,256]{1,0:T(8,128)S(1)}, f32[16,256]{1,0:T(8,128)S(1)}, u32[]{:S(2)}, u32[]{:S(2)}) collective-permute-start(f32[16,256]{1,0:T(8,128)S(1)} %slice_select_fusion.6), channel_id=1, source_target_pairs={{0,1},{1,0},{2,3},{3,2},{4,5},{5,4},{6,7},{7,6},{8,9},{9,8},{10,11... | collective-permute-start | bytes 49160 | tf_op jit(solution)/shard_map/ppermute | solution.py:196
  93.7 2.6 %collective-permute-start.19 = (f32[16,512]{1,0:T(8,128)S(1)}, f32[16,512]{1,0:T(8,128)S(1)}, u32[]{:S(2)}, u32[]{:S(2)}) collective-permute-start(f32[16,512]{1,0:T(8,128)S(1)} %pad_maximum_fusion.3), channel_id=1, source_target_pairs={{6,2},{7,3},{14,10},{15,11},{22,18},{23,19},{30,26},{31,27},{38,34... | collective-permute-start | bytes 98312 | tf_op jit(solution)/shard_map/ppermute | solution.py:222
  94.3 6.2 %collective-permute-start.18 = (f32[16,512]{1,0:T(8,128)S(1)}, f32[16,512]{1,0:T(8,128)S(1)}, u32[]{:S(2)}, u32[]{:S(2)}) collective-permute-start(f32[16,512]{1,0:T(8,128)S(1)} %pad_maximum_fusion.3), channel_id=1, source_target_pairs={{6,0},{7,1},{14,8},{15,9},{22,16},{23,17},{30,24},{31,25},{38,32},... | collective-permute-start | bytes 98312 | tf_op jit(solution)/shard_map/ppermute | solution.py:222
  95.6 4.9 %collective-permute-start.17 = (f32[16,512]{1,0:T(8,128)S(1)}, f32[16,512]{1,0:T(8,128)S(1)}, u32[]{:S(2)}, u32[]{:S(2)}) collective-permute-start(f32[16,512]{1,0:T(8,128)S(1)} %pad_maximum_fusion.3), channel_id=1, source_target_pairs={{6,4},{7,5},{14,12},{15,13},{22,20},{23,21},{30,28},{31,29},{38,36... | collective-permute-start | bytes 98312 | tf_op jit(solution)/shard_map/ppermute | solution.py:222
  100.5 4.5 %collective-permute-start.22 = (f32[16,512]{1,0:T(8,128)S(1)}, f32[16,512]{1,0:T(8,128)S(1)}, u32[]{:S(2)}, u32[]{:S(2)}) collective-permute-start(f32[16,512]{1,0:T(8,128)S(1)} %add_select_fusion.1), channel_id=1, source_target_pairs={{0,24},{8,16},{16,8},{24,0},{1,25},{9,17},{17,9},{25,1},{2,26},{10... | collective-permute-start | bytes 98312 | tf_op jit(solution)/shard_map/ppermute | solution.py:196
  100.9 4.6 %collective-permute-start.21 = (f32[16,512]{1,0:T(8,128)S(1)}, f32[16,512]{1,0:T(8,128)S(1)}, u32[]{:S(2)}, u32[]{:S(2)}) collective-permute-start(f32[16,512]{1,0:T(8,128)S(1)} %add_select_fusion.1), channel_id=1, source_target_pairs={{0,16},{8,24},{16,0},{24,8},{1,17},{9,25},{17,1},{25,9},{2,18},{10... | collective-permute-start | bytes 98312 | tf_op jit(solution)/shard_map/ppermute | solution.py:196
  100.9 5.0 %collective-permute-start.20 = (f32[16,512]{1,0:T(8,128)S(1)}, f32[16,512]{1,0:T(8,128)S(1)}, u32[]{:S(2)}, u32[]{:S(2)}) collective-permute-start(f32[16,512]{1,0:T(8,128)S(1)} %add_select_fusion.1), channel_id=1, source_target_pairs={{0,8},{8,0},{16,24},{24,16},{1,9},{9,1},{17,25},{25,17},{2,10},{10... | collective-permute-start | bytes 98312 | tf_op jit(solution)/shard_map/ppermute | solution.py:196
  109.8 29.8 %copy-start.3 = (f32[8,16,1280]{2,1,0:T(8,128)}, f32[8,16,1280]{2,1,0:T(8,128)S(1)}, u32[]{:S(2)}) copy-start(f32[8,16,1280]{2,1,0:T(8,128)S(1)} %all-to-all-done.refs_1_.refs_0_.refs_5_) | copy-start | bytes 1966084
  109.8 14.0 %collective-permute-start.24 = (f32[8,16,1280]{2,1,0:T(8,128)S(1)}, f32[8,16,1280]{2,1,0:T(8,128)S(1)}, u32[]{:S(2)}, u32[]{:S(2)}) collective-permute-start(f32[8,16,1280]{2,1,0:T(8,128)S(1)} %all-to-all-done.refs_1_.refs_0_.refs_5_), channel_id=1, source_target_pairs={{0,24},{8,0},{16,8},{24,16},{1,25},{9,1},{17,9},{25,17},{2,26},{10... | collective-permute-start | bytes 1966088 | tf_op jit(solution)/shard_map/ppermute | solution.py:236
  110.0 15.4 %collective-permute-start.23 = (f32[8,16,1280]{2,1,0:T(8,128)S(1)}, f32[8,16,1280]{2,1,0:T(8,128)S(1)}, u32[]{:S(2)}, u32[]{:S(2)}) collective-permute-start(f32[8,16,1280]{2,1,0:T(8,128)S(1)} %all-to-all-done.refs_1_.refs_0_.refs_5_), channel_id=1, source_target_pairs={{0,8},{8,16},{16,24},{24,0},{1,9},{9,17},{17,25},{25,1},{2,10},{10... | collective-permute-start | bytes 1966088 | tf_op jit(solution)/shard_map/ppermute | solution.py:236
  112.4 33.6 %all-to-all-start.1 = ((f32[8,4,16,512]{3,2,1,0:T(8,128)}), f32[8,4,16,512]{3,2,1,0:T(8,128)S(1)}, u32[]{:S(2)}, u32[]{:S(2)}) async-start(f32[8,4,16,512]{3,2,1,0:T(8,128)} %broadcast_in_dim.10), calls=%async_computation.1 | async-start | bytes 2097152 | tf_op jit(solution)/shard_map/all_to_all | solution.py:227
  123.9 15.8 %copy-start.4 = (f32[8,16,1280]{2,1,0:T(8,128)}, f32[8,16,1280]{2,1,0:T(8,128)S(1)}, u32[]{:S(2)}) copy-start(f32[8,16,1280]{2,1,0:T(8,128)S(1)} %collective-permute-done.24.refs_3_.refs_2_.refs_7_) | copy-start | bytes 1966084
  123.9 9.0 %collective-permute-start.26 = (f32[4,16,1280]{2,1,0:T(8,128)S(1)}, f32[4,16,1280]{2,1,0:T(8,128)S(1)}, u32[]{:S(2)}, u32[]{:S(2)}) collective-permute-start(f32[4,16,1280]{2,1,0:T(8,128)S(1)} %slice.162), channel_id=1, source_target_pairs={{0,24},{8,0},{16,8},{24,16},{1,25},{9,1},{17,9},{25,17},{2,26},{10... | collective-permute-start | bytes 983048 | tf_op jit(solution)/shard_map/ppermute | solution.py:236
  125.4 14.3 %copy-start.5 = (f32[8,16,1280]{2,1,0:T(8,128)}, f32[8,16,1280]{2,1,0:T(8,128)S(1)}, u32[]{:S(2)}) copy-start(f32[8,16,1280]{2,1,0:T(8,128)S(1)} %collective-permute-done.23.refs_2_.refs_1_.refs_6_) | copy-start | bytes 1966084
  125.4 7.5 %collective-permute-start.25 = (f32[4,16,1280]{2,1,0:T(8,128)S(1)}, f32[4,16,1280]{2,1,0:T(8,128)S(1)}, u32[]{:S(2)}, u32[]{:S(2)}) collective-permute-start(f32[4,16,1280]{2,1,0:T(8,128)S(1)} %slice.160), channel_id=1, source_target_pairs={{0,8},{8,16},{16,24},{24,0},{1,9},{9,17},{17,25},{25,1},{2,10},{10... | collective-permute-start | bytes 983048 | tf_op jit(solution)/shard_map/ppermute | solution.py:236
  132.9 0.7 copy-start.8
  133.6 6.0 %copy-start.7 = (f32[4,16,1280]{2,1,0:T(8,128)}, f32[4,16,1280]{2,1,0:T(8,128)S(1)}, u32[]{:S(2)}) copy-start(f32[4,16,1280]{2,1,0:T(8,128)S(1)} %collective-permute-done.26.refs_5_.refs_4_.refs_9_) | copy-start | bytes 983044
  133.6 6.0 %collective-permute-start.27 = (f32[4,8,16,256]{3,2,1,0:T(8,128)S(1)}, f32[4,8,16,256]{3,2,1,0:T(8,128)}, u32[]{:S(2)}, u32[]{:S(2)}) collective-permute-start(f32[4,8,16,256]{3,2,1,0:T(8,128)S(1)} %bitcast.36), channel_id=1, source_target_pairs={{0,1},{1,0},{2,3},{3,2},{4,5},{5,4},{6,7},{7,6},{8,9},{9,8},{10,11... | collective-permute-start | bytes 1572872 | tf_op jit(solution)/shard_map/ppermute | solution.py:196
  145.5 6.8 %copy-start = (f32[2,512,512]{2,1,0:T(8,128)S(1)}, f32[2,512,512]{2,1,0:T(8,128)}, u32[]{:S(2)}) copy-start(f32[2,512,512]{2,1,0:T(8,128)} %solve.3.own) | copy-start | bytes 6291460
  145.6 6.8 %collective-permute-start.29 = (f32[2,512,512]{2,1,0:T(8,128)}, f32[2,512,512]{2,1,0:T(8,128)}, u32[]{:S(2)}, u32[]{:S(2)}) collective-permute-start(f32[2,512,512]{2,1,0:T(8,128)} %solve.3.own), channel_id=1, source_target_pairs={{0,1},{1,0},{2,3},{3,2},{4,5},{5,4},{6,7},{7,6},{8,9},{9,8},{10,11... | collective-permute-start | bytes 6291464 | tf_op jit(solution)/shard_map/ppermute | solution.py:196
  146.0 1.0 copy-start.6
  152.1 4.0 %copy-start.1 = (f32[2,512,256]{2,1,0:T(8,128)S(1)}, f32[2,512,256]{2,1,0:T(8,128)}, u32[]{:S(2)}) copy-start(f32[2,512,256]{2,1,0:T(8,128)} %solve.2.own) | copy-start | bytes 3145732
  152.1 3.9 %collective-permute-start.28 = (f32[2,512,256]{2,1,0:T(8,128)}, f32[2,512,256]{2,1,0:T(8,128)S(1)}, u32[]{:S(2)}, u32[]{:S(2)}) collective-permute-start(f32[2,512,256]{2,1,0:T(8,128)} %solve.2.own), channel_id=1, source_target_pairs={{0,1},{1,0},{2,3},{3,2},{4,5},{5,4},{6,7},{7,6},{8,9},{9,8},{10,11... | collective-permute-start | bytes 3145736 | tf_op jit(solution)/shard_map/ppermute | solution.py:196

commit v6 on v5

--- a/solution.py
+++ b/solution.py
@@ -202,7 +202,7 @@
 
 def sum_y(slabs):
     near = slabs[0]
-    for ky in range(1, NY):
+    for ky in (1, 3, 2):
         near = near + swap(slabs[ky], "y", ky)
     return near
 

time: 159 us -> 158 us (level)
  waiting for transfers between devices: 50 us -> 45 us
  starting transfers between devices: 67 us -> 71.1 us
    ppermute x4, starting transfers between devices: 3.09 us -> 8.33 us  [step(): return lax.ppermute(x, axis, [(i, (i + by) % n) for i in range(n)])]
    all_to_all x2, waiting for transfers between devices: 3.87 us -> 0.01 us  [gather_z(): lax.all_to_all(jnp.broadcast_to(v, (NZ, *v.shape)), 'z', 0, 0, tiled=True)]
  transfers between devices with their start and end apart: 32 -> 32, of which waited for: 16 -> 14; matrix products, arithmetic and copies ran while one was open for 2% -> 2% of each run, Pallas kernels for 14% -> 14%
where the time goes in v6:
time: 158 us
  starting transfers between devices  71.1 us (45%)
  waiting for transfers between devices  45 us (28%)
  Pallas kernels  36.1 us (23%)
  local copies, waits for them, and re-layouts  3.86 us (2%)
    ppermute x20, starting transfers between devices, swap(): lax.ppermute(x, axis, [(i, (((i + shift) % n ^ bit) - shift) % n) for i i...  47.4 us
    ppermute x20, waiting for transfers between devices, swap(): lax.ppermute(x, axis, [(i, (((i + shift) % n ^ bit) - shift) % n) for i i...  26.6 us
    pallas_call x2, Pallas kernels, term(): pl.pallas_call(functools.partial(term_kernel, part), grid_spec=pltpu.Pref...  19 us
    ppermute x4, waiting for transfers between devices, step(): return lax.ppermute(x, axis, [(i, (i + by) % n) for i in range(n)])  14.4 us
    pallas_call x2, Pallas kernels, solve(): pl.pallas_call(functools.partial(solve_kernel, n), in_specs=[scalar] * 2...  11 us
    all_to_all x2, starting transfers between devices, gather_z(): lax.all_to_all(jnp.broadcast_to(v, (NZ, *v.shape)), 'z', 0, 0, tiled=True)  10 us
    ppermute x4, starting transfers between devices, step(): return lax.ppermute(x, axis, [(i, (i + by) % n) for i in range(n)])  8.33 us
    pallas_call x2, Pallas kernels, finish(): pl.pallas_call(functools.partial(finish_kernel, chunk), in_specs=[pl.Bloc...  6.06 us
  transfers between devices with their start and end apart: 32, of which 14 were waited for; matrix products, arithmetic and copies ran while one was open for 2% of the time, Pallas kernels for 14%

profile of v6, /device:TPU:1, one launch (start us, length us, event | category | flops | bytes accessed | tf_op | source)
XLA Modules:
  0.0 157.6 jit_solution(2095052678537161541)
XLA Ops:
  0.6 11.4 %term.2 = (f32[8,16,1024]{2,1,0:T(8,128)}, f32[8,16,1024]{2,1,0:T(8,128)}, f32[8,16,1024]{2,1,0:T(8,128)}, f32[8,16,1024]{2,1,0:T(8,128)}) custom-call(s32[1]{0:T(128)} %bitcast.3.z_ref, s32[1]{0:T(128)} %bitcast.1.y_ref, f32[4,512,512]{2,1,0:T(8,128)} %bitcast.31, f32[4,512,1536]{2,1,0:T(8,128)} %bitcast.25, f32[4,512,1536]{2,1,0:T(8,128)} %bitcast.26, ...), custom_call_target="tpu_custom_call" | custom-call | flops 6442450944 | bytes 12582912 | tf_op jit(solution)/shard_map/term/pallas_call | solution.py:67
  12.0 2.1 %collective-permute-start = (f32[8,16,1024]{2,1,0:T(8,128)}, f32[8,16,1024]{2,1,0:T(8,128)S(1)}, u32[]{:S(2)}, u32[]{:S(2)}) collective-permute-start(f32[8,16,1024]{2,1,0:T(8,128)} %get-tuple-element.18), channel_id=1, source_target_pairs={{0,8},{8,0},{16,24},{24,16},{1,9},{9,1},{17,25},{25,17},{2,10},{10... | collective-permute-start | bytes 1572872 | tf_op jit(solution)/shard_map/ppermute | solution.py:196
  14.1 1.9 %collective-permute-start.1 = (f32[8,16,1024]{2,1,0:T(8,128)}, f32[8,16,1024]{2,1,0:T(8,128)S(1)}, u32[]{:S(2)}, u32[]{:S(2)}) collective-permute-start(f32[8,16,1024]{2,1,0:T(8,128)} %get-tuple-element.19), channel_id=1, source_target_pairs={{0,24},{8,16},{16,8},{24,0},{1,25},{9,17},{17,9},{25,1},{2,26},{10... | collective-permute-start | bytes 1572872 | tf_op jit(solution)/shard_map/ppermute | solution.py:196
  16.0 0.7 collective-permute-start.2
  16.8 7.6 %term.3 = (f32[8,16,512]{2,1,0:T(8,128)}, f32[8,16,512]{2,1,0:T(8,128)}, f32[8,16,512]{2,1,0:T(8,128)}, f32[8,16,512]{2,1,0:T(8,128)}) custom-call(s32[1]{0:T(128)} %bitcast.3.z_ref, s32[1]{0:T(128)} %bitcast.1.y_ref, f32[4,512,512]{2,1,0:T(8,128)} %bitcast.32, f32[4,512,1536]{2,1,0:T(8,128)} %bitcast.29, f32[4,512,1536]{2,1,0:T(8,128)} %bitcast.30), custom_call_target="tpu_custom_call" | custom-call | flops 3221225472 | bytes 8388608 | tf_op jit(solution)/shard_map/term/pallas_call | solution.py:67
  24.4 0.6 collective-permute-start.10
  25.0 1.9 %collective-permute-start.11 = (f32[8,16,512]{2,1,0:T(8,128)}, f32[8,16,512]{2,1,0:T(8,128)S(1)}, u32[]{:S(2)}, u32[]{:S(2)}) collective-permute-start(f32[8,16,512]{2,1,0:T(8,128)} %get-tuple-element.25), channel_id=1, source_target_pairs={{0,24},{8,16},{16,8},{24,0},{1,25},{9,17},{17,9},{25,1},{2,26},{10... | collective-permute-start | bytes 786440 | tf_op jit(solution)/shard_map/ppermute | solution.py:196
  26.9 1.8 %collective-permute-start.12 = (f32[8,16,512]{2,1,0:T(8,128)}, f32[8,16,512]{2,1,0:T(8,128)S(1)}, u32[]{:S(2)}, u32[]{:S(2)}) collective-permute-start(f32[8,16,512]{2,1,0:T(8,128)} %get-tuple-element.26), channel_id=1, source_target_pairs={{0,16},{8,24},{16,0},{24,8},{1,17},{9,25},{17,1},{25,9},{2,18},{10... | collective-permute-start | bytes 786440 | tf_op jit(solution)/shard_map/ppermute | solution.py:196
  28.8 6.2 %collective-permute-done.1 = f32[8,16,1024]{2,1,0:T(8,128)S(1)} collective-permute-done((f32[8,16,1024]{2,1,0:T(8,128)}, f32[8,16,1024]{2,1,0:T(8,128)S(1)}, u32[]{:S(2)}, u32[]{:S(2)}) %collective-permute-start.1) | collective-permute-done | bytes 524320 | tf_op jit(solution)/shard_map/ppermute | solution.py:196
  34.9 4.6 %collective-permute-done.2 = f32[8,16,1024]{2,1,0:T(8,128)S(1)} collective-permute-done((f32[8,16,1024]{2,1,0:T(8,128)}, f32[8,16,1024]{2,1,0:T(8,128)S(1)}, u32[]{:S(2)}, u32[]{:S(2)}) %collective-permute-start.2) | collective-permute-done | bytes 524320 | tf_op jit(solution)/shard_map/ppermute | solution.py:196
  39.8 1.7 %collective-permute-start.3 = (f32[4,16,1024]{2,1,0:T(8,128)S(1)}, f32[4,16,1024]{2,1,0:T(8,128)S(1)}, u32[]{:S(2)}, u32[]{:S(2)}) collective-permute-start(f32[4,16,1024]{2,1,0:T(8,128)S(1)} %slice.137), channel_id=1, source_target_pairs={{0,32},{32,0},{64,96},{96,64},{128,160},{160,128},{192,224},{224,1... | collective-permute-start | bytes 786440 | tf_op jit(solution)/shard_map/ppermute | solution.py:196
  41.5 4.0 %collective-permute-done.3 = f32[4,16,1024]{2,1,0:T(8,128)S(1)} collective-permute-done((f32[4,16,1024]{2,1,0:T(8,128)S(1)}, f32[4,16,1024]{2,1,0:T(8,128)S(1)}, u32[]{:S(2)}, u32[]{:S(2)}) %collective-permute-start.3) | collective-permute-done | bytes 262176 | tf_op jit(solution)/shard_map/ppermute | solution.py:196
  45.6 3.1 %collective-permute-start.4 = (f32[2,16,1024]{2,1,0:T(8,128)S(1)}, f32[2,16,1024]{2,1,0:T(8,128)S(1)}, u32[]{:S(2)}, u32[]{:S(2)}) collective-permute-start(f32[2,16,1024]{2,1,0:T(8,128)S(1)} %slice.139), channel_id=1, source_target_pairs={{0,64},{32,96},{64,0},{96,32},{128,192},{160,224},{192,128},{224,1... | collective-permute-start | bytes 393224 | tf_op jit(solution)/shard_map/ppermute | solution.py:196
  48.7 2.7 %collective-permute-done.4 = f32[2,16,1024]{2,1,0:T(8,128)S(1)} collective-permute-done((f32[2,16,1024]{2,1,0:T(8,128)S(1)}, f32[2,16,1024]{2,1,0:T(8,128)S(1)}, u32[]{:S(2)}, u32[]{:S(2)}) %collective-permute-start.4) | collective-permute-done | bytes 131104 | tf_op jit(solution)/shard_map/ppermute | solution.py:196
  51.4 7.5 %collective-permute-start.5 = (f32[1,16,1024]{2,1,0:T(8,128)S(1)}, f32[1,16,1024]{2,1,0:T(8,128)S(1)}, u32[]{:S(2)}, u32[]{:S(2)}) collective-permute-start(f32[1,16,1024]{2,1,0:T(8,128)S(1)} %slice.141), channel_id=1, source_target_pairs={{0,128},{32,160},{64,192},{96,224},{128,0},{160,32},{192,64},{224,... | collective-permute-start | bytes 196616 | tf_op jit(solution)/shard_map/ppermute | solution.py:196
  59.2 1.6 %collective-permute-done.5 = f32[1,16,1024]{2,1,0:T(8,128)S(1)} collective-permute-done((f32[1,16,1024]{2,1,0:T(8,128)S(1)}, f32[1,16,1024]{2,1,0:T(8,128)S(1)}, u32[]{:S(2)}, u32[]{:S(2)}) %collective-permute-start.5) | collective-permute-done | bytes 65568 | tf_op jit(solution)/shard_map/ppermute | solution.py:196
  60.8 6.8 %collective-permute-start.6 = (f32[16,768]{1,0:T(8,128)S(1)}, f32[16,768]{1,0:T(8,128)S(1)}, u32[]{:S(2)}, u32[]{:S(2)}) collective-permute-start(f32[16,768]{1,0:T(8,128)S(1)} %pad_maximum_fusion.2), channel_id=1, source_target_pairs={{0,1},{1,0},{2,3},{3,2},{4,5},{5,4},{6,7},{7,6},{8,9},{9,8},{10,11... | collective-permute-start | bytes 147464 | tf_op jit(solution)/shard_map/ppermute | solution.py:196
  67.8 0.7 collective-permute-done.6
  68.6 0.7 collective-permute-start.9
  69.2 1.3 collective-permute-start.8
  70.5 0.7 collective-permute-start.7
  71.8 6.4 %collective-permute-start.15 = (f32[1,16,512]{2,1,0:T(8,128)S(1)}, f32[1,16,512]{2,1,0:T(8,128)S(1)}, u32[]{:S(2)}, u32[]{:S(2)}) collective-permute-start(f32[1,16,512]{2,1,0:T(8,128)S(1)} %slice.155), channel_id=1, source_target_pairs={{0,128},{32,160},{64,192},{96,224},{128,0},{160,32},{192,64},{224,... | collective-permute-start | bytes 98312 | tf_op jit(solution)/shard_map/ppermute | solution.py:196
  78.2 0.9 broadcast_in_dim.9
  79.1 6.3 %all-to-all-start = ((f32[8,16,1280]{2,1,0:T(8,128)}), f32[8,16,1280]{2,1,0:T(8,128)S(1)}, u32[]{:S(2)}, u32[]{:S(2)}) async-start(f32[8,16,1280]{2,1,0:T(8,128)} %broadcast_in_dim.9), calls=%async_computation | async-start | bytes 1310720 | tf_op jit(solution)/shard_map/all_to_all | solution.py:227
  85.5 2.9 %collective-permute-start.16 = (f32[16,256]{1,0:T(8,128)S(1)}, f32[16,256]{1,0:T(8,128)S(1)}, u32[]{:S(2)}, u32[]{:S(2)}) collective-permute-start(f32[16,256]{1,0:T(8,128)S(1)} %slice_select_fusion.6), channel_id=1, source_target_pairs={{0,1},{1,0},{2,3},{3,2},{4,5},{5,4},{6,7},{7,6},{8,9},{9,8},{10,11... | collective-permute-start | bytes 49160 | tf_op jit(solution)/shard_map/ppermute | solution.py:196
  88.4 0.8 collective-permute-done.16
  89.2 0.7 collective-permute-start.19
  89.9 1.3 collective-permute-start.18
  91.2 0.7 collective-permute-start.17
  91.9 4.0 %collective-permute-done.18 = f32[16,512]{1,0:T(8,128)S(1)} collective-permute-done((f32[16,512]{1,0:T(8,128)S(1)}, f32[16,512]{1,0:T(8,128)S(1)}, u32[]{:S(2)}, u32[]{:S(2)}) %collective-permute-start.18) | collective-permute-done | bytes 32800 | tf_op jit(solution)/shard_map/ppermute | solution.py:222
  95.9 4.0 %collective-permute-start.22 = (f32[16,512]{1,0:T(8,128)S(1)}, f32[16,512]{1,0:T(8,128)S(1)}, u32[]{:S(2)}, u32[]{:S(2)}) collective-permute-start(f32[16,512]{1,0:T(8,128)S(1)} %add_select_fusion.1), channel_id=1, source_target_pairs={{0,24},{8,16},{16,8},{24,0},{1,25},{9,17},{17,9},{25,1},{2,26},{10... | collective-permute-start | bytes 98312 | tf_op jit(solution)/shard_map/ppermute | solution.py:196
  100.0 0.7 collective-permute-start.20
  100.6 0.6 collective-permute-done.22
  101.3 3.0 %collective-permute-done.21 = f32[16,512]{1,0:T(8,128)S(1)} collective-permute-done((f32[16,512]{1,0:T(8,128)S(1)}, f32[16,512]{1,0:T(8,128)S(1)}, u32[]{:S(2)}, u32[]{:S(2)}) %collective-permute-start.21) | collective-permute-done | bytes 32800 | tf_op jit(solution)/shard_map/ppermute | solution.py:196
  104.3 4.8 %collective-permute-start.24 = (f32[8,16,1280]{2,1,0:T(8,128)S(1)}, f32[8,16,1280]{2,1,0:T(8,128)S(1)}, u32[]{:S(2)}, u32[]{:S(2)}) collective-permute-start(f32[8,16,1280]{2,1,0:T(8,128)S(1)} %all-to-all-done.refs_1_.refs_0_.refs_5_), channel_id=1, source_target_pairs={{0,24},{8,0},{16,8},{24,16},{1,25},{9,1},{17,9},{25,17},{2,26},{10... | collective-permute-start | bytes 1966088 | tf_op jit(solution)/shard_map/ppermute | solution.py:236
  109.0 1.1 broadcast_in_dim.10
  110.1 3.7 %all-to-all-start.1 = ((f32[8,4,16,512]{3,2,1,0:T(8,128)}), f32[8,4,16,512]{3,2,1,0:T(8,128)S(1)}, u32[]{:S(2)}, u32[]{:S(2)}) async-start(f32[8,4,16,512]{3,2,1,0:T(8,128)} %broadcast_in_dim.10), calls=%async_computation.1 | async-start | bytes 2097152 | tf_op jit(solution)/shard_map/all_to_all | solution.py:227
  113.8 7.0 %collective-permute-done.24.refs_3_.refs_2_.refs_7_ = f32[8,16,1280]{2,1,0:T(8,128)S(1)} collective-permute-done((f32[8,16,1280]{2,1,0:T(8,128)S(1)}, f32[8,16,1280]{2,1,0:T(8,128)S(1)}, u32[]{:S(2)}, u32[]{:S(2)}) %collective-permute-start.24) | collective-permute-done | bytes 655392 | tf_op jit(solution)/shard_map/ppermute | solution.py:236
  120.9 3.5 %collective-permute-start.26 = (f32[4,16,1280]{2,1,0:T(8,128)S(1)}, f32[4,16,1280]{2,1,0:T(8,128)S(1)}, u32[]{:S(2)}, u32[]{:S(2)}) collective-permute-start(f32[4,16,1280]{2,1,0:T(8,128)S(1)} %slice.162), channel_id=1, source_target_pairs={{0,24},{8,0},{16,8},{24,16},{1,25},{9,1},{17,9},{25,17},{2,26},{10... | collective-permute-start | bytes 983048 | tf_op jit(solution)/shard_map/ppermute | solution.py:236
  124.5 7.4 %collective-permute-done.25.refs_4_.refs_3_.refs_8_ = f32[4,16,1280]{2,1,0:T(8,128)S(1)} collective-permute-done((f32[4,16,1280]{2,1,0:T(8,128)S(1)}, f32[4,16,1280]{2,1,0:T(8,128)S(1)}, u32[]{:S(2)}, u32[]{:S(2)}) %collective-permute-start.25) | collective-permute-done | bytes 327712 | tf_op jit(solution)/shard_map/ppermute | solution.py:236
  131.9 0.7 copy-done.8
  132.7 4.3 %collective-permute-start.27 = (f32[4,8,16,256]{3,2,1,0:T(8,128)S(1)}, f32[4,8,16,256]{3,2,1,0:T(8,128)}, u32[]{:S(2)}, u32[]{:S(2)}) collective-permute-start(f32[4,8,16,256]{3,2,1,0:T(8,128)S(1)} %bitcast.36), channel_id=1, source_target_pairs={{0,1},{1,0},{2,3},{3,2},{4,5},{5,4},{6,7},{7,6},{8,9},{9,8},{10,11... | collective-permute-start | bytes 1572872 | tf_op jit(solution)/shard_map/ppermute | solution.py:196
  137.0 1.7 %collective-permute-done.27.other_hbm = f32[4,8,16,256]{3,2,1,0:T(8,128)} collective-permute-done((f32[4,8,16,256]{3,2,1,0:T(8,128)S(1)}, f32[4,8,16,256]{3,2,1,0:T(8,128)}, u32[]{:S(2)}, u32[]{:S(2)}) %collective-permute-start.27) | collective-permute-done | bytes 524320 | tf_op jit(solution)/shard_map/ppermute | solution.py:196
  138.7 5.9 %solve.3.own = f32[2,512,512]{2,1,0:T(8,128)} custom-call(s32[1]{0:T(128)} %bitcast.1.y_ref, s32[1]{0:T(128)} %bitcast.core_ref, f32[2,512,512]{2,1,0:T(8,128)} %inv_hbm.3, f32[4,8,16,256]{3,2,1,0:T(8,128)} %collective-permute-done.27.other_hbm, f32[8,16,1280]{2,1,0:T(8,128)} %copy-done.3, f32[8,16,1280]{2,1,0:T(8,128)} %copy-done.5, ...), custom_call_target="tpu_custom_call" | custom-call | flops 2415919104 | bytes 6291456 | tf_op jit(solution)/shard_map/solve/pallas_call | solution.py:132
  145.1 1.0 copy-done.6
  146.1 5.1 %solve.2.own = f32[2,512,256]{2,1,0:T(8,128)} custom-call(s32[1]{0:T(128)} %bitcast.1.y_ref, s32[1]{0:T(128)} %bitcast.core_ref, f32[2,512,512]{2,1,0:T(8,128)} %inv_hbm.3, f32[4,8,16,256]{3,2,1,0:T(8,128)} %collective-permute-done.27.other_hbm, f32[8,4,16,512]{3,2,1,0:T(8,128)} %copy-done.6, f32[8,16,1280]{2,1,0:T(8,128)} %copy-done.3, ...), custom_call_target="tpu_custom_call" | custom-call | flops 1207959552 | bytes 6291456 | tf_op jit(solution)/shard_map/solve/pallas_call | solution.py:132
  151.4 3.7 %finish.2 = (f32[2,512,1536]{2,1,0:T(8,128)}, f32[16,1536]{1,0:T(8,128)S(1)}) custom-call(s32[1]{0:T(128)} %bitcast.core_ref, f32[2,512,512]{2,1,0:T(8,128)S(1)} %copy-done, f32[2,512,512]{2,1,0:T(8,128)} %collective-permute-done.29.other, f32[16,1024]{1,0:T(8,128)S(1)} %fusion.1.base, f32[2,16,512]{2,1,0:T(8,128)S(1)} %bitcast.23), custom_call_target="tpu_custom_call" | custom-call | flops 100663296 | bytes 6291456 | tf_op jit(solution)/shard_map/finish/pallas_call | solution.py:176
  155.1 2.3 %finish.3 = (f32[2,512,1536]{2,1,0:T(8,128)}, f32[16,1536]{1,0:T(8,128)}) custom-call(s32[1]{0:T(128)} %bitcast.core_ref, f32[2,512,256]{2,1,0:T(8,128)S(1)} %copy-done.1, f32[2,512,256]{2,1,0:T(8,128)S(1)} %collective-permute-done.28.other, f32[16,512]{1,0:T(8,128)S(1)} %fusion.3.base, f32[2,16,512]{2,1,0:T(8,128)S(1)} %bitcast.24, ...), custom_call_target="tpu_custom_call", output_to_operand_aliasing={{0}: (5, {})} | custom-call | flops 50331648 | bytes 6291456 | tf_op jit(solution)/shard_map/finish/pallas_call | solution.py:176
  (84 shorter events, 2.2 us)
Async XLA Ops:
  12.0 14.9 %collective-permute-start = (f32[8,16,1024]{2,1,0:T(8,128)}, f32[8,16,1024]{2,1,0:T(8,128)S(1)}, u32[]{:S(2)}, u32[]{:S(2)}) collective-permute-start(f32[8,16,1024]{2,1,0:T(8,128)} %get-tuple-element.18), channel_id=1, source_target_pairs={{0,8},{8,0},{16,24},{24,16},{1,9},{9,1},{17,25},{25,17},{2,10},{10... | collective-permute-start | bytes 1572872 | tf_op jit(solution)/shard_map/ppermute | solution.py:196
  14.1 20.8 %collective-permute-start.1 = (f32[8,16,1024]{2,1,0:T(8,128)}, f32[8,16,1024]{2,1,0:T(8,128)S(1)}, u32[]{:S(2)}, u32[]{:S(2)}) collective-permute-start(f32[8,16,1024]{2,1,0:T(8,128)} %get-tuple-element.19), channel_id=1, source_target_pairs={{0,24},{8,16},{16,8},{24,0},{1,25},{9,17},{17,9},{25,1},{2,26},{10... | collective-permute-start | bytes 1572872 | tf_op jit(solution)/shard_map/ppermute | solution.py:196
  16.0 23.5 %collective-permute-start.2 = (f32[8,16,1024]{2,1,0:T(8,128)}, f32[8,16,1024]{2,1,0:T(8,128)S(1)}, u32[]{:S(2)}, u32[]{:S(2)}) collective-permute-start(f32[8,16,1024]{2,1,0:T(8,128)} %get-tuple-element.20), channel_id=1, source_target_pairs={{0,16},{8,24},{16,0},{24,8},{1,17},{9,25},{17,1},{25,9},{2,18},{10... | collective-permute-start | bytes 1572872 | tf_op jit(solution)/shard_map/ppermute | solution.py:196
  16.8 22.8 %copy-start.9 = (f32[8,16,1024]{2,1,0:T(8,128)S(1)}, f32[8,16,1024]{2,1,0:T(8,128)}, u32[]{:S(2)}) copy-start(f32[8,16,1024]{2,1,0:T(8,128)} %get-tuple-element.17) | copy-start | bytes 1572868
  16.8 24.7 %copy-start.2 = (f32[1,1,2,16,512]{4,3,2,1,0:T(8,128)S(1)}, f32[1,1,2,16,512]{4,3,2,1,0:T(8,128)}, u32[]{:S(2)}) copy-start(f32[1,1,2,16,512]{4,3,2,1,0:T(8,128)} %param.8) | copy-start | bytes 196612
  16.8 24.7 %copy-start.11 = (f32[1,1,16,1536]{3,2,1,0:T(8,128)S(1)}, f32[1,1,16,1536]{3,2,1,0:T(8,128)}, u32[]{:S(2)}) copy-start(f32[1,1,16,1536]{3,2,1,0:T(8,128)} %param.7) | copy-start | bytes 294916
  24.4 34.6 %copy-start.10 = (f32[8,16,512]{2,1,0:T(8,128)S(1)}, f32[8,16,512]{2,1,0:T(8,128)}, u32[]{:S(2)}) copy-start(f32[8,16,512]{2,1,0:T(8,128)} %get-tuple-element.23) | copy-start | bytes 786436
  24.4 34.6 %collective-permute-start.10 = (f32[8,16,512]{2,1,0:T(8,128)}, f32[8,16,512]{2,1,0:T(8,128)S(1)}, u32[]{:S(2)}, u32[]{:S(2)}) collective-permute-start(f32[8,16,512]{2,1,0:T(8,128)} %get-tuple-element.24), channel_id=1, source_target_pairs={{0,8},{8,0},{16,24},{24,16},{1,9},{9,1},{17,25},{25,17},{2,10},{10... | collective-permute-start | bytes 786440 | tf_op jit(solution)/shard_map/ppermute | solution.py:196
  25.0 33.9 %collective-permute-start.11 = (f32[8,16,512]{2,1,0:T(8,128)}, f32[8,16,512]{2,1,0:T(8,128)S(1)}, u32[]{:S(2)}, u32[]{:S(2)}) collective-permute-start(f32[8,16,512]{2,1,0:T(8,128)} %get-tuple-element.25), channel_id=1, source_target_pairs={{0,24},{8,16},{16,8},{24,0},{1,25},{9,17},{17,9},{25,1},{2,26},{10... | collective-permute-start | bytes 786440 | tf_op jit(solution)/shard_map/ppermute | solution.py:196
  26.9 32.0 %collective-permute-start.12 = (f32[8,16,512]{2,1,0:T(8,128)}, f32[8,16,512]{2,1,0:T(8,128)S(1)}, u32[]{:S(2)}, u32[]{:S(2)}) collective-permute-start(f32[8,16,512]{2,1,0:T(8,128)} %get-tuple-element.26), channel_id=1, source_target_pairs={{0,16},{8,24},{16,0},{24,8},{1,17},{9,25},{17,1},{25,9},{2,18},{10... | collective-permute-start | bytes 786440 | tf_op jit(solution)/shard_map/ppermute | solution.py:196
  39.8 5.8 %collective-permute-start.3 = (f32[4,16,1024]{2,1,0:T(8,128)S(1)}, f32[4,16,1024]{2,1,0:T(8,128)S(1)}, u32[]{:S(2)}, u32[]{:S(2)}) collective-permute-start(f32[4,16,1024]{2,1,0:T(8,128)S(1)} %slice.137), channel_id=1, source_target_pairs={{0,32},{32,0},{64,96},{96,64},{128,160},{160,128},{192,224},{224,1... | collective-permute-start | bytes 786440 | tf_op jit(solution)/shard_map/ppermute | solution.py:196
  45.6 5.8 %collective-permute-start.4 = (f32[2,16,1024]{2,1,0:T(8,128)S(1)}, f32[2,16,1024]{2,1,0:T(8,128)S(1)}, u32[]{:S(2)}, u32[]{:S(2)}) collective-permute-start(f32[2,16,1024]{2,1,0:T(8,128)S(1)} %slice.139), channel_id=1, source_target_pairs={{0,64},{32,96},{64,0},{96,32},{128,192},{160,224},{192,128},{224,1... | collective-permute-start | bytes 393224 | tf_op jit(solution)/shard_map/ppermute | solution.py:196
  51.4 9.3 %collective-permute-start.5 = (f32[1,16,1024]{2,1,0:T(8,128)S(1)}, f32[1,16,1024]{2,1,0:T(8,128)S(1)}, u32[]{:S(2)}, u32[]{:S(2)}) collective-permute-start(f32[1,16,1024]{2,1,0:T(8,128)S(1)} %slice.141), channel_id=1, source_target_pairs={{0,128},{32,160},{64,192},{96,224},{128,0},{160,32},{192,64},{224,... | collective-permute-start | bytes 196616 | tf_op jit(solution)/shard_map/ppermute | solution.py:196
  59.1 8.6 %collective-permute-start.13 = (f32[4,16,512]{2,1,0:T(8,128)S(1)}, f32[4,16,512]{2,1,0:T(8,128)S(1)}, u32[]{:S(2)}, u32[]{:S(2)}) collective-permute-start(f32[4,16,512]{2,1,0:T(8,128)S(1)} %slice.151), channel_id=1, source_target_pairs={{0,224},{32,64},{64,32},{96,128},{128,96},{160,192},{192,160},{224... | collective-permute-start | bytes 393224 | tf_op jit(solution)/shard_map/ppermute | solution.py:196
  60.8 7.7 %collective-permute-start.6 = (f32[16,768]{1,0:T(8,128)S(1)}, f32[16,768]{1,0:T(8,128)S(1)}, u32[]{:S(2)}, u32[]{:S(2)}) collective-permute-start(f32[16,768]{1,0:T(8,128)S(1)} %pad_maximum_fusion.2), channel_id=1, source_target_pairs={{0,1},{1,0},{2,3},{3,2},{4,5},{5,4},{6,7},{7,6},{8,9},{9,8},{10,11... | collective-permute-start | bytes 147464 | tf_op jit(solution)/shard_map/ppermute | solution.py:196
  67.7 4.1 %collective-permute-start.14 = (f32[2,16,512]{2,1,0:T(8,128)S(1)}, f32[2,16,512]{2,1,0:T(8,128)S(1)}, u32[]{:S(2)}, u32[]{:S(2)}) collective-permute-start(f32[2,16,512]{2,1,0:T(8,128)S(1)} %slice.153), channel_id=1, source_target_pairs={{0,64},{32,224},{64,0},{96,160},{128,192},{160,96},{192,128},{224,... | collective-permute-start | bytes 196616 | tf_op jit(solution)/shard_map/ppermute | solution.py:196
  68.6 9.6 %collective-permute-start.9 = (f32[16,1280]{1,0:T(8,128)S(1)}, f32[16,1280]{1,0:T(8,128)S(1)}, u32[]{:S(2)}, u32[]{:S(2)}) collective-permute-start(f32[16,1280]{1,0:T(8,128)S(1)} %pad_maximum_fusion.1), channel_id=1, source_target_pairs={{6,2},{7,3},{14,10},{15,11},{22,18},{23,19},{30,26},{31,27},{38,34... | collective-permute-start | bytes 245768 | tf_op jit(solution)/shard_map/ppermute | solution.py:222
  69.2 9.0 %collective-permute-start.8 = (f32[16,1280]{1,0:T(8,128)S(1)}, f32[16,1280]{1,0:T(8,128)S(1)}, u32[]{:S(2)}, u32[]{:S(2)}) collective-permute-start(f32[16,1280]{1,0:T(8,128)S(1)} %pad_maximum_fusion.1), channel_id=1, source_target_pairs={{6,0},{7,1},{14,8},{15,9},{22,16},{23,17},{30,24},{31,25},{38,32},... | collective-permute-start | bytes 245768 | tf_op jit(solution)/shard_map/ppermute | solution.py:222
  70.5 7.7 %collective-permute-start.7 = (f32[16,1280]{1,0:T(8,128)S(1)}, f32[16,1280]{1,0:T(8,128)S(1)}, u32[]{:S(2)}, u32[]{:S(2)}) collective-permute-start(f32[16,1280]{1,0:T(8,128)S(1)} %pad_maximum_fusion.1), channel_id=1, source_target_pairs={{6,4},{7,5},{14,12},{15,13},{22,20},{23,21},{30,28},{31,29},{38,36... | collective-permute-start | bytes 245768 | tf_op jit(solution)/shard_map/ppermute | solution.py:222
  71.8 13.6 %collective-permute-start.15 = (f32[1,16,512]{2,1,0:T(8,128)S(1)}, f32[1,16,512]{2,1,0:T(8,128)S(1)}, u32[]{:S(2)}, u32[]{:S(2)}) collective-permute-start(f32[1,16,512]{2,1,0:T(8,128)S(1)} %slice.155), channel_id=1, source_target_pairs={{0,128},{32,160},{64,192},{96,224},{128,0},{160,32},{192,64},{224,... | collective-permute-start | bytes 98312 | tf_op jit(solution)/shard_map/ppermute | solution.py:196
  79.1 25.2 %all-to-all-start = ((f32[8,16,1280]{2,1,0:T(8,128)}), f32[8,16,1280]{2,1,0:T(8,128)S(1)}, u32[]{:S(2)}, u32[]{:S(2)}) async-start(f32[8,16,1280]{2,1,0:T(8,128)} %broadcast_in_dim.9), calls=%async_computation | async-start | bytes 1310720 | tf_op jit(solution)/shard_map/all_to_all | solution.py:227
  85.5 3.7 %collective-permute-start.16 = (f32[16,256]{1,0:T(8,128)S(1)}, f32[16,256]{1,0:T(8,128)S(1)}, u32[]{:S(2)}, u32[]{:S(2)}) collective-permute-start(f32[16,256]{1,0:T(8,128)S(1)} %slice_select_fusion.6), channel_id=1, source_target_pairs={{0,1},{1,0},{2,3},{3,2},{4,5},{5,4},{6,7},{7,6},{8,9},{9,8},{10,11... | collective-permute-start | bytes 49160 | tf_op jit(solution)/shard_map/ppermute | solution.py:196
  89.2 2.6 %collective-permute-start.19 = (f32[16,512]{1,0:T(8,128)S(1)}, f32[16,512]{1,0:T(8,128)S(1)}, u32[]{:S(2)}, u32[]{:S(2)}) collective-permute-start(f32[16,512]{1,0:T(8,128)S(1)} %pad_maximum_fusion.3), channel_id=1, source_target_pairs={{6,2},{7,3},{14,10},{15,11},{22,18},{23,19},{30,26},{31,27},{38,34... | collective-permute-start | bytes 98312 | tf_op jit(solution)/shard_map/ppermute | solution.py:222
  89.9 6.0 %collective-permute-start.18 = (f32[16,512]{1,0:T(8,128)S(1)}, f32[16,512]{1,0:T(8,128)S(1)}, u32[]{:S(2)}, u32[]{:S(2)}) collective-permute-start(f32[16,512]{1,0:T(8,128)S(1)} %pad_maximum_fusion.3), channel_id=1, source_target_pairs={{6,0},{7,1},{14,8},{15,9},{22,16},{23,17},{30,24},{31,25},{38,32},... | collective-permute-start | bytes 98312 | tf_op jit(solution)/shard_map/ppermute | solution.py:222
  91.2 4.7 %collective-permute-start.17 = (f32[16,512]{1,0:T(8,128)S(1)}, f32[16,512]{1,0:T(8,128)S(1)}, u32[]{:S(2)}, u32[]{:S(2)}) collective-permute-start(f32[16,512]{1,0:T(8,128)S(1)} %pad_maximum_fusion.3), channel_id=1, source_target_pairs={{6,4},{7,5},{14,12},{15,13},{22,20},{23,21},{30,28},{31,29},{38,36... | collective-permute-start | bytes 98312 | tf_op jit(solution)/shard_map/ppermute | solution.py:222
  95.9 5.3 %collective-permute-start.22 = (f32[16,512]{1,0:T(8,128)S(1)}, f32[16,512]{1,0:T(8,128)S(1)}, u32[]{:S(2)}, u32[]{:S(2)}) collective-permute-start(f32[16,512]{1,0:T(8,128)S(1)} %add_select_fusion.1), channel_id=1, source_target_pairs={{0,24},{8,16},{16,8},{24,0},{1,25},{9,17},{17,9},{25,1},{2,26},{10... | collective-permute-start | bytes 98312 | tf_op jit(solution)/shard_map/ppermute | solution.py:196
  100.0 4.3 %collective-permute-start.21 = (f32[16,512]{1,0:T(8,128)S(1)}, f32[16,512]{1,0:T(8,128)S(1)}, u32[]{:S(2)}, u32[]{:S(2)}) collective-permute-start(f32[16,512]{1,0:T(8,128)S(1)} %add_select_fusion.1), channel_id=1, source_target_pairs={{0,16},{8,24},{16,0},{24,8},{1,17},{9,25},{17,1},{25,9},{2,18},{10... | collective-permute-start | bytes 98312 | tf_op jit(solution)/shard_map/ppermute | solution.py:196
  100.0 4.3 %collective-permute-start.20 = (f32[16,512]{1,0:T(8,128)S(1)}, f32[16,512]{1,0:T(8,128)S(1)}, u32[]{:S(2)}, u32[]{:S(2)}) collective-permute-start(f32[16,512]{1,0:T(8,128)S(1)} %add_select_fusion.1), channel_id=1, source_target_pairs={{0,8},{8,0},{16,24},{24,16},{1,9},{9,1},{17,25},{25,17},{2,10},{10... | collective-permute-start | bytes 98312 | tf_op jit(solution)/shard_map/ppermute | solution.py:196
  104.3 34.4 %copy-start.3 = (f32[8,16,1280]{2,1,0:T(8,128)}, f32[8,16,1280]{2,1,0:T(8,128)S(1)}, u32[]{:S(2)}) copy-start(f32[8,16,1280]{2,1,0:T(8,128)S(1)} %all-to-all-done.refs_1_.refs_0_.refs_5_) | copy-start | bytes 1966084
  104.3 16.6 %collective-permute-start.24 = (f32[8,16,1280]{2,1,0:T(8,128)S(1)}, f32[8,16,1280]{2,1,0:T(8,128)S(1)}, u32[]{:S(2)}, u32[]{:S(2)}) collective-permute-start(f32[8,16,1280]{2,1,0:T(8,128)S(1)} %all-to-all-done.refs_1_.refs_0_.refs_5_), channel_id=1, source_target_pairs={{0,24},{8,0},{16,8},{24,16},{1,25},{9,1},{17,9},{25,17},{2,26},{10... | collective-permute-start | bytes 1966088 | tf_op jit(solution)/shard_map/ppermute | solution.py:236
  109.0 15.4 %collective-permute-start.23 = (f32[8,16,1280]{2,1,0:T(8,128)S(1)}, f32[8,16,1280]{2,1,0:T(8,128)S(1)}, u32[]{:S(2)}, u32[]{:S(2)}) collective-permute-start(f32[8,16,1280]{2,1,0:T(8,128)S(1)} %all-to-all-done.refs_1_.refs_0_.refs_5_), channel_id=1, source_target_pairs={{0,8},{8,16},{16,24},{24,0},{1,9},{9,17},{17,25},{25,1},{2,10},{10... | collective-permute-start | bytes 1966088 | tf_op jit(solution)/shard_map/ppermute | solution.py:236
  110.1 34.9 %all-to-all-start.1 = ((f32[8,4,16,512]{3,2,1,0:T(8,128)}), f32[8,4,16,512]{3,2,1,0:T(8,128)S(1)}, u32[]{:S(2)}, u32[]{:S(2)}) async-start(f32[8,4,16,512]{3,2,1,0:T(8,128)} %broadcast_in_dim.10), calls=%async_computation.1 | async-start | bytes 2097152 | tf_op jit(solution)/shard_map/all_to_all | solution.py:227
  120.9 17.8 %copy-start.4 = (f32[8,16,1280]{2,1,0:T(8,128)}, f32[8,16,1280]{2,1,0:T(8,128)S(1)}, u32[]{:S(2)}) copy-start(f32[8,16,1280]{2,1,0:T(8,128)S(1)} %collective-permute-done.24.refs_3_.refs_2_.refs_7_) | copy-start | bytes 1966084
  120.9 11.0 %collective-permute-start.26 = (f32[4,16,1280]{2,1,0:T(8,128)S(1)}, f32[4,16,1280]{2,1,0:T(8,128)S(1)}, u32[]{:S(2)}, u32[]{:S(2)}) collective-permute-start(f32[4,16,1280]{2,1,0:T(8,128)S(1)} %slice.162), channel_id=1, source_target_pairs={{0,24},{8,0},{16,8},{24,16},{1,25},{9,1},{17,9},{25,17},{2,26},{10... | collective-permute-start | bytes 983048 | tf_op jit(solution)/shard_map/ppermute | solution.py:236
  124.4 14.3 %copy-start.5 = (f32[8,16,1280]{2,1,0:T(8,128)}, f32[8,16,1280]{2,1,0:T(8,128)S(1)}, u32[]{:S(2)}) copy-start(f32[8,16,1280]{2,1,0:T(8,128)S(1)} %collective-permute-done.23.refs_2_.refs_1_.refs_6_) | copy-start | bytes 1966084
  124.4 7.5 %collective-permute-start.25 = (f32[4,16,1280]{2,1,0:T(8,128)S(1)}, f32[4,16,1280]{2,1,0:T(8,128)S(1)}, u32[]{:S(2)}, u32[]{:S(2)}) collective-permute-start(f32[4,16,1280]{2,1,0:T(8,128)S(1)} %slice.160), channel_id=1, source_target_pairs={{0,8},{8,16},{16,24},{24,0},{1,9},{9,17},{17,25},{25,1},{2,10},{10... | collective-permute-start | bytes 983048 | tf_op jit(solution)/shard_map/ppermute | solution.py:236
  131.9 0.7 copy-start.8
  132.6 6.0 %copy-start.7 = (f32[4,16,1280]{2,1,0:T(8,128)}, f32[4,16,1280]{2,1,0:T(8,128)S(1)}, u32[]{:S(2)}) copy-start(f32[4,16,1280]{2,1,0:T(8,128)S(1)} %collective-permute-done.26.refs_5_.refs_4_.refs_9_) | copy-start | bytes 983044
  132.7 6.0 %collective-permute-start.27 = (f32[4,8,16,256]{3,2,1,0:T(8,128)S(1)}, f32[4,8,16,256]{3,2,1,0:T(8,128)}, u32[]{:S(2)}, u32[]{:S(2)}) collective-permute-start(f32[4,8,16,256]{3,2,1,0:T(8,128)S(1)} %bitcast.36), channel_id=1, source_target_pairs={{0,1},{1,0},{2,3},{3,2},{4,5},{5,4},{6,7},{7,6},{8,9},{9,8},{10,11... | collective-permute-start | bytes 1572872 | tf_op jit(solution)/shard_map/ppermute | solution.py:196
  144.6 6.8 %copy-start = (f32[2,512,512]{2,1,0:T(8,128)S(1)}, f32[2,512,512]{2,1,0:T(8,128)}, u32[]{:S(2)}) copy-start(f32[2,512,512]{2,1,0:T(8,128)} %solve.3.own) | copy-start | bytes 6291460
  144.6 6.8 %collective-permute-start.29 = (f32[2,512,512]{2,1,0:T(8,128)}, f32[2,512,512]{2,1,0:T(8,128)}, u32[]{:S(2)}, u32[]{:S(2)}) collective-permute-start(f32[2,512,512]{2,1,0:T(8,128)} %solve.3.own), channel_id=1, source_target_pairs={{0,1},{1,0},{2,3},{3,2},{4,5},{5,4},{6,7},{7,6},{8,9},{9,8},{10,11... | collective-permute-start | bytes 6291464 | tf_op jit(solution)/shard_map/ppermute | solution.py:196
  145.1 1.0 copy-start.6
  151.2 4.0 %copy-start.1 = (f32[2,512,256]{2,1,0:T(8,128)S(1)}, f32[2,512,256]{2,1,0:T(8,128)}, u32[]{:S(2)}) copy-start(f32[2,512,256]{2,1,0:T(8,128)} %solve.2.own) | copy-start | bytes 3145732
  151.2 3.9 %collective-permute-start.28 = (f32[2,512,256]{2,1,0:T(8,128)}, f32[2,512,256]{2,1,0:T(8,128)S(1)}, u32[]{:S(2)}, u32[]{:S(2)}) collective-permute-start(f32[2,512,256]{2,1,0:T(8,128)} %solve.2.own), channel_id=1, source_target_pairs={{0,1},{1,0},{2,3},{3,2},{4,5},{5,4},{6,7},{7,6},{8,9},{9,8},{10,11... | collective-permute-start | bytes 3145736 | tf_op jit(solution)/shard_map/ppermute | solution.py:196

commit v7 on v6

--- a/solution.py
+++ b/solution.py
@@ -228,7 +228,8 @@
 
 
 def gather_y(v):
-    return [v] + [swap(v, "y", ky) for ky in range(1, NY)]
+    came = {ky: swap(v, "y", ky) for ky in (1, 3, 2)}
+    return [v] + [came[ky] for ky in range(1, NY)]
 
 
 def step(x, axis, by):

time: 158 us -> 158 us (level)
  no operation moved by 1% of the time
where the time goes in v7:
time: 158 us
  starting transfers between devices  71.1 us (45%)
  waiting for transfers between devices  45 us (28%)
  Pallas kernels  36.1 us (23%)
  local copies, waits for them, and re-layouts  3.86 us (2%)
    ppermute x20, starting transfers between devices, swap(): lax.ppermute(x, axis, [(i, (((i + shift) % n ^ bit) - shift) % n) for i i...  47.4 us
    ppermute x20, waiting for transfers between devices, swap(): lax.ppermute(x, axis, [(i, (((i + shift) % n ^ bit) - shift) % n) for i i...  26.6 us
    pallas_call x2, Pallas kernels, term(): pl.pallas_call(functools.partial(term_kernel, part), grid_spec=pltpu.Pref...  19 us
    ppermute x4, waiting for transfers between devices, step(): return lax.ppermute(x, axis, [(i, (i + by) % n) for i in range(n)])  14.4 us
    pallas_call x2, Pallas kernels, solve(): pl.pallas_call(functools.partial(solve_kernel, n), in_specs=[scalar] * 2...  11 us
    all_to_all x2, starting transfers between devices, gather_z(): lax.all_to_all(jnp.broadcast_to(v, (NZ, *v.shape)), 'z', 0, 0, tiled=True)  10 us
    ppermute x4, starting transfers between devices, step(): return lax.ppermute(x, axis, [(i, (i + by) % n) for i in range(n)])  8.33 us
    pallas_call x2, Pallas kernels, finish(): pl.pallas_call(functools.partial(finish_kernel, chunk), in_specs=[pl.Bloc...  6.06 us
  transfers between devices with their start and end apart: 32, of which 14 were waited for; matrix products, arithmetic and copies ran while one was open for 2% of the time, Pallas kernels for 14%

profile of v7, /device:TPU:1, one launch (start us, length us, event | category | flops | bytes accessed | tf_op | source)
XLA Modules:
  0.0 157.6 jit_solution(2095052678537161541)
XLA Ops:
  0.6 11.4 %term.2 = (f32[8,16,1024]{2,1,0:T(8,128)}, f32[8,16,1024]{2,1,0:T(8,128)}, f32[8,16,1024]{2,1,0:T(8,128)}, f32[8,16,1024]{2,1,0:T(8,128)}) custom-call(s32[1]{0:T(128)} %bitcast.3.z_ref, s32[1]{0:T(128)} %bitcast.1.y_ref, f32[4,512,512]{2,1,0:T(8,128)} %bitcast.31, f32[4,512,1536]{2,1,0:T(8,128)} %bitcast.25, f32[4,512,1536]{2,1,0:T(8,128)} %bitcast.26, ...), custom_call_target="tpu_custom_call" | custom-call | flops 6442450944 | bytes 12582912 | tf_op jit(solution)/shard_map/term/pallas_call | solution.py:67
  12.0 2.1 %collective-permute-start = (f32[8,16,1024]{2,1,0:T(8,128)}, f32[8,16,1024]{2,1,0:T(8,128)S(1)}, u32[]{:S(2)}, u32[]{:S(2)}) collective-permute-start(f32[8,16,1024]{2,1,0:T(8,128)} %get-tuple-element.18), channel_id=1, source_target_pairs={{0,8},{8,0},{16,24},{24,16},{1,9},{9,1},{17,25},{25,17},{2,10},{10... | collective-permute-start | bytes 1572872 | tf_op jit(solution)/shard_map/ppermute | solution.py:196
  14.1 1.9 %collective-permute-start.1 = (f32[8,16,1024]{2,1,0:T(8,128)}, f32[8,16,1024]{2,1,0:T(8,128)S(1)}, u32[]{:S(2)}, u32[]{:S(2)}) collective-permute-start(f32[8,16,1024]{2,1,0:T(8,128)} %get-tuple-element.19), channel_id=1, source_target_pairs={{0,24},{8,16},{16,8},{24,0},{1,25},{9,17},{17,9},{25,1},{2,26},{10... | collective-permute-start | bytes 1572872 | tf_op jit(solution)/shard_map/ppermute | solution.py:196
  16.0 0.7 collective-permute-start.2
  16.8 7.6 %term.3 = (f32[8,16,512]{2,1,0:T(8,128)}, f32[8,16,512]{2,1,0:T(8,128)}, f32[8,16,512]{2,1,0:T(8,128)}, f32[8,16,512]{2,1,0:T(8,128)}) custom-call(s32[1]{0:T(128)} %bitcast.3.z_ref, s32[1]{0:T(128)} %bitcast.1.y_ref, f32[4,512,512]{2,1,0:T(8,128)} %bitcast.32, f32[4,512,1536]{2,1,0:T(8,128)} %bitcast.29, f32[4,512,1536]{2,1,0:T(8,128)} %bitcast.30), custom_call_target="tpu_custom_call" | custom-call | flops 3221225472 | bytes 8388608 | tf_op jit(solution)/shard_map/term/pallas_call | solution.py:67
  24.4 0.6 collective-permute-start.10
  25.0 1.9 %collective-permute-start.11 = (f32[8,16,512]{2,1,0:T(8,128)}, f32[8,16,512]{2,1,0:T(8,128)S(1)}, u32[]{:S(2)}, u32[]{:S(2)}) collective-permute-start(f32[8,16,512]{2,1,0:T(8,128)} %get-tuple-element.25), channel_id=1, source_target_pairs={{0,24},{8,16},{16,8},{24,0},{1,25},{9,17},{17,9},{25,1},{2,26},{10... | collective-permute-start | bytes 786440 | tf_op jit(solution)/shard_map/ppermute | solution.py:196
  26.9 1.8 %collective-permute-start.12 = (f32[8,16,512]{2,1,0:T(8,128)}, f32[8,16,512]{2,1,0:T(8,128)S(1)}, u32[]{:S(2)}, u32[]{:S(2)}) collective-permute-start(f32[8,16,512]{2,1,0:T(8,128)} %get-tuple-element.26), channel_id=1, source_target_pairs={{0,16},{8,24},{16,0},{24,8},{1,17},{9,25},{17,1},{25,9},{2,18},{10... | collective-permute-start | bytes 786440 | tf_op jit(solution)/shard_map/ppermute | solution.py:196
  28.8 6.2 %collective-permute-done.1 = f32[8,16,1024]{2,1,0:T(8,128)S(1)} collective-permute-done((f32[8,16,1024]{2,1,0:T(8,128)}, f32[8,16,1024]{2,1,0:T(8,128)S(1)}, u32[]{:S(2)}, u32[]{:S(2)}) %collective-permute-start.1) | collective-permute-done | bytes 524320 | tf_op jit(solution)/shard_map/ppermute | solution.py:196
  34.9 4.6 %collective-permute-done.2 = f32[8,16,1024]{2,1,0:T(8,128)S(1)} collective-permute-done((f32[8,16,1024]{2,1,0:T(8,128)}, f32[8,16,1024]{2,1,0:T(8,128)S(1)}, u32[]{:S(2)}, u32[]{:S(2)}) %collective-permute-start.2) | collective-permute-done | bytes 524320 | tf_op jit(solution)/shard_map/ppermute | solution.py:196
  39.8 1.7 %collective-permute-start.3 = (f32[4,16,1024]{2,1,0:T(8,128)S(1)}, f32[4,16,1024]{2,1,0:T(8,128)S(1)}, u32[]{:S(2)}, u32[]{:S(2)}) collective-permute-start(f32[4,16,1024]{2,1,0:T(8,128)S(1)} %slice.137), channel_id=1, source_target_pairs={{0,32},{32,0},{64,96},{96,64},{128,160},{160,128},{192,224},{224,1... | collective-permute-start | bytes 786440 | tf_op jit(solution)/shard_map/ppermute | solution.py:196
  41.5 4.0 %collective-permute-done.3 = f32[4,16,1024]{2,1,0:T(8,128)S(1)} collective-permute-done((f32[4,16,1024]{2,1,0:T(8,128)S(1)}, f32[4,16,1024]{2,1,0:T(8,128)S(1)}, u32[]{:S(2)}, u32[]{:S(2)}) %collective-permute-start.3) | collective-permute-done | bytes 262176 | tf_op jit(solution)/shard_map/ppermute | solution.py:196
  45.6 3.1 %collective-permute-start.4 = (f32[2,16,1024]{2,1,0:T(8,128)S(1)}, f32[2,16,1024]{2,1,0:T(8,128)S(1)}, u32[]{:S(2)}, u32[]{:S(2)}) collective-permute-start(f32[2,16,1024]{2,1,0:T(8,128)S(1)} %slice.139), channel_id=1, source_target_pairs={{0,64},{32,96},{64,0},{96,32},{128,192},{160,224},{192,128},{224,1... | collective-permute-start | bytes 393224 | tf_op jit(solution)/shard_map/ppermute | solution.py:196
  48.7 2.7 %collective-permute-done.4 = f32[2,16,1024]{2,1,0:T(8,128)S(1)} collective-permute-done((f32[2,16,1024]{2,1,0:T(8,128)S(1)}, f32[2,16,1024]{2,1,0:T(8,128)S(1)}, u32[]{:S(2)}, u32[]{:S(2)}) %collective-permute-start.4) | collective-permute-done | bytes 131104 | tf_op jit(solution)/shard_map/ppermute | solution.py:196
  51.4 7.5 %collective-permute-start.5 = (f32[1,16,1024]{2,1,0:T(8,128)S(1)}, f32[1,16,1024]{2,1,0:T(8,128)S(1)}, u32[]{:S(2)}, u32[]{:S(2)}) collective-permute-start(f32[1,16,1024]{2,1,0:T(8,128)S(1)} %slice.141), channel_id=1, source_target_pairs={{0,128},{32,160},{64,192},{96,224},{128,0},{160,32},{192,64},{224,... | collective-permute-start | bytes 196616 | tf_op jit(solution)/shard_map/ppermute | solution.py:196
  59.2 1.6 %collective-permute-done.5 = f32[1,16,1024]{2,1,0:T(8,128)S(1)} collective-permute-done((f32[1,16,1024]{2,1,0:T(8,128)S(1)}, f32[1,16,1024]{2,1,0:T(8,128)S(1)}, u32[]{:S(2)}, u32[]{:S(2)}) %collective-permute-start.5) | collective-permute-done | bytes 65568 | tf_op jit(solution)/shard_map/ppermute | solution.py:196
  60.8 6.8 %collective-permute-start.6 = (f32[16,768]{1,0:T(8,128)S(1)}, f32[16,768]{1,0:T(8,128)S(1)}, u32[]{:S(2)}, u32[]{:S(2)}) collective-permute-start(f32[16,768]{1,0:T(8,128)S(1)} %pad_maximum_fusion.2), channel_id=1, source_target_pairs={{0,1},{1,0},{2,3},{3,2},{4,5},{5,4},{6,7},{7,6},{8,9},{9,8},{10,11... | collective-permute-start | bytes 147464 | tf_op jit(solution)/shard_map/ppermute | solution.py:196
  67.8 0.7 collective-permute-done.6
  68.6 0.7 collective-permute-start.9
  69.2 1.3 collective-permute-start.8
  70.5 0.7 collective-permute-start.7
  71.8 6.4 %collective-permute-start.15 = (f32[1,16,512]{2,1,0:T(8,128)S(1)}, f32[1,16,512]{2,1,0:T(8,128)S(1)}, u32[]{:S(2)}, u32[]{:S(2)}) collective-permute-start(f32[1,16,512]{2,1,0:T(8,128)S(1)} %slice.155), channel_id=1, source_target_pairs={{0,128},{32,160},{64,192},{96,224},{128,0},{160,32},{192,64},{224,... | collective-permute-start | bytes 98312 | tf_op jit(solution)/shard_map/ppermute | solution.py:196
  78.2 0.9 broadcast_in_dim.9
  79.1 6.3 %all-to-all-start = ((f32[8,16,1280]{2,1,0:T(8,128)}), f32[8,16,1280]{2,1,0:T(8,128)S(1)}, u32[]{:S(2)}, u32[]{:S(2)}) async-start(f32[8,16,1280]{2,1,0:T(8,128)} %broadcast_in_dim.9), calls=%async_computation | async-start | bytes 1310720 | tf_op jit(solution)/shard_map/all_to_all | solution.py:227
  85.5 2.9 %collective-permute-start.16 = (f32[16,256]{1,0:T(8,128)S(1)}, f32[16,256]{1,0:T(8,128)S(1)}, u32[]{:S(2)}, u32[]{:S(2)}) collective-permute-start(f32[16,256]{1,0:T(8,128)S(1)} %slice_select_fusion.6), channel_id=1, source_target_pairs={{0,1},{1,0},{2,3},{3,2},{4,5},{5,4},{6,7},{7,6},{8,9},{9,8},{10,11... | collective-permute-start | bytes 49160 | tf_op jit(solution)/shard_map/ppermute | solution.py:196
  88.4 0.8 collective-permute-done.16
  89.2 0.7 collective-permute-start.19
  89.9 1.3 collective-permute-start.18
  91.2 0.7 collective-permute-start.17
  91.9 4.0 %collective-permute-done.18 = f32[16,512]{1,0:T(8,128)S(1)} collective-permute-done((f32[16,512]{1,0:T(8,128)S(1)}, f32[16,512]{1,0:T(8,128)S(1)}, u32[]{:S(2)}, u32[]{:S(2)}) %collective-permute-start.18) | collective-permute-done | bytes 32800 | tf_op jit(solution)/shard_map/ppermute | solution.py:222
  95.9 4.0 %collective-permute-start.22 = (f32[16,512]{1,0:T(8,128)S(1)}, f32[16,512]{1,0:T(8,128)S(1)}, u32[]{:S(2)}, u32[]{:S(2)}) collective-permute-start(f32[16,512]{1,0:T(8,128)S(1)} %add_select_fusion.1), channel_id=1, source_target_pairs={{0,24},{8,16},{16,8},{24,0},{1,25},{9,17},{17,9},{25,1},{2,26},{10... | collective-permute-start | bytes 98312 | tf_op jit(solution)/shard_map/ppermute | solution.py:196
  100.0 0.7 collective-permute-start.20
  100.6 0.6 collective-permute-done.22
  101.3 3.0 %collective-permute-done.21 = f32[16,512]{1,0:T(8,128)S(1)} collective-permute-done((f32[16,512]{1,0:T(8,128)S(1)}, f32[16,512]{1,0:T(8,128)S(1)}, u32[]{:S(2)}, u32[]{:S(2)}) %collective-permute-start.21) | collective-permute-done | bytes 32800 | tf_op jit(solution)/shard_map/ppermute | solution.py:196
  104.3 4.8 %collective-permute-start.24 = (f32[8,16,1280]{2,1,0:T(8,128)S(1)}, f32[8,16,1280]{2,1,0:T(8,128)S(1)}, u32[]{:S(2)}, u32[]{:S(2)}) collective-permute-start(f32[8,16,1280]{2,1,0:T(8,128)S(1)} %all-to-all-done.refs_1_.refs_0_.refs_5_), channel_id=1, source_target_pairs={{0,24},{8,0},{16,8},{24,16},{1,25},{9,1},{17,9},{25,17},{2,26},{10... | collective-permute-start | bytes 1966088 | tf_op jit(solution)/shard_map/ppermute | solution.py:237
  109.0 1.1 broadcast_in_dim.10
  110.1 3.7 %all-to-all-start.1 = ((f32[8,4,16,512]{3,2,1,0:T(8,128)}), f32[8,4,16,512]{3,2,1,0:T(8,128)S(1)}, u32[]{:S(2)}, u32[]{:S(2)}) async-start(f32[8,4,16,512]{3,2,1,0:T(8,128)} %broadcast_in_dim.10), calls=%async_computation.1 | async-start | bytes 2097152 | tf_op jit(solution)/shard_map/all_to_all | solution.py:227
  113.8 7.0 %collective-permute-done.24.refs_3_.refs_2_.refs_7_ = f32[8,16,1280]{2,1,0:T(8,128)S(1)} collective-permute-done((f32[8,16,1280]{2,1,0:T(8,128)S(1)}, f32[8,16,1280]{2,1,0:T(8,128)S(1)}, u32[]{:S(2)}, u32[]{:S(2)}) %collective-permute-start.24) | collective-permute-done | bytes 655392 | tf_op jit(solution)/shard_map/ppermute | solution.py:237
  120.9 3.5 %collective-permute-start.26 = (f32[4,16,1280]{2,1,0:T(8,128)S(1)}, f32[4,16,1280]{2,1,0:T(8,128)S(1)}, u32[]{:S(2)}, u32[]{:S(2)}) collective-permute-start(f32[4,16,1280]{2,1,0:T(8,128)S(1)} %slice.162), channel_id=1, source_target_pairs={{0,24},{8,0},{16,8},{24,16},{1,25},{9,1},{17,9},{25,17},{2,26},{10... | collective-permute-start | bytes 983048 | tf_op jit(solution)/shard_map/ppermute | solution.py:237
  124.5 7.4 %collective-permute-done.25.refs_4_.refs_3_.refs_8_ = f32[4,16,1280]{2,1,0:T(8,128)S(1)} collective-permute-done((f32[4,16,1280]{2,1,0:T(8,128)S(1)}, f32[4,16,1280]{2,1,0:T(8,128)S(1)}, u32[]{:S(2)}, u32[]{:S(2)}) %collective-permute-start.25) | collective-permute-done | bytes 327712 | tf_op jit(solution)/shard_map/ppermute | solution.py:237
  131.9 0.7 copy-done.8
  132.7 4.3 %collective-permute-start.27 = (f32[4,8,16,256]{3,2,1,0:T(8,128)S(1)}, f32[4,8,16,256]{3,2,1,0:T(8,128)}, u32[]{:S(2)}, u32[]{:S(2)}) collective-permute-start(f32[4,8,16,256]{3,2,1,0:T(8,128)S(1)} %bitcast.36), channel_id=1, source_target_pairs={{0,1},{1,0},{2,3},{3,2},{4,5},{5,4},{6,7},{7,6},{8,9},{9,8},{10,11... | collective-permute-start | bytes 1572872 | tf_op jit(solution)/shard_map/ppermute | solution.py:196
  137.0 1.7 %collective-permute-done.27.other_hbm = f32[4,8,16,256]{3,2,1,0:T(8,128)} collective-permute-done((f32[4,8,16,256]{3,2,1,0:T(8,128)S(1)}, f32[4,8,16,256]{3,2,1,0:T(8,128)}, u32[]{:S(2)}, u32[]{:S(2)}) %collective-permute-start.27) | collective-permute-done | bytes 524320 | tf_op jit(solution)/shard_map/ppermute | solution.py:196
  138.7 5.9 %solve.3.own = f32[2,512,512]{2,1,0:T(8,128)} custom-call(s32[1]{0:T(128)} %bitcast.1.y_ref, s32[1]{0:T(128)} %bitcast.core_ref, f32[2,512,512]{2,1,0:T(8,128)} %inv_hbm.3, f32[4,8,16,256]{3,2,1,0:T(8,128)} %collective-permute-done.27.other_hbm, f32[8,16,1280]{2,1,0:T(8,128)} %copy-done.3, f32[8,16,1280]{2,1,0:T(8,128)} %copy-done.5, ...), custom_call_target="tpu_custom_call" | custom-call | flops 2415919104 | bytes 6291456 | tf_op jit(solution)/shard_map/solve/pallas_call | solution.py:132
  145.1 1.0 copy-done.6
  146.1 5.1 %solve.2.own = f32[2,512,256]{2,1,0:T(8,128)} custom-call(s32[1]{0:T(128)} %bitcast.1.y_ref, s32[1]{0:T(128)} %bitcast.core_ref, f32[2,512,512]{2,1,0:T(8,128)} %inv_hbm.3, f32[4,8,16,256]{3,2,1,0:T(8,128)} %collective-permute-done.27.other_hbm, f32[8,4,16,512]{3,2,1,0:T(8,128)} %copy-done.6, f32[8,16,1280]{2,1,0:T(8,128)} %copy-done.3, ...), custom_call_target="tpu_custom_call" | custom-call | flops 1207959552 | bytes 6291456 | tf_op jit(solution)/shard_map/solve/pallas_call | solution.py:132
  151.4 3.7 %finish.2 = (f32[2,512,1536]{2,1,0:T(8,128)}, f32[16,1536]{1,0:T(8,128)S(1)}) custom-call(s32[1]{0:T(128)} %bitcast.core_ref, f32[2,512,512]{2,1,0:T(8,128)S(1)} %copy-done, f32[2,512,512]{2,1,0:T(8,128)} %collective-permute-done.29.other, f32[16,1024]{1,0:T(8,128)S(1)} %fusion.1.base, f32[2,16,512]{2,1,0:T(8,128)S(1)} %bitcast.23), custom_call_target="tpu_custom_call" | custom-call | flops 100663296 | bytes 6291456 | tf_op jit(solution)/shard_map/finish/pallas_call | solution.py:176
  155.1 2.3 %finish.3 = (f32[2,512,1536]{2,1,0:T(8,128)}, f32[16,1536]{1,0:T(8,128)}) custom-call(s32[1]{0:T(128)} %bitcast.core_ref, f32[2,512,256]{2,1,0:T(8,128)S(1)} %copy-done.1, f32[2,512,256]{2,1,0:T(8,128)S(1)} %collective-permute-done.28.other, f32[16,512]{1,0:T(8,128)S(1)} %fusion.3.base, f32[2,16,512]{2,1,0:T(8,128)S(1)} %bitcast.24, ...), custom_call_target="tpu_custom_call", output_to_operand_aliasing={{0}: (5, {})} | custom-call | flops 50331648 | bytes 6291456 | tf_op jit(solution)/shard_map/finish/pallas_call | solution.py:176
  (84 shorter events, 2.2 us)
Async XLA Ops:
  12.0 14.9 %collective-permute-start = (f32[8,16,1024]{2,1,0:T(8,128)}, f32[8,16,1024]{2,1,0:T(8,128)S(1)}, u32[]{:S(2)}, u32[]{:S(2)}) collective-permute-start(f32[8,16,1024]{2,1,0:T(8,128)} %get-tuple-element.18), channel_id=1, source_target_pairs={{0,8},{8,0},{16,24},{24,16},{1,9},{9,1},{17,25},{25,17},{2,10},{10... | collective-permute-start | bytes 1572872 | tf_op jit(solution)/shard_map/ppermute | solution.py:196
  14.1 20.8 %collective-permute-start.1 = (f32[8,16,1024]{2,1,0:T(8,128)}, f32[8,16,1024]{2,1,0:T(8,128)S(1)}, u32[]{:S(2)}, u32[]{:S(2)}) collective-permute-start(f32[8,16,1024]{2,1,0:T(8,128)} %get-tuple-element.19), channel_id=1, source_target_pairs={{0,24},{8,16},{16,8},{24,0},{1,25},{9,17},{17,9},{25,1},{2,26},{10... | collective-permute-start | bytes 1572872 | tf_op jit(solution)/shard_map/ppermute | solution.py:196
  16.0 23.5 %collective-permute-start.2 = (f32[8,16,1024]{2,1,0:T(8,128)}, f32[8,16,1024]{2,1,0:T(8,128)S(1)}, u32[]{:S(2)}, u32[]{:S(2)}) collective-permute-start(f32[8,16,1024]{2,1,0:T(8,128)} %get-tuple-element.20), channel_id=1, source_target_pairs={{0,16},{8,24},{16,0},{24,8},{1,17},{9,25},{17,1},{25,9},{2,18},{10... | collective-permute-start | bytes 1572872 | tf_op jit(solution)/shard_map/ppermute | solution.py:196
  16.8 22.8 %copy-start.9 = (f32[8,16,1024]{2,1,0:T(8,128)S(1)}, f32[8,16,1024]{2,1,0:T(8,128)}, u32[]{:S(2)}) copy-start(f32[8,16,1024]{2,1,0:T(8,128)} %get-tuple-element.17) | copy-start | bytes 1572868
  16.8 24.7 %copy-start.2 = (f32[1,1,2,16,512]{4,3,2,1,0:T(8,128)S(1)}, f32[1,1,2,16,512]{4,3,2,1,0:T(8,128)}, u32[]{:S(2)}) copy-start(f32[1,1,2,16,512]{4,3,2,1,0:T(8,128)} %param.8) | copy-start | bytes 196612
  16.8 24.7 %copy-start.11 = (f32[1,1,16,1536]{3,2,1,0:T(8,128)S(1)}, f32[1,1,16,1536]{3,2,1,0:T(8,128)}, u32[]{:S(2)}) copy-start(f32[1,1,16,1536]{3,2,1,0:T(8,128)} %param.7) | copy-start | bytes 294916
  24.4 34.6 %copy-start.10 = (f32[8,16,512]{2,1,0:T(8,128)S(1)}, f32[8,16,512]{2,1,0:T(8,128)}, u32[]{:S(2)}) copy-start(f32[8,16,512]{2,1,0:T(8,128)} %get-tuple-element.23) | copy-start | bytes 786436
  24.4 34.6 %collective-permute-start.10 = (f32[8,16,512]{2,1,0:T(8,128)}, f32[8,16,512]{2,1,0:T(8,128)S(1)}, u32[]{:S(2)}, u32[]{:S(2)}) collective-permute-start(f32[8,16,512]{2,1,0:T(8,128)} %get-tuple-element.24), channel_id=1, source_target_pairs={{0,8},{8,0},{16,24},{24,16},{1,9},{9,1},{17,25},{25,17},{2,10},{10... | collective-permute-start | bytes 786440 | tf_op jit(solution)/shard_map/ppermute | solution.py:196
  25.0 33.9 %collective-permute-start.11 = (f32[8,16,512]{2,1,0:T(8,128)}, f32[8,16,512]{2,1,0:T(8,128)S(1)}, u32[]{:S(2)}, u32[]{:S(2)}) collective-permute-start(f32[8,16,512]{2,1,0:T(8,128)} %get-tuple-element.25), channel_id=1, source_target_pairs={{0,24},{8,16},{16,8},{24,0},{1,25},{9,17},{17,9},{25,1},{2,26},{10... | collective-permute-start | bytes 786440 | tf_op jit(solution)/shard_map/ppermute | solution.py:196
  26.9 32.0 %collective-permute-start.12 = (f32[8,16,512]{2,1,0:T(8,128)}, f32[8,16,512]{2,1,0:T(8,128)S(1)}, u32[]{:S(2)}, u32[]{:S(2)}) collective-permute-start(f32[8,16,512]{2,1,0:T(8,128)} %get-tuple-element.26), channel_id=1, source_target_pairs={{0,16},{8,24},{16,0},{24,8},{1,17},{9,25},{17,1},{25,9},{2,18},{10... | collective-permute-start | bytes 786440 | tf_op jit(solution)/shard_map/ppermute | solution.py:196
  39.8 5.8 %collective-permute-start.3 = (f32[4,16,1024]{2,1,0:T(8,128)S(1)}, f32[4,16,1024]{2,1,0:T(8,128)S(1)}, u32[]{:S(2)}, u32[]{:S(2)}) collective-permute-start(f32[4,16,1024]{2,1,0:T(8,128)S(1)} %slice.137), channel_id=1, source_target_pairs={{0,32},{32,0},{64,96},{96,64},{128,160},{160,128},{192,224},{224,1... | collective-permute-start | bytes 786440 | tf_op jit(solution)/shard_map/ppermute | solution.py:196
  45.6 5.8 %collective-permute-start.4 = (f32[2,16,1024]{2,1,0:T(8,128)S(1)}, f32[2,16,1024]{2,1,0:T(8,128)S(1)}, u32[]{:S(2)}, u32[]{:S(2)}) collective-permute-start(f32[2,16,1024]{2,1,0:T(8,128)S(1)} %slice.139), channel_id=1, source_target_pairs={{0,64},{32,96},{64,0},{96,32},{128,192},{160,224},{192,128},{224,1... | collective-permute-start | bytes 393224 | tf_op jit(solution)/shard_map/ppermute | solution.py:196
  51.4 9.3 %collective-permute-start.5 = (f32[1,16,1024]{2,1,0:T(8,128)S(1)}, f32[1,16,1024]{2,1,0:T(8,128)S(1)}, u32[]{:S(2)}, u32[]{:S(2)}) collective-permute-start(f32[1,16,1024]{2,1,0:T(8,128)S(1)} %slice.141), channel_id=1, source_target_pairs={{0,128},{32,160},{64,192},{96,224},{128,0},{160,32},{192,64},{224,... | collective-permute-start | bytes 196616 | tf_op jit(solution)/shard_map/ppermute | solution.py:196
  59.1 8.6 %collective-permute-start.13 = (f32[4,16,512]{2,1,0:T(8,128)S(1)}, f32[4,16,512]{2,1,0:T(8,128)S(1)}, u32[]{:S(2)}, u32[]{:S(2)}) collective-permute-start(f32[4,16,512]{2,1,0:T(8,128)S(1)} %slice.151), channel_id=1, source_target_pairs={{0,224},{32,64},{64,32},{96,128},{128,96},{160,192},{192,160},{224... | collective-permute-start | bytes 393224 | tf_op jit(solution)/shard_map/ppermute | solution.py:196
  60.8 7.7 %collective-permute-start.6 = (f32[16,768]{1,0:T(8,128)S(1)}, f32[16,768]{1,0:T(8,128)S(1)}, u32[]{:S(2)}, u32[]{:S(2)}) collective-permute-start(f32[16,768]{1,0:T(8,128)S(1)} %pad_maximum_fusion.2), channel_id=1, source_target_pairs={{0,1},{1,0},{2,3},{3,2},{4,5},{5,4},{6,7},{7,6},{8,9},{9,8},{10,11... | collective-permute-start | bytes 147464 | tf_op jit(solution)/shard_map/ppermute | solution.py:196
  67.7 4.1 %collective-permute-start.14 = (f32[2,16,512]{2,1,0:T(8,128)S(1)}, f32[2,16,512]{2,1,0:T(8,128)S(1)}, u32[]{:S(2)}, u32[]{:S(2)}) collective-permute-start(f32[2,16,512]{2,1,0:T(8,128)S(1)} %slice.153), channel_id=1, source_target_pairs={{0,64},{32,224},{64,0},{96,160},{128,192},{160,96},{192,128},{224,... | collective-permute-start | bytes 196616 | tf_op jit(solution)/shard_map/ppermute | solution.py:196
  68.6 9.6 %collective-permute-start.9 = (f32[16,1280]{1,0:T(8,128)S(1)}, f32[16,1280]{1,0:T(8,128)S(1)}, u32[]{:S(2)}, u32[]{:S(2)}) collective-permute-start(f32[16,1280]{1,0:T(8,128)S(1)} %pad_maximum_fusion.1), channel_id=1, source_target_pairs={{6,2},{7,3},{14,10},{15,11},{22,18},{23,19},{30,26},{31,27},{38,34... | collective-permute-start | bytes 245768 | tf_op jit(solution)/shard_map/ppermute | solution.py:222
  69.2 9.0 %collective-permute-start.8 = (f32[16,1280]{1,0:T(8,128)S(1)}, f32[16,1280]{1,0:T(8,128)S(1)}, u32[]{:S(2)}, u32[]{:S(2)}) collective-permute-start(f32[16,1280]{1,0:T(8,128)S(1)} %pad_maximum_fusion.1), channel_id=1, source_target_pairs={{6,0},{7,1},{14,8},{15,9},{22,16},{23,17},{30,24},{31,25},{38,32},... | collective-permute-start | bytes 245768 | tf_op jit(solution)/shard_map/ppermute | solution.py:222
  70.5 7.7 %collective-permute-start.7 = (f32[16,1280]{1,0:T(8,128)S(1)}, f32[16,1280]{1,0:T(8,128)S(1)}, u32[]{:S(2)}, u32[]{:S(2)}) collective-permute-start(f32[16,1280]{1,0:T(8,128)S(1)} %pad_maximum_fusion.1), channel_id=1, source_target_pairs={{6,4},{7,5},{14,12},{15,13},{22,20},{23,21},{30,28},{31,29},{38,36... | collective-permute-start | bytes 245768 | tf_op jit(solution)/shard_map/ppermute | solution.py:222
  71.8 13.6 %collective-permute-start.15 = (f32[1,16,512]{2,1,0:T(8,128)S(1)}, f32[1,16,512]{2,1,0:T(8,128)S(1)}, u32[]{:S(2)}, u32[]{:S(2)}) collective-permute-start(f32[1,16,512]{2,1,0:T(8,128)S(1)} %slice.155), channel_id=1, source_target_pairs={{0,128},{32,160},{64,192},{96,224},{128,0},{160,32},{192,64},{224,... | collective-permute-start | bytes 98312 | tf_op jit(solution)/shard_map/ppermute | solution.py:196
  79.1 25.2 %all-to-all-start = ((f32[8,16,1280]{2,1,0:T(8,128)}), f32[8,16,1280]{2,1,0:T(8,128)S(1)}, u32[]{:S(2)}, u32[]{:S(2)}) async-start(f32[8,16,1280]{2,1,0:T(8,128)} %broadcast_in_dim.9), calls=%async_computation | async-start | bytes 1310720 | tf_op jit(solution)/shard_map/all_to_all | solution.py:227
  85.5 3.7 %collective-permute-start.16 = (f32[16,256]{1,0:T(8,128)S(1)}, f32[16,256]{1,0:T(8,128)S(1)}, u32[]{:S(2)}, u32[]{:S(2)}) collective-permute-start(f32[16,256]{1,0:T(8,128)S(1)} %slice_select_fusion.6), channel_id=1, source_target_pairs={{0,1},{1,0},{2,3},{3,2},{4,5},{5,4},{6,7},{7,6},{8,9},{9,8},{10,11... | collective-permute-start | bytes 49160 | tf_op jit(solution)/shard_map/ppermute | solution.py:196
  89.2 2.6 %collective-permute-start.19 = (f32[16,512]{1,0:T(8,128)S(1)}, f32[16,512]{1,0:T(8,128)S(1)}, u32[]{:S(2)}, u32[]{:S(2)}) collective-permute-start(f32[16,512]{1,0:T(8,128)S(1)} %pad_maximum_fusion.3), channel_id=1, source_target_pairs={{6,2},{7,3},{14,10},{15,11},{22,18},{23,19},{30,26},{31,27},{38,34... | collective-permute-start | bytes 98312 | tf_op jit(solution)/shard_map/ppermute | solution.py:222
  89.9 6.0 %collective-permute-start.18 = (f32[16,512]{1,0:T(8,128)S(1)}, f32[16,512]{1,0:T(8,128)S(1)}, u32[]{:S(2)}, u32[]{:S(2)}) collective-permute-start(f32[16,512]{1,0:T(8,128)S(1)} %pad_maximum_fusion.3), channel_id=1, source_target_pairs={{6,0},{7,1},{14,8},{15,9},{22,16},{23,17},{30,24},{31,25},{38,32},... | collective-permute-start | bytes 98312 | tf_op jit(solution)/shard_map/ppermute | solution.py:222
  91.2 4.7 %collective-permute-start.17 = (f32[16,512]{1,0:T(8,128)S(1)}, f32[16,512]{1,0:T(8,128)S(1)}, u32[]{:S(2)}, u32[]{:S(2)}) collective-permute-start(f32[16,512]{1,0:T(8,128)S(1)} %pad_maximum_fusion.3), channel_id=1, source_target_pairs={{6,4},{7,5},{14,12},{15,13},{22,20},{23,21},{30,28},{31,29},{38,36... | collective-permute-start | bytes 98312 | tf_op jit(solution)/shard_map/ppermute | solution.py:222
  95.9 5.3 %collective-permute-start.22 = (f32[16,512]{1,0:T(8,128)S(1)}, f32[16,512]{1,0:T(8,128)S(1)}, u32[]{:S(2)}, u32[]{:S(2)}) collective-permute-start(f32[16,512]{1,0:T(8,128)S(1)} %add_select_fusion.1), channel_id=1, source_target_pairs={{0,24},{8,16},{16,8},{24,0},{1,25},{9,17},{17,9},{25,1},{2,26},{10... | collective-permute-start | bytes 98312 | tf_op jit(solution)/shard_map/ppermute | solution.py:196
  100.0 4.3 %collective-permute-start.21 = (f32[16,512]{1,0:T(8,128)S(1)}, f32[16,512]{1,0:T(8,128)S(1)}, u32[]{:S(2)}, u32[]{:S(2)}) collective-permute-start(f32[16,512]{1,0:T(8,128)S(1)} %add_select_fusion.1), channel_id=1, source_target_pairs={{0,16},{8,24},{16,0},{24,8},{1,17},{9,25},{17,1},{25,9},{2,18},{10... | collective-permute-start | bytes 98312 | tf_op jit(solution)/shard_map/ppermute | solution.py:196
  100.0 4.3 %collective-permute-start.20 = (f32[16,512]{1,0:T(8,128)S(1)}, f32[16,512]{1,0:T(8,128)S(1)}, u32[]{:S(2)}, u32[]{:S(2)}) collective-permute-start(f32[16,512]{1,0:T(8,128)S(1)} %add_select_fusion.1), channel_id=1, source_target_pairs={{0,8},{8,0},{16,24},{24,16},{1,9},{9,1},{17,25},{25,17},{2,10},{10... | collective-permute-start | bytes 98312 | tf_op jit(solution)/shard_map/ppermute | solution.py:196
  104.3 34.4 %copy-start.3 = (f32[8,16,1280]{2,1,0:T(8,128)}, f32[8,16,1280]{2,1,0:T(8,128)S(1)}, u32[]{:S(2)}) copy-start(f32[8,16,1280]{2,1,0:T(8,128)S(1)} %all-to-all-done.refs_1_.refs_0_.refs_5_) | copy-start | bytes 1966084
  104.3 16.6 %collective-permute-start.24 = (f32[8,16,1280]{2,1,0:T(8,128)S(1)}, f32[8,16,1280]{2,1,0:T(8,128)S(1)}, u32[]{:S(2)}, u32[]{:S(2)}) collective-permute-start(f32[8,16,1280]{2,1,0:T(8,128)S(1)} %all-to-all-done.refs_1_.refs_0_.refs_5_), channel_id=1, source_target_pairs={{0,24},{8,0},{16,8},{24,16},{1,25},{9,1},{17,9},{25,17},{2,26},{10... | collective-permute-start | bytes 1966088 | tf_op jit(solution)/shard_map/ppermute | solution.py:237
  109.0 15.4 %collective-permute-start.23 = (f32[8,16,1280]{2,1,0:T(8,128)S(1)}, f32[8,16,1280]{2,1,0:T(8,128)S(1)}, u32[]{:S(2)}, u32[]{:S(2)}) collective-permute-start(f32[8,16,1280]{2,1,0:T(8,128)S(1)} %all-to-all-done.refs_1_.refs_0_.refs_5_), channel_id=1, source_target_pairs={{0,8},{8,16},{16,24},{24,0},{1,9},{9,17},{17,25},{25,1},{2,10},{10... | collective-permute-start | bytes 1966088 | tf_op jit(solution)/shard_map/ppermute | solution.py:237
  110.1 34.9 %all-to-all-start.1 = ((f32[8,4,16,512]{3,2,1,0:T(8,128)}), f32[8,4,16,512]{3,2,1,0:T(8,128)S(1)}, u32[]{:S(2)}, u32[]{:S(2)}) async-start(f32[8,4,16,512]{3,2,1,0:T(8,128)} %broadcast_in_dim.10), calls=%async_computation.1 | async-start | bytes 2097152 | tf_op jit(solution)/shard_map/all_to_all | solution.py:227
  120.9 17.8 %copy-start.4 = (f32[8,16,1280]{2,1,0:T(8,128)}, f32[8,16,1280]{2,1,0:T(8,128)S(1)}, u32[]{:S(2)}) copy-start(f32[8,16,1280]{2,1,0:T(8,128)S(1)} %collective-permute-done.24.refs_3_.refs_2_.refs_7_) | copy-start | bytes 1966084
  120.9 11.0 %collective-permute-start.26 = (f32[4,16,1280]{2,1,0:T(8,128)S(1)}, f32[4,16,1280]{2,1,0:T(8,128)S(1)}, u32[]{:S(2)}, u32[]{:S(2)}) collective-permute-start(f32[4,16,1280]{2,1,0:T(8,128)S(1)} %slice.162), channel_id=1, source_target_pairs={{0,24},{8,0},{16,8},{24,16},{1,25},{9,1},{17,9},{25,17},{2,26},{10... | collective-permute-start | bytes 983048 | tf_op jit(solution)/shard_map/ppermute | solution.py:237
  124.4 14.3 %copy-start.5 = (f32[8,16,1280]{2,1,0:T(8,128)}, f32[8,16,1280]{2,1,0:T(8,128)S(1)}, u32[]{:S(2)}) copy-start(f32[8,16,1280]{2,1,0:T(8,128)S(1)} %collective-permute-done.23.refs_2_.refs_1_.refs_6_) | copy-start | bytes 1966084
  124.4 7.5 %collective-permute-start.25 = (f32[4,16,1280]{2,1,0:T(8,128)S(1)}, f32[4,16,1280]{2,1,0:T(8,128)S(1)}, u32[]{:S(2)}, u32[]{:S(2)}) collective-permute-start(f32[4,16,1280]{2,1,0:T(8,128)S(1)} %slice.160), channel_id=1, source_target_pairs={{0,8},{8,16},{16,24},{24,0},{1,9},{9,17},{17,25},{25,1},{2,10},{10... | collective-permute-start | bytes 983048 | tf_op jit(solution)/shard_map/ppermute | solution.py:237
  131.9 0.7 copy-start.8
  132.6 6.0 %copy-start.7 = (f32[4,16,1280]{2,1,0:T(8,128)}, f32[4,16,1280]{2,1,0:T(8,128)S(1)}, u32[]{:S(2)}) copy-start(f32[4,16,1280]{2,1,0:T(8,128)S(1)} %collective-permute-done.26.refs_5_.refs_4_.refs_9_) | copy-start | bytes 983044
  132.7 6.0 %collective-permute-start.27 = (f32[4,8,16,256]{3,2,1,0:T(8,128)S(1)}, f32[4,8,16,256]{3,2,1,0:T(8,128)}, u32[]{:S(2)}, u32[]{:S(2)}) collective-permute-start(f32[4,8,16,256]{3,2,1,0:T(8,128)S(1)} %bitcast.36), channel_id=1, source_target_pairs={{0,1},{1,0},{2,3},{3,2},{4,5},{5,4},{6,7},{7,6},{8,9},{9,8},{10,11... | collective-permute-start | bytes 1572872 | tf_op jit(solution)/shard_map/ppermute | solution.py:196
  144.6 6.8 %copy-start = (f32[2,512,512]{2,1,0:T(8,128)S(1)}, f32[2,512,512]{2,1,0:T(8,128)}, u32[]{:S(2)}) copy-start(f32[2,512,512]{2,1,0:T(8,128)} %solve.3.own) | copy-start | bytes 6291460
  144.6 6.8 %collective-permute-start.29 = (f32[2,512,512]{2,1,0:T(8,128)}, f32[2,512,512]{2,1,0:T(8,128)}, u32[]{:S(2)}, u32[]{:S(2)}) collective-permute-start(f32[2,512,512]{2,1,0:T(8,128)} %solve.3.own), channel_id=1, source_target_pairs={{0,1},{1,0},{2,3},{3,2},{4,5},{5,4},{6,7},{7,6},{8,9},{9,8},{10,11... | collective-permute-start | bytes 6291464 | tf_op jit(solution)/shard_map/ppermute | solution.py:196
  145.1 1.0 copy-start.6
  151.2 4.0 %copy-start.1 = (f32[2,512,256]{2,1,0:T(8,128)S(1)}, f32[2,512,256]{2,1,0:T(8,128)}, u32[]{:S(2)}) copy-start(f32[2,512,256]{2,1,0:T(8,128)} %solve.2.own) | copy-start | bytes 3145732
  151.2 3.9 %collective-permute-start.28 = (f32[2,512,256]{2,1,0:T(8,128)}, f32[2,512,256]{2,1,0:T(8,128)S(1)}, u32[]{:S(2)}, u32[]{:S(2)}) collective-permute-start(f32[2,512,256]{2,1,0:T(8,128)} %solve.2.own), channel_id=1, source_target_pairs={{0,1},{1,0},{2,3},{3,2},{4,5},{5,4},{6,7},{7,6},{8,9},{9,8},{10,11... | collective-permute-start | bytes 3145736 | tf_op jit(solution)/shard_map/ppermute | solution.py:196
